TPU v7x, 32 devices: a whole 2x2x4 slice. The times are simulated.
32 devices in a mesh: grp: 2 (over x), wid: 16 (over z, y, core).
Axes of the slice: x: 2, y: 2, z: 4, core: 2. Of those that a mesh axis runs over, the one named last changes fastest.
Arguments:
- grad_out: bfloat16 [512, 8192], P('grp', 'wid'), parts along dimension 0, may hold values from -6 to 6
- gate_saved: bfloat16 [512, 16384], P('grp', 'wid'), parts along dimension 0, may hold values from -10 to 10
- up_saved: bfloat16 [512, 16384], P('grp', 'wid'), parts along dimension 0, may hold values from -6 to 6
- w_gate: bfloat16 [8192, 16384], P(None, 'wid'), may hold values from -0.0625 to 0.0625
- w_up: bfloat16 [8192, 16384], P(None, 'wid'), may hold values from -0.0625 to 0.0625
- w_down: bfloat16 [16384, 8192], P('wid'), may hold values from -0.09375 to 0.09375
Outputs:
- grad_in: bfloat16 [512, 8192], P('grp', 'wid'), parts along dimension 0
There are 2 independent parts, one for each index of `grp`. A program takes and returns all parts, laid end to end along the dimension named above; an argument that names none is the same for every part. Nothing has to cross between parts.
All inputs are finite; a program needn't handle non-finite values.
Results may differ from a plain program's by a relative error of at most 0.0051.
Values may be sent and summed in bfloat16 or wider, within the bound.
No kernel may reach another device: no remote copies, remote signals or barrier semaphores. Data moves between devices by JAX's collectives and lax.ppermute only.
A program may use at most 128 MiB of HBM per device.

v0:
```python
import jax
import jax.numpy as jnp
from jax import lax
from jax.sharding import PartitionSpec as P


def contract_last(left, right):
    return lax.dot_general(
        left, right, (((1,), (1,)), ((), ())), preferred_element_type=jnp.float32
    )


def local(grad_out, gate_saved, up_saved, w_gate, w_up, w_down):
    grad_hidden = contract_last(lax.all_gather(grad_out, "wid", axis=1, tiled=True), w_down)
    gate = gate_saved.astype(jnp.float32)
    up = up_saved.astype(jnp.float32)
    sig = jax.nn.sigmoid(gate)
    grad_gate = (grad_hidden * up * sig * (1.0 + gate * (1.0 - sig))).astype(jnp.bfloat16)
    grad_up = (grad_hidden * gate * sig).astype(jnp.bfloat16)
    summed = lax.psum_scatter(
        contract_last(w_gate, grad_gate) + contract_last(w_up, grad_up),
        "wid",
        scatter_dimension=0,
        tiled=True,
    )
    return summed.astype(jnp.bfloat16).T


def solution(mesh):
    in_specs = (
        P("grp", "wid"),
        P("grp", "wid"),
        P("grp", "wid"),
        P(None, "wid"),
        P(None, "wid"),
        P("wid", None),
    )
    out_specs = P("grp", "wid")
    return jax.shard_map(local, mesh=mesh, in_specs=in_specs, out_specs=out_specs, check_vma=False)
```

profile of v0, /device:TPU:0, one launch (start us, length us, event | category | flops | bytes accessed | tf_op | source)
XLA Modules:
  0.0 218.4 jit_solution(14056833642521643478)
XLA Ops:
  6.5 0.0 copy-start
  6.5 0.0 copy-start.1
  6.5 0.0 all-gather.2.cloned.1.call-start
  6.5 0.7 all-gather.2.cloned.1.call-update
  7.3 0.0 reduce-scatter.2.cloned.1.call-start
  7.3 58.2 %all-gather.2.cloned.1.call-done = bf16[256,8192]{1,0:T(8,128)(2,1)} async-done(((bf16[256,512]{1,0:T(8,128)(2,1)}), bf16[256,8192]{1,0:T(8,128)(2,1)}) %all-gather.2.cloned.1.call-update) | async-done | bytes 4194320 | tf_op jit(solution)/shard_map/all_gather | solution.py:14
  65.5 9.3 %fusion.16 = f32[256,1024]{1,0:T(8,128)S(1)} fusion(bf16[256,8192]{1,0:T(8,128)(2,1)} %all-gather.2.cloned.1.call-done, bf16[1024,8192]{1,0:T(8,128)(2,1)} %param.11), kind=kOutput, calls=%fused_computation.19 | convolution fusion | flops 4294967296 | bytes 22020096 | tf_op jit(solution)/shard_map/dot_general | solution.py:8
  74.8 0.0 copy-done
  74.8 0.0 copy-done.1
  74.8 18.9 %fusion.10 = f32[256,8192]{1,0:T(8,128)} fusion(bf16[8192,1024]{1,0:T(8,128)(2,1)} %param.9, bf16[256,1024]{1,0:T(8,128)(2,1)S(1)} %copy-done, f32[256,1024]{1,0:T(8,128)S(1)} %fusion.16, bf16[256,1024]{1,0:T(8,128)(2,1)S(1)} %copy-done.1), kind=kOutput, calls=%fused_computation.13 | convolution fusion | flops 4298113024 | bytes 27262976 | tf_op jit(solution)/shard_map/dot_general | solution.py:8
  93.8 12.8 %fusion = f32[8192,256]{0,1:T(8,128)} fusion(f32[256,8192]{1,0:T(8,128)} %fusion.10, bf16[8192,1024]{1,0:T(8,128)(2,1)} %param.10, f32[256,1024]{1,0:T(8,128)S(1)} %fusion.16, bf16[256,1024]{1,0:T(8,128)(2,1)S(1)} %copy-done), kind=kOutput, calls=%fused_computation.1 | convolution fusion | flops 4298899456 | bytes 35127296 | tf_op jit(solution)/shard_map/dot_general | solution.py:8
  106.6 0.0 reduce-scatter.2.cloned.1.call-update
  106.6 103.2 %reduce-scatter.2.cloned.1.call-done = f32[512,256]{0,1:T(8,128)} async-done(((f32[8192,256]{0,1:T(8,128)}), f32[512,256]{0,1:T(8,128)}) %reduce-scatter.2.cloned.1.call-update) | async-done | bytes 524304 | tf_op jit(solution)/shard_map/reduce_scatter | solution.py:20
  209.8 1.8 convert_bitcast_fusion
Async XLA Ops:
  6.5 68.3 %copy-start = (bf16[256,1024]{1,0:T(8,128)(2,1)S(1)}, bf16[256,1024]{1,0:T(8,128)(2,1)}, u32[]{:S(2)}) copy-start(bf16[256,1024]{1,0:T(8,128)(2,1)} %param.7) | copy-start | bytes 1572868
  6.5 68.3 %copy-start.1 = (bf16[256,1024]{1,0:T(8,128)(2,1)S(1)}, bf16[256,1024]{1,0:T(8,128)(2,1)}, u32[]{:S(2)}) copy-start(bf16[256,1024]{1,0:T(8,128)(2,1)} %param.8) | copy-start | bytes 1572868
  6.5 58.9 %all-gather.2.cloned.1.call-start = ((), (), s32[]{:S(2)}) async-start(), calls=%async_computation.1 | async-start | bytes 4456448 | tf_op jit(solution)/shard_map/all_gather | solution.py:14
  7.3 202.5 %reduce-scatter.2.cloned.1.call-start = ((), (), s32[]{:S(2)}) async-start(), calls=%async_computation.2 | async-start | bytes 8912896 | tf_op jit(solution)/shard_map/reduce_scatter | solution.py:20
Sparse Core Ops, SparseCore 0:
  9.5 55.9 all-gather.1
  106.8 103.0 reduce-scatter.1
where the time goes:
time: 219 us; the launch traced here: 218 us
  waiting for transfers between devices  162 us (74%)
  matrix products  41.1 us (19%)
  between operations  13.4 us (6%)
    reduce_scatter x1, waiting for transfers between devices, local(): lax.psum_scatter(contract_last(w_gate, grad_gate) + contract_last(w_up, g...  103 us
    all_gather x1, waiting for transfers between devices, local(): lax.all_gather(grad_out, 'wid', axis=1, tiled=True)  58.2 us
    dot_general x3, matrix products, contract_last(): lax.dot_general(left, right, (((1,), (1,)), ((), ())), preferred_element_...  41.1 us
  transfers between devices with their start and end apart: 2, of which 2 were waited for; matrix products, arithmetic and copies ran while one was open for 0% of the time, Pallas kernels for 0%

commit v1 on v0

v1 whole, which is shorter than its diff:
```python
import functools

import jax
import jax.numpy as jnp
from jax import lax
from jax.experimental import pallas as pl
from jax.experimental.pallas import tpu as pltpu
from jax.sharding import PartitionSpec as P

BF16, F32 = jnp.bfloat16, jnp.float32
TILE = 256
VMEM = 24 * 2**20


def contract_last(left, right):
    return lax.dot_general(
        left, right, (((1,), (1,)), ((), ())), preferred_element_type=F32
    )


def call(body, blocks, grid, ins, outs, args, flops, read):
    return pl.pallas_call(
        body,
        grid_spec=pltpu.PrefetchScalarGridSpec(
            num_scalar_prefetch=1,
            grid=(grid,),
            in_specs=[pl.BlockSpec(shape, index) for shape, index in ins],
            out_specs=[pl.BlockSpec(shape, index) for shape, index, _ in outs],
        ),
        out_shape=[out for _, _, out in outs],
        compiler_params=pltpu.CompilerParams(vmem_limit_bytes=VMEM),
        cost_estimate=pl.CostEstimate(
            flops=flops, bytes_accessed=read, transcendentals=0
        ),
    )(blocks, *args)


def whole(i, b):
    return 0, 0


def column(i, b):
    return 0, i


def factors_body(blocks, gate_ref, up_ref, to_gate_ref, to_up_ref):
    gate = gate_ref[...].astype(F32)
    up = up_ref[...].astype(F32)
    sig = jax.nn.sigmoid(gate)
    to_gate_ref[...] = up * sig * (1.0 + gate * (1.0 - sig))
    to_up_ref[...] = gate * sig


def factors(blocks, gate, up):
    tok, ff = gate.shape
    spec = ((tok, TILE), column)
    out = (*spec, jax.ShapeDtypeStruct((tok, ff), F32))
    return call(factors_body, blocks, ff // TILE, [spec] * 2, [out] * 2, (gate, up), 0, 12 * tok * ff)


def hidden_body(parts, first, last, blocks, *refs):
    pieces, weights, rest = refs[:parts], refs[parts : 2 * parts], list(refs[2 * parts :])
    total = 0.0 if first else rest.pop(0)[...]
    for piece, weight in zip(pieces, weights):
        total = total + contract_last(piece[...], weight[...])
    if last:
        to_gate, to_up, grad_gate, grad_up = rest
        grad_gate[...] = (total * to_gate[...]).astype(BF16)
        grad_up[...] = (total * to_up[...]).astype(BF16)
    else:
        rest[0][...] = total


def hidden(blocks, pieces, w_down, total=None, scale=None):
    tok, width = pieces[0].shape
    ff = w_down.shape[0]
    parts = len(pieces)
    tile = ((tok, TILE), column)
    ins = [((tok, width), whole)] * parts
    ins += [((TILE, width), lambda i, b, j=j: (i, b[j])) for j in range(parts)]
    args = (*pieces, *([w_down] * parts))
    if total is not None:
        ins, args = ins + [tile], (*args, total)
    if scale is not None:
        ins, args = ins + [tile] * 2, (*args, *scale)
        outs = [(*tile, jax.ShapeDtypeStruct((tok, ff), BF16))] * 2
    else:
        outs = [(*tile, jax.ShapeDtypeStruct((tok, ff), F32))]
    body = functools.partial(hidden_body, parts, total is None, scale is not None)
    done = call(body, blocks, ff // TILE, ins, outs, args, 2 * parts * tok * width * ff, 2 * parts * width * ff)
    return done if scale is not None else done[0]


def partial_sum(grad_gate, grad_up, w_gate, w_up):
    return contract_last(grad_gate[...], w_gate[...]) + contract_last(grad_up[...], w_up[...])


def send_body(blocks, grad_gate, grad_up, w_gate, w_up, out):
    out[...] = partial_sum(grad_gate, grad_up, w_gate, w_up).astype(BF16)


def keep_body(half, blocks, grad_gate, grad_up, w_gate, w_up, got, keep, send):
    total = partial_sum(grad_gate, grad_up, w_gate, w_up) + got[...].astype(F32)
    i = pl.program_id(0)

    @pl.when(i < half)
    def _():
        send[...] = total.astype(BF16)

    @pl.when(i >= half)
    def _():
        keep[...] = total


def rows(per):
    return lambda i, b: (b[i // per] * per + i % per, 0)


def send_parts(blocks, grads, weights, width):
    tok, ff = grads[0].shape
    per = width // TILE
    ins = [((tok, ff), whole)] * 2 + [((TILE, ff), rows(per))] * 2
    outs = [((tok, TILE), column, jax.ShapeDtypeStruct((tok, 2 * width), BF16))]
    return call(send_body, blocks, 2 * per, ins, outs, (*grads, *weights), 8 * tok * ff * width, 8 * ff * width)[0]


def keep_parts(blocks, grads, weights, got, width):
    tok, ff = grads[0].shape
    per = width // TILE
    ins = [((tok, ff), whole)] * 2 + [((TILE, ff), rows(per))] * 2 + [((tok, TILE), column)]
    outs = [
        ((tok, TILE), lambda i, b: (0, jnp.maximum(i - per, 0)), jax.ShapeDtypeStruct((tok, width), F32)),
        ((tok, TILE), lambda i, b: (0, jnp.minimum(i, per - 1)), jax.ShapeDtypeStruct((tok, width), BF16)),
    ]
    body = functools.partial(keep_body, per)
    return call(body, blocks, 2 * per, ins, outs, (*grads, *weights, got), 8 * tok * ff * width, 8 * ff * width)


def staged(grad_out, gate_saved, up_saved, w_gate, w_up, w_down):
    n = 16
    width = grad_out.shape[1]
    me = lax.axis_index("wid")
    line, row, pair = me // 4, (me // 2) % 2, me % 2
    places = {
        "own": line,
        "near": line ^ 1,
        "mid": jnp.where(line < 2, 2, 1),
        "far": jnp.where(line < 2, 3, 0),
    }

    def blocks(name, order):
        first = 4 * places[name]
        return jnp.stack([first + 2 * (row ^ r) + (pair ^ p) for r, p in order]).astype(jnp.int32)

    pairs = [(i, i ^ 1) for i in range(n)]
    rows_ = [(i, i ^ 2) for i in range(n)]
    outer = [(i, i ^ 4) for i in range(n)]
    inner = [(i, i + 4) for i in range(4, 8)] + [(i, i - 4) for i in range(8, 12)]
    outward = [(i, i - 4) for i in range(4, 8)] + [(i, i + 4) for i in range(8, 12)]
    inward = [(j, i) for i, j in outward]
    is_mid = (line == 1) | (line == 2)

    def move(x, perm):
        return lax.ppermute(x, "wid", perm)

    scale = factors(blocks("own", [(0, 0)]), gate_saved, up_saved)

    held = {"own": grad_out}
    held["near"] = move(grad_out, outer)
    mid = move(grad_out, inner)
    far = move(held["near"], inner)
    held["mid"] = mid + move(mid, outward)
    held["far"] = far + move(far, outward)

    order = [(0, 0), (0, 1), (1, 0), (1, 1)]
    total = None
    for name in ("own", "near", "mid", "far"):
        here = held[name]
        across = move(here, rows_)
        pieces = [here, move(here, pairs), across, move(across, pairs)]
        last = name == "far"
        total = hidden(blocks(name, order), pieces, w_down, total, scale if last else None)
    grads, weights = total, (w_gate, w_up)

    kept = {}
    for name in ("far", "mid", "near", "own"):
        sent = send_parts(blocks(name, [(1, 1), (0, 1)]), grads, weights, width)
        got = move(sent, pairs)
        keep, across = keep_parts(blocks(name, [(1, 0), (0, 0)]), grads, weights, got, width)
        kept[name] = keep + move(across, rows_).astype(F32)

    far = kept["far"] + move(kept["far"].astype(BF16), inward).astype(F32)
    near = kept["near"] + move(far.astype(BF16), inner).astype(F32)
    mid = kept["mid"] + move(kept["mid"].astype(BF16), inward).astype(F32)
    own = kept["own"] + move(mid.astype(BF16), inner).astype(F32)
    own = own + move(near.astype(BF16), outer).astype(F32)
    return own.astype(BF16)


def local(grad_out, gate_saved, up_saved, w_gate, w_up, w_down):
    grad_hidden = contract_last(lax.all_gather(grad_out, "wid", axis=1, tiled=True), w_down)
    gate = gate_saved.astype(F32)
    up = up_saved.astype(F32)
    sig = jax.nn.sigmoid(gate)
    grad_gate = (grad_hidden * up * sig * (1.0 + gate * (1.0 - sig))).astype(BF16)
    grad_up = (grad_hidden * gate * sig).astype(BF16)
    summed = lax.psum_scatter(
        contract_last(w_gate, grad_gate) + contract_last(w_up, grad_up),
        "wid",
        scatter_dimension=0,
        tiled=True,
    )
    return summed.astype(BF16).T


def solution(mesh):
    in_specs = (
        P("grp", "wid"),
        P("grp", "wid"),
        P("grp", "wid"),
        P(None, "wid"),
        P(None, "wid"),
        P("wid", None),
    )
    out_specs = P("grp", "wid")
    body = staged if mesh.shape["wid"] == 16 else local
    return jax.shard_map(body, mesh=mesh, in_specs=in_specs, out_specs=out_specs, check_vma=False)
```

time: 219 us -> 137 us (0.63)
  waiting for transfers between devices: 162 us -> 29.4 us
  Pallas kernels: 0 us -> 51.5 us
  matrix products: 41.1 us -> 0 us
  starting transfers between devices: 0.04 us -> 29.4 us
  local copies, waits for them, and re-layouts: 0.01 us -> 23 us
  between operations: 13.4 us -> 0.37 us
    reduce_scatter x1 -> x0, waiting for transfers between devices: 103 us -> none  [local(): lax.psum_scatter(contract_last(w_gate, grad_gate) + contract_last(w_up, g...]
    all_gather x1 -> x0, waiting for transfers between devices: 58.2 us -> none  [local(): lax.all_gather(grad_out, 'wid', axis=1, tiled=True)]
    pallas_call x0 -> x13, Pallas kernels: none -> 51.5 us  [call(): pl.pallas_call(body, grid_spec=pltpu.PrefetchScalarGridSpec(num_scalar_pr...]
    dot_general x3 -> x0, matrix products: 41.1 us -> none  [contract_last(): lax.dot_general(left, right, (((1,), (1,)), ((), ())), preferred_element_...]
    ppermute x0 -> x30, waiting for transfers between devices: none -> 29.4 us  [move(): return lax.ppermute(x, 'wid', perm)]
    ppermute x0 -> x30, starting transfers between devices: none -> 29.4 us  [move(): return lax.ppermute(x, 'wid', perm)]
    unnamed x4 -> x18, local copies, waits for them, and re-layouts: 0.01 us -> 23 us
  transfers between devices with their start and end apart: 2 -> 30, of which waited for: 2 -> 6; matrix products, arithmetic and copies ran while one was open for 0% -> 1% of each run, Pallas kernels for 0% -> 32%
where the time goes in v1:
time: 137 us; the launch traced here: 136 us
  Pallas kernels  51.5 us (38%)
  starting transfers between devices  29.4 us (21%)
  waiting for transfers between devices  29.4 us (21%)
  local copies, waits for them, and re-layouts  23 us (17%)
  other arithmetic  2.37 us (2%)
    pallas_call x13, Pallas kernels, call(): pl.pallas_call(body, grid_spec=pltpu.PrefetchScalarGridSpec(num_scalar_pr...  51.5 us
    ppermute x30, waiting for transfers between devices, move(): return lax.ppermute(x, 'wid', perm)  29.4 us
    ppermute x30, starting transfers between devices, move(): return lax.ppermute(x, 'wid', perm)  29.4 us
    unnamed x18, local copies, waits for them, and re-layouts  23 us
  transfers between devices with their start and end apart: 30, of which 6 were waited for; matrix products, arithmetic and copies ran while one was open for 1% of the time, Pallas kernels for 32%

profile of v1, /device:TPU:0, one launch (start us, length us, event | category | flops | bytes accessed | tf_op | source)
XLA Modules:
  0.0 136.0 jit_solution(5385271786973349744)
XLA Ops:
  0.0 3.0 %collective-permute-start = (bf16[256,512]{1,0:T(8,128)(2,1)}, bf16[256,512]{1,0:T(8,128)(2,1)S(1)}, u32[]{:S(2)}, u32[]{:S(2)}) collective-permute-start(bf16[256,512]{1,0:T(8,128)(2,1)} %refs_0_.1), channel_id=1, source_target_pairs={{0,4},{1,5},{2,6},{3,7},{4,0},{5,1},{6,2},{7,3},{8,12},{9,13},{10,... | collective-permute-start | bytes 786440 | tf_op jit(solution)/shard_map/ppermute | solution.py:164
  3.0 0.7 collective-permute-start.6
  3.7 5.8 %collective-permute-done.refs_0_ = bf16[256,512]{1,0:T(8,128)(2,1)S(1)} collective-permute-done((bf16[256,512]{1,0:T(8,128)(2,1)}, bf16[256,512]{1,0:T(8,128)(2,1)S(1)}, u32[]{:S(2)}, u32[]{:S(2)}) %collective-permute-start) | collective-permute-done | bytes 262176 | tf_op jit(solution)/shard_map/ppermute | solution.py:164
  9.5 0.7 collective-permute-start.1
  10.3 1.8 %collective-permute-start.15 = (bf16[256,512]{1,0:T(8,128)(2,1)}, bf16[256,512]{1,0:T(8,128)(2,1)}, u32[]{:S(2)}, u32[]{:S(2)}) collective-permute-start(bf16[256,512]{1,0:T(8,128)(2,1)} %refs_0_.1), channel_id=1, source_target_pairs={{0,2},{1,3},{2,0},{3,1},{4,6},{5,7},{6,4},{7,5},{8,10},{9,11},{10,... | collective-permute-start | bytes 786440 | tf_op jit(solution)/shard_map/ppermute | solution.py:164
  12.1 1.3 collective-permute-start.7
  13.4 0.1 pad_add_fusion.4.blocks
  13.5 1.3 collective-permute-start.2
  14.8 0.1 pad_add_fusion.blocks
  14.9 0.4 collective-permute-start.12
  15.2 0.1 pad_add_fusion.10.blocks
  15.3 9.5 %collective-permute-done.7 = bf16[256,512]{1,0:T(8,128)(2,1)S(1)} collective-permute-done((bf16[256,512]{1,0:T(8,128)(2,1)S(1)}, bf16[256,512]{1,0:T(8,128)(2,1)S(1)}, u32[]{:S(2)}, u32[]{:S(2)}) %collective-permute-start.7) | collective-permute-done | bytes 262176 | tf_op jit(solution)/shard_map/ppermute | solution.py:164
  24.9 0.6 collective-permute-start.9
  25.5 0.1 pad_add_fusion.1.blocks
  25.6 4.4 %collective-permute-done.2 = bf16[256,512]{1,0:T(8,128)(2,1)S(1)} collective-permute-done((bf16[256,512]{1,0:T(8,128)(2,1)S(1)}, bf16[256,512]{1,0:T(8,128)(2,1)S(1)}, u32[]{:S(2)}, u32[]{:S(2)}) %collective-permute-start.2) | collective-permute-done | bytes 262176 | tf_op jit(solution)/shard_map/ppermute | solution.py:164
  30.1 0.6 collective-permute-start.4
  30.8 0.2 collective-permute-start.13
  31.0 0.1 pad_add_fusion.2.blocks
  31.1 1.0 copy-done.4
  32.1 1.0 copy-done.5
  33.2 0.8 shard_map.67
  34.0 0.3 collective-permute-start.8
  34.3 0.2 collective-permute-start.10
  34.6 0.1 pad_add_fusion.3.blocks
  34.6 0.3 collective-permute-start.3
  34.9 4.5 %collective-permute-done.4.refs_2_ = bf16[256,512]{1,0:T(8,128)(2,1)} collective-permute-done((bf16[256,512]{1,0:T(8,128)(2,1)S(1)}, bf16[256,512]{1,0:T(8,128)(2,1)}, u32[]{:S(2)}, u32[]{:S(2)}) %collective-permute-start.4) | collective-permute-done | bytes 262176 | tf_op jit(solution)/shard_map/ppermute | solution.py:164
  39.5 5.8 %copy-done = bf16[1024,8192]{1,0:T(8,128)(2,1)S(1)} copy-done((bf16[1024,8192]{1,0:T(8,128)(2,1)S(1)}, bf16[1024,8192]{1,0:T(8,128)(2,1)}, u32[]{:S(2)}) %copy-start) | copy-done | bytes 16777240
  45.2 0.9 copy-done.6
  46.2 0.9 copy-done.8
  47.1 4.2 %shard_map.64.refs_8_ = f32[256,1024]{1,0:T(8,128)S(1)} custom-call(s32[4]{0:T(128)S(1)} %pad_add_fusion.4.blocks, bf16[256,512]{1,0:T(8,128)(2,1)S(1)} %copy-done.6, bf16[256,512]{1,0:T(8,128)(2,1)S(1)} %copy-done.8, bf16[256,512]{1,0:T(8,128)(2,1)} %collective-permute-done.15.refs_2_, bf16[256,512]{1,0:T(8,128)(2,1)} %collective-permute-done.16.refs_3_, ...), custom_call_target="tpu_custom_call" | custom-call | flops 1073741824 | bytes 4194304 | tf_op jit(solution)/shard_map/pallas_call | solution.py:22
  51.3 1.7 %copy-done.1 = bf16[1024,8192]{1,0:T(8,128)(2,1)S(1)} copy-done((bf16[1024,8192]{1,0:T(8,128)(2,1)S(1)}, bf16[1024,8192]{1,0:T(8,128)(2,1)}, u32[]{:S(2)}) %copy-start.1) | copy-done | bytes 16777240
  53.1 4.1 %shard_map.65.refs_8_ = f32[256,1024]{1,0:T(8,128)S(1)} custom-call(s32[4]{0:T(128)S(1)} %pad_add_fusion.3.blocks, bf16[256,512]{1,0:T(8,128)(2,1)S(1)} %collective-permute-done.refs_0_, bf16[256,512]{1,0:T(8,128)(2,1)} %collective-permute-done.11.refs_1_, bf16[256,512]{1,0:T(8,128)(2,1)} %collective-permute-done.12.refs_2_, ...), custom_call_target="tpu_custom_call" | custom-call | flops 1073741824 | bytes 4194304 | tf_op jit(solution)/shard_map/pallas_call | solution.py:22
  57.2 3.9 %shard_map.66.refs_8_ = f32[256,1024]{1,0:T(8,128)S(1)} custom-call(s32[4]{0:T(128)S(1)} %pad_add_fusion.2.blocks, bf16[256,512]{1,0:T(8,128)(2,1)S(1)} %add.175.refs_0_, bf16[256,512]{1,0:T(8,128)(2,1)S(1)} %collective-permute-done.8.refs_1_, bf16[256,512]{1,0:T(8,128)(2,1)} %collective-permute-done.9.refs_2_, ...), custom_call_target="tpu_custom_call" | custom-call | flops 1073741824 | bytes 4194304 | tf_op jit(solution)/shard_map/pallas_call | solution.py:22
  61.1 4.1 %shard_map.68 = (bf16[256,1024]{1,0:T(8,128)(2,1)S(1)}, bf16[256,1024]{1,0:T(8,128)(2,1)S(1)}) custom-call(s32[4]{0:T(128)S(1)} %pad_add_fusion.1.blocks, bf16[256,512]{1,0:T(8,128)(2,1)S(1)} %add.168.refs_0_, bf16[256,512]{1,0:T(8,128)(2,1)S(1)} %collective-permute-done.3.refs_1_, bf16[256,512]{1,0:T(8,128)(2,1)} %collective-permute-done.4.refs_2_, ...), custom_call_target="tpu_custom_call" | custom-call | flops 1073741824 | bytes 4194304 | tf_op jit(solution)/shard_map/pallas_call | solution.py:22
  65.2 5.8 %copy-done.2 = bf16[8192,1024]{1,0:T(8,128)(2,1)S(1)} copy-done((bf16[8192,1024]{1,0:T(8,128)(2,1)S(1)}, bf16[8192,1024]{1,0:T(8,128)(2,1)}, u32[]{:S(2)}) %copy-start.2) | copy-done | bytes 16777240
  71.0 4.2 %shard_map.75 = bf16[256,1024]{1,0:T(8,128)(2,1)S(1)} custom-call(s32[2]{0:T(128)S(1)} %pad_add_fusion.11.blocks, bf16[256,1024]{1,0:T(8,128)(2,1)S(1)} %get-tuple-element.19.grad_gate, bf16[256,1024]{1,0:T(8,128)(2,1)S(1)} %get-tuple-element.20.grad_up, bf16[8192,1024]{1,0:T(8,128)(2,1)S(1)} %copy-done.2, bf16[8192,1024]{1,0:T(8,128)(2,1)} %w_up.15), custom_call_target="tpu_custom_call" | custom-call | flops 1073741824 | bytes 4194304 | tf_op jit(solution)/shard_map/pallas_call | solution.py:22
  75.2 0.6 collective-permute-start.25
  75.9 5.8 %copy-done.3 = bf16[8192,1024]{1,0:T(8,128)(2,1)S(1)} copy-done((bf16[8192,1024]{1,0:T(8,128)(2,1)S(1)}, bf16[8192,1024]{1,0:T(8,128)(2,1)}, u32[]{:S(2)}) %copy-start.3) | copy-done | bytes 16777240
  81.7 4.2 %shard_map.71 = bf16[256,1024]{1,0:T(8,128)(2,1)S(1)} custom-call(s32[2]{0:T(128)S(1)} %pad_add_fusion.7.blocks, bf16[256,1024]{1,0:T(8,128)(2,1)S(1)} %get-tuple-element.19.grad_gate, bf16[256,1024]{1,0:T(8,128)(2,1)S(1)} %get-tuple-element.20.grad_up, bf16[8192,1024]{1,0:T(8,128)(2,1)S(1)} %copy-done.3, bf16[8192,1024]{1,0:T(8,128)(2,1)} %w_up.15), custom_call_target="tpu_custom_call" | custom-call | flops 1073741824 | bytes 4194304 | tf_op jit(solution)/shard_map/pallas_call | solution.py:22
  86.0 0.1 collective-permute-start.19
  86.0 0.1 pad_add_fusion.9.blocks
  86.1 4.2 %shard_map.73 = bf16[256,1024]{1,0:T(8,128)(2,1)S(1)} custom-call(s32[2]{0:T(128)S(1)} %pad_add_fusion.9.blocks, bf16[256,1024]{1,0:T(8,128)(2,1)S(1)} %get-tuple-element.19.grad_gate, bf16[256,1024]{1,0:T(8,128)(2,1)S(1)} %get-tuple-element.20.grad_up, bf16[8192,1024]{1,0:T(8,128)(2,1)S(1)} %copy-done.3, bf16[8192,1024]{1,0:T(8,128)(2,1)} %w_up.15), custom_call_target="tpu_custom_call" | custom-call | flops 1073741824 | bytes 4194304 | tf_op jit(solution)/shard_map/pallas_call | solution.py:22
  90.4 0.6 collective-permute-start.23
  90.9 4.4 %shard_map.76 = (f32[256,512]{1,0:T(8,128)S(1)}, bf16[256,512]{1,0:T(8,128)(2,1)S(1)}) custom-call(s32[2]{0:T(128)S(1)} %pad_add_fusion.10.blocks, bf16[256,1024]{1,0:T(8,128)(2,1)S(1)} %get-tuple-element.19.grad_gate, bf16[256,1024]{1,0:T(8,128)(2,1)S(1)} %get-tuple-element.20.grad_up, bf16[8192,1024]{1,0:T(8,128)(2,1)S(1)} %copy-done.3, ...), custom_call_target="tpu_custom_call" | custom-call | flops 1073741824 | bytes 4194304 | tf_op jit(solution)/shard_map/pallas_call | solution.py:22
  95.3 0.6 collective-permute-start.26
  95.9 4.2 %shard_map.69 = bf16[256,1024]{1,0:T(8,128)(2,1)S(1)} custom-call(s32[2]{0:T(128)S(1)} %pad_add_fusion.5.blocks, bf16[256,1024]{1,0:T(8,128)(2,1)S(1)} %get-tuple-element.19.grad_gate, bf16[256,1024]{1,0:T(8,128)(2,1)S(1)} %get-tuple-element.20.grad_up, bf16[8192,1024]{1,0:T(8,128)(2,1)S(1)} %copy-done.3, bf16[8192,1024]{1,0:T(8,128)(2,1)} %w_up.15), custom_call_target="tpu_custom_call" | custom-call | flops 1073741824 | bytes 4194304 | tf_op jit(solution)/shard_map/pallas_call | solution.py:22
  100.3 4.4 %shard_map.72 = (f32[256,512]{1,0:T(8,128)S(1)}, bf16[256,512]{1,0:T(8,128)(2,1)S(1)}) custom-call(s32[2]{0:T(128)S(1)} %pad_add_fusion.6.blocks, bf16[256,1024]{1,0:T(8,128)(2,1)S(1)} %get-tuple-element.19.grad_gate, bf16[256,1024]{1,0:T(8,128)(2,1)S(1)} %get-tuple-element.20.grad_up, bf16[8192,1024]{1,0:T(8,128)(2,1)S(1)} %copy-done.3, ...), custom_call_target="tpu_custom_call" | custom-call | flops 1073741824 | bytes 4194304 | tf_op jit(solution)/shard_map/pallas_call | solution.py:22
  104.6 1.6 %collective-permute-start.20 = (bf16[256,512]{1,0:T(8,128)(2,1)S(1)}, bf16[256,512]{1,0:T(8,128)(2,1)S(1)}, u32[]{:S(2)}, u32[]{:S(2)}) collective-permute-start(bf16[256,512]{1,0:T(8,128)(2,1)S(1)} %get-tuple-element.24), channel_id=1, source_target_pairs={{0,2},{1,3},{2,0},{3,1},{4,6},{5,7},{6,4},{7,5},{8,10},{9,11},{10,... | collective-permute-start | bytes 786440 | tf_op jit(solution)/shard_map/ppermute | solution.py:164
  106.3 3.2 %collective-permute-start.27 = (bf16[256,512]{1,0:T(8,128)(2,1)S(1)}, bf16[256,512]{1,0:T(8,128)(2,1)S(1)}, u32[]{:S(2)}, u32[]{:S(2)}) collective-permute-start(bf16[256,512]{1,0:T(8,128)(2,1)S(1)} %fusion.1), channel_id=1, source_target_pairs={{0,4},{1,5},{2,6},{3,7},{12,8},{13,9},{14,10},{15,11},{16,20},{17,... | collective-permute-start | bytes 786440 | tf_op jit(solution)/shard_map/ppermute | solution.py:164
  109.5 4.4 %shard_map.74 = (f32[256,512]{1,0:T(8,128)S(1)}, bf16[256,512]{1,0:T(8,128)(2,1)S(1)}) custom-call(s32[2]{0:T(128)S(1)} %pad_add_fusion.8.blocks, bf16[256,1024]{1,0:T(8,128)(2,1)S(1)} %get-tuple-element.19.grad_gate, bf16[256,1024]{1,0:T(8,128)(2,1)S(1)} %get-tuple-element.20.grad_up, bf16[8192,1024]{1,0:T(8,128)(2,1)S(1)} %copy-done.3, ...), custom_call_target="tpu_custom_call" | custom-call | flops 1073741824 | bytes 4194304 | tf_op jit(solution)/shard_map/pallas_call | solution.py:22
  113.9 1.6 %collective-permute-start.24 = (bf16[256,512]{1,0:T(8,128)(2,1)S(1)}, bf16[256,512]{1,0:T(8,128)(2,1)S(1)}, u32[]{:S(2)}, u32[]{:S(2)}) collective-permute-start(bf16[256,512]{1,0:T(8,128)(2,1)S(1)} %get-tuple-element.26), channel_id=1, source_target_pairs={{0,2},{1,3},{2,0},{3,1},{4,6},{5,7},{6,4},{7,5},{8,10},{9,11},{10,... | collective-permute-start | bytes 786440 | tf_op jit(solution)/shard_map/ppermute | solution.py:164
  115.5 0.1 fusion
  115.6 2.1 %collective-permute-start.21 = (bf16[256,512]{1,0:T(8,128)(2,1)S(1)}, bf16[256,512]{1,0:T(8,128)(2,1)S(1)}, u32[]{:S(2)}, u32[]{:S(2)}) collective-permute-start(bf16[256,512]{1,0:T(8,128)(2,1)S(1)} %fusion), channel_id=1, source_target_pairs={{0,4},{1,5},{2,6},{3,7},{12,8},{13,9},{14,10},{15,11},{16,20},{17,... | collective-permute-start | bytes 786440 | tf_op jit(solution)/shard_map/ppermute | solution.py:164
  117.7 0.1 add_convert_fusion.2
  117.8 0.7 collective-permute-start.28
  118.5 4.4 %shard_map.70 = (f32[256,512]{1,0:T(8,128)S(1)}, bf16[256,512]{1,0:T(8,128)(2,1)S(1)}) custom-call(s32[2]{0:T(128)S(1)} %pad_add_fusion.blocks, bf16[256,1024]{1,0:T(8,128)(2,1)S(1)} %get-tuple-element.19.grad_gate, bf16[256,1024]{1,0:T(8,128)(2,1)S(1)} %get-tuple-element.20.grad_up, bf16[8192,1024]{1,0:T(8,128)(2,1)S(1)} %copy-done.3, ...), custom_call_target="tpu_custom_call" | custom-call | flops 1073741824 | bytes 4194304 | tf_op jit(solution)/shard_map/pallas_call | solution.py:22
  122.9 0.6 collective-permute-start.18
  123.5 0.1 add_convert_fusion.3
  123.6 0.7 collective-permute-start.22
  124.3 0.1 add_convert_fusion.1
  124.4 5.7 %collective-permute-start.29 = (bf16[256,512]{1,0:T(8,128)(2,1)S(1)}, bf16[256,512]{1,0:T(8,128)(2,1)S(1)}, u32[]{:S(2)}, u32[]{:S(2)}) collective-permute-start(bf16[256,512]{1,0:T(8,128)(2,1)S(1)} %add_convert_fusion.1), channel_id=1, source_target_pairs={{0,4},{1,5},{2,6},{3,7},{4,0},{5,1},{6,2},{7,3},{8,12},{9,13},{10,... | collective-permute-start | bytes 786440 | tf_op jit(solution)/shard_map/ppermute | solution.py:164
  130.2 0.4 collective-permute-done.18
  130.6 4.6 %collective-permute-done.29 = bf16[256,512]{1,0:T(8,128)(2,1)S(1)} collective-permute-done((bf16[256,512]{1,0:T(8,128)(2,1)S(1)}, bf16[256,512]{1,0:T(8,128)(2,1)S(1)}, u32[]{:S(2)}, u32[]{:S(2)}) %collective-permute-start.29) | collective-permute-done | bytes 262176 | tf_op jit(solution)/shard_map/ppermute | solution.py:164
  135.2 0.8 add_convert_fusion
  (47 shorter events, 0.8 us)
Async XLA Ops:
  0.0 9.5 %collective-permute-start = (bf16[256,512]{1,0:T(8,128)(2,1)}, bf16[256,512]{1,0:T(8,128)(2,1)S(1)}, u32[]{:S(2)}, u32[]{:S(2)}) collective-permute-start(bf16[256,512]{1,0:T(8,128)(2,1)} %refs_0_.1), channel_id=1, source_target_pairs={{0,4},{1,5},{2,6},{3,7},{4,0},{5,1},{6,2},{7,3},{8,12},{9,13},{10,... | collective-permute-start | bytes 786440 | tf_op jit(solution)/shard_map/ppermute | solution.py:164
  3.0 9.1 %collective-permute-start.6 = (bf16[256,512]{1,0:T(8,128)(2,1)}, bf16[256,512]{1,0:T(8,128)(2,1)S(1)}, u32[]{:S(2)}, u32[]{:S(2)}) collective-permute-start(bf16[256,512]{1,0:T(8,128)(2,1)} %refs_0_.1), channel_id=1, source_target_pairs={{4,8},{5,9},{6,10},{7,11},{8,4},{9,5},{10,6},{11,7},{20,24},{21,25... | collective-permute-start | bytes 786440 | tf_op jit(solution)/shard_map/ppermute | solution.py:164
  9.5 4.0 %collective-permute-start.1 = (bf16[256,512]{1,0:T(8,128)(2,1)S(1)}, bf16[256,512]{1,0:T(8,128)(2,1)S(1)}, u32[]{:S(2)}, u32[]{:S(2)}) collective-permute-start(bf16[256,512]{1,0:T(8,128)(2,1)S(1)} %collective-permute-done.refs_0_), channel_id=1, source_target_pairs={{4,8},{5,9},{6,10},{7,11},{8,4},{9,5},{10,6},{11,7},{20,24},{21,25... | collective-permute-start | bytes 786440 | tf_op jit(solution)/shard_map/ppermute | solution.py:164
  10.2 19.9 %collective-permute-start.14 = (bf16[256,512]{1,0:T(8,128)(2,1)}, bf16[256,512]{1,0:T(8,128)(2,1)S(1)}, u32[]{:S(2)}, u32[]{:S(2)}) collective-permute-start(bf16[256,512]{1,0:T(8,128)(2,1)} %refs_0_.1), channel_id=1, source_target_pairs={{0,1},{1,0},{2,3},{3,2},{4,5},{5,4},{6,7},{7,6},{8,9},{9,8},{10,11... | collective-permute-start | bytes 786440 | tf_op jit(solution)/shard_map/ppermute | solution.py:164
  10.3 14.6 %collective-permute-start.15 = (bf16[256,512]{1,0:T(8,128)(2,1)}, bf16[256,512]{1,0:T(8,128)(2,1)}, u32[]{:S(2)}, u32[]{:S(2)}) collective-permute-start(bf16[256,512]{1,0:T(8,128)(2,1)} %refs_0_.1), channel_id=1, source_target_pairs={{0,2},{1,3},{2,0},{3,1},{4,6},{5,7},{6,4},{7,5},{8,10},{9,11},{10,... | collective-permute-start | bytes 786440 | tf_op jit(solution)/shard_map/ppermute | solution.py:164
  12.1 12.7 %collective-permute-start.7 = (bf16[256,512]{1,0:T(8,128)(2,1)S(1)}, bf16[256,512]{1,0:T(8,128)(2,1)S(1)}, u32[]{:S(2)}, u32[]{:S(2)}) collective-permute-start(bf16[256,512]{1,0:T(8,128)(2,1)S(1)} %collective-permute-done.6), channel_id=1, source_target_pairs={{4,0},{5,1},{6,2},{7,3},{8,12},{9,13},{10,14},{11,15},{20,16},{21,... | collective-permute-start | bytes 786440 | tf_op jit(solution)/shard_map/ppermute | solution.py:164
  13.5 16.5 %collective-permute-start.2 = (bf16[256,512]{1,0:T(8,128)(2,1)S(1)}, bf16[256,512]{1,0:T(8,128)(2,1)S(1)}, u32[]{:S(2)}, u32[]{:S(2)}) collective-permute-start(bf16[256,512]{1,0:T(8,128)(2,1)S(1)} %collective-permute-done.1), channel_id=1, source_target_pairs={{4,0},{5,1},{6,2},{7,3},{8,12},{9,13},{10,14},{11,15},{20,16},{21,... | collective-permute-start | bytes 786440 | tf_op jit(solution)/shard_map/ppermute | solution.py:164
  14.9 15.9 %collective-permute-start.12 = (bf16[256,512]{1,0:T(8,128)(2,1)S(1)}, bf16[256,512]{1,0:T(8,128)(2,1)}, u32[]{:S(2)}, u32[]{:S(2)}) collective-permute-start(bf16[256,512]{1,0:T(8,128)(2,1)S(1)} %collective-permute-done.refs_0_), channel_id=1, source_target_pairs={{0,2},{1,3},{2,0},{3,1},{4,6},{5,7},{6,4},{7,5},{8,10},{9,11},{10,... | collective-permute-start | bytes 786440 | tf_op jit(solution)/shard_map/ppermute | solution.py:164
  24.9 9.1 %collective-permute-start.11 = (bf16[256,512]{1,0:T(8,128)(2,1)S(1)}, bf16[256,512]{1,0:T(8,128)(2,1)}, u32[]{:S(2)}, u32[]{:S(2)}) collective-permute-start(bf16[256,512]{1,0:T(8,128)(2,1)S(1)} %collective-permute-done.refs_0_), channel_id=1, source_target_pairs={{0,1},{1,0},{2,3},{3,2},{4,5},{5,4},{6,7},{7,6},{8,9},{9,8},{10,11... | collective-permute-start | bytes 786440 | tf_op jit(solution)/shard_map/ppermute | solution.py:164
  24.9 9.4 %collective-permute-start.9 = (bf16[256,512]{1,0:T(8,128)(2,1)S(1)}, bf16[256,512]{1,0:T(8,128)(2,1)}, u32[]{:S(2)}, u32[]{:S(2)}) collective-permute-start(bf16[256,512]{1,0:T(8,128)(2,1)S(1)} %add.175.refs_0_), channel_id=1, source_target_pairs={{0,2},{1,3},{2,0},{3,1},{4,6},{5,7},{6,4},{7,5},{8,10},{9,11},{10,... | collective-permute-start | bytes 786440 | tf_op jit(solution)/shard_map/ppermute | solution.py:164
  30.0 4.6 %collective-permute-start.16 = (bf16[256,512]{1,0:T(8,128)(2,1)}, bf16[256,512]{1,0:T(8,128)(2,1)}, u32[]{:S(2)}, u32[]{:S(2)}) collective-permute-start(bf16[256,512]{1,0:T(8,128)(2,1)} %collective-permute-done.15.refs_2_), channel_id=1, source_target_pairs={{0,1},{1,0},{2,3},{3,2},{4,5},{5,4},{6,7},{7,6},{8,9},{9,8},{10,11... | collective-permute-start | bytes 786440 | tf_op jit(solution)/shard_map/ppermute | solution.py:164
  30.1 9.3 %copy-start.7 = (bf16[256,512]{1,0:T(8,128)(2,1)}, bf16[256,512]{1,0:T(8,128)(2,1)S(1)}, u32[]{:S(2)}) copy-start(bf16[256,512]{1,0:T(8,128)(2,1)S(1)} %collective-permute-done.14.refs_1_) | copy-start | bytes 786436
  30.1 9.3 %collective-permute-start.4 = (bf16[256,512]{1,0:T(8,128)(2,1)S(1)}, bf16[256,512]{1,0:T(8,128)(2,1)}, u32[]{:S(2)}, u32[]{:S(2)}) collective-permute-start(bf16[256,512]{1,0:T(8,128)(2,1)S(1)} %add.168.refs_0_), channel_id=1, source_target_pairs={{0,2},{1,3},{2,0},{3,1},{4,6},{5,7},{6,4},{7,5},{8,10},{9,11},{10,... | collective-permute-start | bytes 786440 | tf_op jit(solution)/shard_map/ppermute | solution.py:164
  30.8 20.6 %collective-permute-start.13 = (bf16[256,512]{1,0:T(8,128)(2,1)}, bf16[256,512]{1,0:T(8,128)(2,1)}, u32[]{:S(2)}, u32[]{:S(2)}) collective-permute-start(bf16[256,512]{1,0:T(8,128)(2,1)} %collective-permute-done.12.refs_2_), channel_id=1, source_target_pairs={{0,1},{1,0},{2,3},{3,2},{4,5},{5,4},{6,7},{7,6},{8,9},{9,8},{10,11... | collective-permute-start | bytes 786440 | tf_op jit(solution)/shard_map/ppermute | solution.py:164
  31.1 1.0 copy-start.4
  32.1 1.0 copy-start.5
  34.0 23.2 %collective-permute-start.8 = (bf16[256,512]{1,0:T(8,128)(2,1)S(1)}, bf16[256,512]{1,0:T(8,128)(2,1)S(1)}, u32[]{:S(2)}, u32[]{:S(2)}) collective-permute-start(bf16[256,512]{1,0:T(8,128)(2,1)S(1)} %add.175.refs_0_), channel_id=1, source_target_pairs={{0,1},{1,0},{2,3},{3,2},{4,5},{5,4},{6,7},{7,6},{8,9},{9,8},{10,11... | collective-permute-start | bytes 786440 | tf_op jit(solution)/shard_map/ppermute | solution.py:164
  34.3 22.8 %collective-permute-start.10 = (bf16[256,512]{1,0:T(8,128)(2,1)}, bf16[256,512]{1,0:T(8,128)(2,1)S(1)}, u32[]{:S(2)}, u32[]{:S(2)}) collective-permute-start(bf16[256,512]{1,0:T(8,128)(2,1)} %collective-permute-done.9.refs_2_), channel_id=1, source_target_pairs={{0,1},{1,0},{2,3},{3,2},{4,5},{5,4},{6,7},{7,6},{8,9},{9,8},{10,11... | collective-permute-start | bytes 786440 | tf_op jit(solution)/shard_map/ppermute | solution.py:164
  34.6 26.4 %collective-permute-start.3 = (bf16[256,512]{1,0:T(8,128)(2,1)S(1)}, bf16[256,512]{1,0:T(8,128)(2,1)S(1)}, u32[]{:S(2)}, u32[]{:S(2)}) collective-permute-start(bf16[256,512]{1,0:T(8,128)(2,1)S(1)} %add.168.refs_0_), channel_id=1, source_target_pairs={{0,1},{1,0},{2,3},{3,2},{4,5},{5,4},{6,7},{7,6},{8,9},{9,8},{10,11... | collective-permute-start | bytes 786440 | tf_op jit(solution)/shard_map/ppermute | solution.py:164
  39.4 21.6 %collective-permute-start.5 = (bf16[256,512]{1,0:T(8,128)(2,1)}, bf16[256,512]{1,0:T(8,128)(2,1)S(1)}, u32[]{:S(2)}, u32[]{:S(2)}) collective-permute-start(bf16[256,512]{1,0:T(8,128)(2,1)} %collective-permute-done.4.refs_2_), channel_id=1, source_target_pairs={{0,1},{1,0},{2,3},{3,2},{4,5},{5,4},{6,7},{7,6},{8,9},{9,8},{10,11... | collective-permute-start | bytes 786440 | tf_op jit(solution)/shard_map/ppermute | solution.py:164
  39.5 5.8 %copy-start = (bf16[1024,8192]{1,0:T(8,128)(2,1)S(1)}, bf16[1024,8192]{1,0:T(8,128)(2,1)}, u32[]{:S(2)}) copy-start(bf16[1024,8192]{1,0:T(8,128)(2,1)} %refs_7_.7) | copy-start | bytes 50331652
  45.2 0.9 copy-start.6
  46.2 0.9 copy-start.8
  47.1 5.9 %copy-start.1 = (bf16[1024,8192]{1,0:T(8,128)(2,1)S(1)}, bf16[1024,8192]{1,0:T(8,128)(2,1)}, u32[]{:S(2)}) copy-start(bf16[1024,8192]{1,0:T(8,128)(2,1)} %refs_7_.7) | copy-start | bytes 50331652
  65.2 5.8 %copy-start.2 = (bf16[8192,1024]{1,0:T(8,128)(2,1)S(1)}, bf16[8192,1024]{1,0:T(8,128)(2,1)}, u32[]{:S(2)}) copy-start(bf16[8192,1024]{1,0:T(8,128)(2,1)} %w_gate.15) | copy-start | bytes 50331652
  75.2 15.7 %collective-permute-start.25 = (bf16[256,1024]{1,0:T(8,128)(2,1)S(1)}, bf16[256,1024]{1,0:T(8,128)(2,1)S(1)}, u32[]{:S(2)}, u32[]{:S(2)}) collective-permute-start(bf16[256,1024]{1,0:T(8,128)(2,1)S(1)} %shard_map.75), channel_id=1, source_target_pairs={{0,1},{1,0},{2,3},{3,2},{4,5},{5,4},{6,7},{7,6},{8,9},{9,8},{10,11... | collective-permute-start | bytes 1572872 | tf_op jit(solution)/shard_map/ppermute | solution.py:164
  75.9 5.8 %copy-start.3 = (bf16[8192,1024]{1,0:T(8,128)(2,1)S(1)}, bf16[8192,1024]{1,0:T(8,128)(2,1)}, u32[]{:S(2)}) copy-start(bf16[8192,1024]{1,0:T(8,128)(2,1)} %w_gate.15) | copy-start | bytes 50331652
  86.0 14.3 %collective-permute-start.19 = (bf16[256,1024]{1,0:T(8,128)(2,1)S(1)}, bf16[256,1024]{1,0:T(8,128)(2,1)S(1)}, u32[]{:S(2)}, u32[]{:S(2)}) collective-permute-start(bf16[256,1024]{1,0:T(8,128)(2,1)S(1)} %shard_map.71), channel_id=1, source_target_pairs={{0,1},{1,0},{2,3},{3,2},{4,5},{5,4},{6,7},{7,6},{8,9},{9,8},{10,11... | collective-permute-start | bytes 1572872 | tf_op jit(solution)/shard_map/ppermute | solution.py:164
  90.4 19.2 %collective-permute-start.23 = (bf16[256,1024]{1,0:T(8,128)(2,1)S(1)}, bf16[256,1024]{1,0:T(8,128)(2,1)S(1)}, u32[]{:S(2)}, u32[]{:S(2)}) collective-permute-start(bf16[256,1024]{1,0:T(8,128)(2,1)S(1)} %shard_map.73), channel_id=1, source_target_pairs={{0,1},{1,0},{2,3},{3,2},{4,5},{5,4},{6,7},{7,6},{8,9},{9,8},{10,11... | collective-permute-start | bytes 1572872 | tf_op jit(solution)/shard_map/ppermute | solution.py:164
  95.3 10.9 %collective-permute-start.26 = (bf16[256,512]{1,0:T(8,128)(2,1)S(1)}, bf16[256,512]{1,0:T(8,128)(2,1)S(1)}, u32[]{:S(2)}, u32[]{:S(2)}) collective-permute-start(bf16[256,512]{1,0:T(8,128)(2,1)S(1)} %get-tuple-element.28), channel_id=1, source_target_pairs={{0,2},{1,3},{2,0},{3,1},{4,6},{5,7},{6,4},{7,5},{8,10},{9,11},{10,... | collective-permute-start | bytes 786440 | tf_op jit(solution)/shard_map/ppermute | solution.py:164
  100.2 18.4 %collective-permute-start.17 = (bf16[256,1024]{1,0:T(8,128)(2,1)S(1)}, bf16[256,1024]{1,0:T(8,128)(2,1)S(1)}, u32[]{:S(2)}, u32[]{:S(2)}) collective-permute-start(bf16[256,1024]{1,0:T(8,128)(2,1)S(1)} %shard_map.69), channel_id=1, source_target_pairs={{0,1},{1,0},{2,3},{3,2},{4,5},{5,4},{6,7},{7,6},{8,9},{9,8},{10,11... | collective-permute-start | bytes 1572872 | tf_op jit(solution)/shard_map/ppermute | solution.py:164
  104.6 10.9 %collective-permute-start.20 = (bf16[256,512]{1,0:T(8,128)(2,1)S(1)}, bf16[256,512]{1,0:T(8,128)(2,1)S(1)}, u32[]{:S(2)}, u32[]{:S(2)}) collective-permute-start(bf16[256,512]{1,0:T(8,128)(2,1)S(1)} %get-tuple-element.24), channel_id=1, source_target_pairs={{0,2},{1,3},{2,0},{3,1},{4,6},{5,7},{6,4},{7,5},{8,10},{9,11},{10,... | collective-permute-start | bytes 786440 | tf_op jit(solution)/shard_map/ppermute | solution.py:164
  106.3 11.4 %collective-permute-start.27 = (bf16[256,512]{1,0:T(8,128)(2,1)S(1)}, bf16[256,512]{1,0:T(8,128)(2,1)S(1)}, u32[]{:S(2)}, u32[]{:S(2)}) collective-permute-start(bf16[256,512]{1,0:T(8,128)(2,1)S(1)} %fusion.1), channel_id=1, source_target_pairs={{0,4},{1,5},{2,6},{3,7},{12,8},{13,9},{14,10},{15,11},{16,20},{17,... | collective-permute-start | bytes 786440 | tf_op jit(solution)/shard_map/ppermute | solution.py:164
  113.9 10.4 %collective-permute-start.24 = (bf16[256,512]{1,0:T(8,128)(2,1)S(1)}, bf16[256,512]{1,0:T(8,128)(2,1)S(1)}, u32[]{:S(2)}, u32[]{:S(2)}) collective-permute-start(bf16[256,512]{1,0:T(8,128)(2,1)S(1)} %get-tuple-element.26), channel_id=1, source_target_pairs={{0,2},{1,3},{2,0},{3,1},{4,6},{5,7},{6,4},{7,5},{8,10},{9,11},{10,... | collective-permute-start | bytes 786440 | tf_op jit(solution)/shard_map/ppermute | solution.py:164
  115.6 7.9 %collective-permute-start.21 = (bf16[256,512]{1,0:T(8,128)(2,1)S(1)}, bf16[256,512]{1,0:T(8,128)(2,1)S(1)}, u32[]{:S(2)}, u32[]{:S(2)}) collective-permute-start(bf16[256,512]{1,0:T(8,128)(2,1)S(1)} %fusion), channel_id=1, source_target_pairs={{0,4},{1,5},{2,6},{3,7},{12,8},{13,9},{14,10},{15,11},{16,20},{17,... | collective-permute-start | bytes 786440 | tf_op jit(solution)/shard_map/ppermute | solution.py:164
  117.8 6.5 %collective-permute-start.28 = (bf16[256,512]{1,0:T(8,128)(2,1)S(1)}, bf16[256,512]{1,0:T(8,128)(2,1)S(1)}, u32[]{:S(2)}, u32[]{:S(2)}) collective-permute-start(bf16[256,512]{1,0:T(8,128)(2,1)S(1)} %add_convert_fusion.2), channel_id=1, source_target_pairs={{4,8},{5,9},{6,10},{7,11},{8,4},{9,5},{10,6},{11,7},{20,24},{21,25... | collective-permute-start | bytes 786440 | tf_op jit(solution)/shard_map/ppermute | solution.py:164
  122.9 7.7 %collective-permute-start.18 = (bf16[256,512]{1,0:T(8,128)(2,1)S(1)}, bf16[256,512]{1,0:T(8,128)(2,1)S(1)}, u32[]{:S(2)}, u32[]{:S(2)}) collective-permute-start(bf16[256,512]{1,0:T(8,128)(2,1)S(1)} %get-tuple-element.22), channel_id=1, source_target_pairs={{0,2},{1,3},{2,0},{3,1},{4,6},{5,7},{6,4},{7,5},{8,10},{9,11},{10,... | collective-permute-start | bytes 786440 | tf_op jit(solution)/shard_map/ppermute | solution.py:164
  123.6 7.0 %collective-permute-start.22 = (bf16[256,512]{1,0:T(8,128)(2,1)S(1)}, bf16[256,512]{1,0:T(8,128)(2,1)S(1)}, u32[]{:S(2)}, u32[]{:S(2)}) collective-permute-start(bf16[256,512]{1,0:T(8,128)(2,1)S(1)} %add_convert_fusion.3), channel_id=1, source_target_pairs={{4,8},{5,9},{6,10},{7,11},{8,4},{9,5},{10,6},{11,7},{20,24},{21,25... | collective-permute-start | bytes 786440 | tf_op jit(solution)/shard_map/ppermute | solution.py:164
  124.4 10.8 %collective-permute-start.29 = (bf16[256,512]{1,0:T(8,128)(2,1)S(1)}, bf16[256,512]{1,0:T(8,128)(2,1)S(1)}, u32[]{:S(2)}, u32[]{:S(2)}) collective-permute-start(bf16[256,512]{1,0:T(8,128)(2,1)S(1)} %add_convert_fusion.1), channel_id=1, source_target_pairs={{0,4},{1,5},{2,6},{3,7},{4,0},{5,1},{6,2},{7,3},{8,12},{9,13},{10,... | collective-permute-start | bytes 786440 | tf_op jit(solution)/shard_map/ppermute | solution.py:164

commit v2 on v0

v2 whole, which is shorter than its diff:
```python
import functools

import jax
import jax.numpy as jnp
from jax import lax
from jax.experimental import pallas as pl
from jax.experimental.pallas import tpu as pltpu
from jax.sharding import PartitionSpec as P

BF16, F32 = jnp.bfloat16, jnp.float32
TILE = 256
VMEM = 16 * 2**20


def contract_last(left, right):
    return lax.dot_general(
        left, right, (((1,), (1,)), ((), ())), preferred_element_type=F32
    )


def call(body, blocks, ins, outs, args, scratch, micros):
    return pl.pallas_call(
        body,
        in_specs=[pl.BlockSpec(memory_space=space) for space in (pltpu.SMEM, *ins)],
        out_specs=[pl.BlockSpec(memory_space=pltpu.VMEM) for _ in outs],
        out_shape=outs,
        scratch_shapes=scratch,
        compiler_params=pltpu.CompilerParams(vmem_limit_bytes=VMEM),
        cost_estimate=pl.CostEstimate(flops=int(micros * 1e9), bytes_accessed=0, transcendentals=0),
    )(blocks, *args)


class Ahead:
    def __init__(self, blocks, first, weights, outs, sem):
        self.blocks, self.first, self.weights, self.outs, self.sem = blocks, first, weights, outs, sem
        self.width = outs[0].shape[0] // 4

    def copies(self, j):
        source = pl.ds(pl.multiple_of(self.blocks[self.first + j] * self.width, self.width), self.width)
        at = pl.ds(j * self.width, self.width)
        return [
            pltpu.make_async_copy(weight.at[source], out.at[at], self.sem.at[k, j])
            for k, (weight, out) in enumerate(zip(self.weights, self.outs))
        ]

    def start(self):
        for j in range(4):
            for copy in self.copies(j):
                copy.start()

    def wait(self):
        for j in range(4):
            for copy in self.copies(j):
                copy.wait()


def factors_body(
    blocks, gate, up, w_gate, w_up, to_gate_ref, to_up_ref, ahead_gate, ahead_up, gate_ref, up_ref, saved_sem, sem
):
    saved = [
        pltpu.make_async_copy(source, to, saved_sem.at[k])
        for k, (source, to) in enumerate([(gate, gate_ref), (up, up_ref)])
    ]
    for copy in saved:
        copy.start()
    ahead = Ahead(blocks, 0, (w_gate, w_up), (ahead_gate, ahead_up), sem)
    ahead.start()
    for copy in saved:
        copy.wait()

    def step(i, carry):
        at = pl.ds(pl.multiple_of(i * 32, 32), 32)
        gate = gate_ref[at].astype(F32)
        up = up_ref[at].astype(F32)
        sig = jax.nn.sigmoid(gate)
        to_gate_ref[at] = up * sig * (1.0 + gate * (1.0 - sig))
        to_up_ref[at] = gate * sig
        return carry

    lax.fori_loop(0, gate_ref.shape[0] // 32, step, 0)
    ahead.wait()


def held_weights(weights, width):
    return [pltpu.VMEM((4 * width, weight.shape[1]), BF16) for weight in weights]


def factors(blocks, gate, up, weights, width):
    tok, ff = gate.shape
    outs = [jax.ShapeDtypeStruct((tok, ff), F32)] * 2 + held_weights(weights, width)
    ins = [pl.ANY] * 4
    scratch = [pltpu.VMEM((tok, ff), BF16)] * 2 + [pltpu.SemaphoreType.DMA((2,)), pltpu.SemaphoreType.DMA((2, 4))]
    *scale, ahead_gate, ahead_up = call(factors_body, blocks, ins, outs, (gate, up, *weights), scratch, 4.0)
    return scale, (ahead_gate, ahead_up)


def hidden_body(parts, first, last, fetch, blocks, *refs):
    refs = list(refs)
    pieces, w_down, rest = refs[:parts], refs[parts], refs[parts + 1 :]
    ahead_sem = rest.pop() if fetch else None
    piece_sem, weight_sem = rest.pop(), rest.pop()
    held, weights = rest.pop(), rest.pop()
    if fetch:
        outs = [rest.pop(), rest.pop()][::-1]
        ahead = Ahead(blocks, parts, [rest.pop(0), rest.pop(0)], outs, ahead_sem)
    before = None if first else rest.pop(0)
    width = pieces[0].shape[1]
    count = w_down.shape[0] // TILE

    def arrival(j):
        return pltpu.make_async_copy(pieces[j], held.at[:, pl.ds(j * width, width)], piece_sem.at[j])

    def weight(i, j):
        at = pl.ds(pl.multiple_of(i * TILE, TILE), TILE)
        source = pl.ds(pl.multiple_of(blocks[j] * width, width), width)
        return pltpu.make_async_copy(
            w_down.at[at, source], weights.at[at, pl.ds(j * width, width)], weight_sem.at[i, j]
        )

    def start(i, carry):
        for j in range(parts):
            weight(i, j).start()
        return carry

    for j in range(parts):
        arrival(j).start()
    lax.fori_loop(0, count, start, 0)
    if fetch:
        ahead.start()
    for j in range(parts):
        arrival(j).wait()

    def step(i, carry):
        for j in range(parts):
            weight(i, j).wait()
        at = pl.ds(pl.multiple_of(i * TILE, TILE), TILE)
        total = contract_last(held[...], weights[at])
        if not first:
            total = total + before[:, at]
        if last:
            to_gate, to_up, grad_gate, grad_up = rest
            grad_gate[:, at] = (total * to_gate[:, at]).astype(BF16)
            grad_up[:, at] = (total * to_up[:, at]).astype(BF16)
        else:
            rest[0][:, at] = total
        return carry

    lax.fori_loop(0, count, step, 0)
    if fetch:
        ahead.wait()


def hidden(blocks, pieces, w_down, total=None, scale=None, fetch=None):
    tok, width = pieces[0].shape
    ff = w_down.shape[0]
    parts = len(pieces)
    ins, args = [pl.ANY] * (parts + 1), (*pieces, w_down)
    if fetch is not None:
        ins, args = ins + [pl.ANY] * 2, (*args, *fetch)
    if total is not None:
        ins, args = ins + [pltpu.VMEM], (*args, total)
    if scale is not None:
        ins, args = ins + [pltpu.VMEM] * 2, (*args, *scale)
        outs = [jax.ShapeDtypeStruct((tok, ff), BF16)] * 2
    else:
        outs = [jax.ShapeDtypeStruct((tok, ff), F32)]
    scratch = [
        pltpu.VMEM((ff, parts * width), BF16),
        pltpu.VMEM((tok, parts * width), BF16),
        pltpu.SemaphoreType.DMA((ff // TILE, parts)),
        pltpu.SemaphoreType.DMA((parts,)),
    ]
    if fetch is not None:
        outs += held_weights(fetch, width)
        scratch.append(pltpu.SemaphoreType.DMA((2, 4)))
    body = functools.partial(hidden_body, parts, total is None, scale is not None, fetch is not None)
    done = call(body, blocks, ins, outs, args, scratch, 5.0 if fetch is not None else 3.0)
    return done


def partial_sum(at, grad_gate, grad_up, w_gate, w_up):
    return contract_last(grad_gate[...], w_gate[at]) + contract_last(grad_up[...], w_up[at])


def send_body(width, grad_gate, grad_up, w_gate, w_up, out):
    def step(i, carry):
        at = pl.ds(pl.multiple_of(i * width, width), width)
        out[:, at] = partial_sum(at, grad_gate, grad_up, w_gate, w_up).astype(BF16)
        return carry

    lax.fori_loop(0, 2, step, 0)


def keep_body(width, grad_gate, grad_up, w_gate, w_up, got, keep, send):
    def step(i, carry):
        here = pl.ds(pl.multiple_of(i * width, width), width)
        at = pl.ds(pl.multiple_of((2 + i) * width, width), width)
        total = partial_sum(at, grad_gate, grad_up, w_gate, w_up) + got[:, here].astype(F32)

        @pl.when(i == 0)
        def _():
            send[...] = total.astype(BF16)

        @pl.when(i == 1)
        def _():
            keep[...] = total

        return carry

    lax.fori_loop(0, 2, step, 0)


def plain(body, args, outs, micros):
    spec = pl.BlockSpec(memory_space=pltpu.VMEM)
    return pl.pallas_call(
        body,
        in_specs=[spec] * len(args),
        out_specs=[spec] * len(outs),
        out_shape=[jax.ShapeDtypeStruct(*out) for out in outs],
        compiler_params=pltpu.CompilerParams(vmem_limit_bytes=VMEM),
        cost_estimate=pl.CostEstimate(flops=int(micros * 1e9), bytes_accessed=0, transcendentals=0),
    )(*args)


def send_parts(grads, weights, width):
    outs = [((grads[0].shape[0], 2 * width), BF16)]
    return plain(functools.partial(send_body, width), (*grads, *weights), outs, 2.0)[0]


def keep_parts(grads, weights, got, width):
    tok = grads[0].shape[0]
    outs = [((tok, width), F32), ((tok, width), BF16)]
    return plain(functools.partial(keep_body, width), (*grads, *weights, got), outs, 2.0)


def staged(grad_out, gate_saved, up_saved, w_gate, w_up, w_down):
    n = 16
    width = grad_out.shape[1]
    me = lax.axis_index("wid")
    line, row, pair = me // 4, (me // 2) % 2, me % 2
    places = {
        "own": line,
        "near": line ^ 1,
        "mid": jnp.where(line < 2, 2, 1),
        "far": jnp.where(line < 2, 3, 0),
    }

    def blocks(*wanted):
        return jnp.stack(
            [4 * places[name] + 2 * (row ^ r) + (pair ^ p) for name, order in wanted for r, p in order]
        ).astype(jnp.int32)

    pairs = [(i, i ^ 1) for i in range(n)]
    rows = [(i, i ^ 2) for i in range(n)]
    outer = [(i, i ^ 4) for i in range(n)]
    inner = [(i, i + 4) for i in range(4, 8)] + [(i, i - 4) for i in range(8, 12)]
    outward = [(i, i - 4) for i in range(4, 8)] + [(i, i + 4) for i in range(8, 12)]
    inward = [(j, i) for i, j in outward]

    def move(x, perm):
        return lax.ppermute(x, "wid", perm)

    in_hbm = functools.partial(pltpu.with_memory_space_constraint, memory_space=pltpu.HBM)
    gate_saved, up_saved, w_gate, w_up, w_down = map(in_hbm, (gate_saved, up_saved, w_gate, w_up, w_down))
    weights = (w_gate, w_up)
    arriving = [(0, 0), (0, 1), (1, 0), (1, 1)]
    leaving = [(1, 1), (0, 1), (1, 0), (0, 0)]
    ahead = {}
    scale, ahead["own"] = factors(blocks(("own", leaving)), gate_saved, up_saved, weights, width)

    near = move(grad_out, outer)
    mid = move(grad_out, inner)
    own_row = move(grad_out, rows)
    own_pair = move(grad_out, pairs)

    far = move(near, inner)
    mid = mid + move(mid, outward)
    near_row = move(near, rows)
    near_pair = move(near, pairs)
    own_both = move(own_row, pairs)
    total, *ahead["near"] = hidden(
        blocks(("own", arriving), ("near", leaving)), [grad_out, own_pair, own_row, own_both], w_down, fetch=weights
    )

    far = far + move(far, outward)
    mid_row = move(mid, rows)
    mid_pair = move(mid, pairs)
    near_both = move(near_row, pairs)
    total, *ahead["mid"] = hidden(
        blocks(("near", arriving), ("mid", leaving)), [near, near_pair, near_row, near_both], w_down, total, fetch=weights
    )

    far_row = move(far, rows)
    far_pair = move(far, pairs)
    mid_both = move(mid_row, pairs)
    total, *ahead["far"] = hidden(
        blocks(("mid", arriving), ("far", arriving[:2] + leaving)),
        [mid, mid_pair, mid_row, mid_both, far, far_pair], w_down, total, fetch=weights,
    )

    far_both = move(far_row, pairs)
    grads = hidden(blocks(("far", arriving[2:])), [far_row, far_both], w_down, total, scale)

    kept = {}
    for name in ("far", "mid", "near", "own"):
        got = move(send_parts(grads, ahead[name], width), pairs)
        keep, across = keep_parts(grads, ahead[name], got, width)
        kept[name] = keep + move(across, rows).astype(F32)

    far = kept["far"] + move(kept["far"].astype(BF16), inward).astype(F32)
    near = kept["near"] + move(far.astype(BF16), inner).astype(F32)
    mid = kept["mid"] + move(kept["mid"].astype(BF16), inward).astype(F32)
    own = kept["own"] + move(mid.astype(BF16), inner).astype(F32)
    own = own + move(near.astype(BF16), outer).astype(F32)
    return own.astype(BF16)


def local(grad_out, gate_saved, up_saved, w_gate, w_up, w_down):
    grad_hidden = contract_last(lax.all_gather(grad_out, "wid", axis=1, tiled=True), w_down)
    gate = gate_saved.astype(F32)
    up = up_saved.astype(F32)
    sig = jax.nn.sigmoid(gate)
    grad_gate = (grad_hidden * up * sig * (1.0 + gate * (1.0 - sig))).astype(BF16)
    grad_up = (grad_hidden * gate * sig).astype(BF16)
    summed = lax.psum_scatter(
        contract_last(w_gate, grad_gate) + contract_last(w_up, grad_up),
        "wid",
        scatter_dimension=0,
        tiled=True,
    )
    return summed.astype(BF16).T


def solution(mesh):
    in_specs = (
        P("grp", "wid"),
        P("grp", "wid"),
        P("grp", "wid"),
        P(None, "wid"),
        P(None, "wid"),
        P("wid", None),
    )
    out_specs = P("grp", "wid")
    body = staged if mesh.shape["wid"] == 16 else local
    return jax.shard_map(body, mesh=mesh, in_specs=in_specs, out_specs=out_specs, check_vma=False)
```

time: 219 us -> 92 us (0.42)
  waiting for transfers between devices: 162 us -> 22.8 us
  matrix products: 41.1 us -> 0 us
  Pallas kernels: 0 us -> 37 us
  starting transfers between devices: 0.04 us -> 29.9 us
  between operations: 13.4 us -> 0.35 us
    reduce_scatter x1 -> x0, waiting for transfers between devices: 103 us -> none  [local(): lax.psum_scatter(contract_last(w_gate, grad_gate) + contract_last(w_up, g...]
    all_gather x1 -> x0, waiting for transfers between devices: 58.2 us -> none  [local(): lax.all_gather(grad_out, 'wid', axis=1, tiled=True)]
    dot_general x3 -> x0, matrix products: 41.1 us -> none  [contract_last(): lax.dot_general(left, right, (((1,), (1,)), ((), ())), preferred_element_...]
    pallas_call x0 -> x13, Pallas kernels: none -> 37 us  [the longest x5 24.8 us: call(): pl.pallas_call(body, in_specs=[pl.BlockSpec(memory_space=space) for space...]
    ppermute x0 -> x30, starting transfers between devices: none -> 29.9 us  [move(): return lax.ppermute(x, 'wid', perm)]
    ppermute x0 -> x30, waiting for transfers between devices: none -> 22.8 us  [move(): return lax.ppermute(x, 'wid', perm)]
  transfers between devices with their start and end apart: 2 -> 30, of which waited for: 2 -> 8; matrix products, arithmetic and copies ran while one was open for 0% -> 1% of each run, Pallas kernels for 0% -> 35%
where the time goes in v2:
time: 92 us; the launch traced here: 91.8 us
  Pallas kernels  37 us (40%)
  starting transfers between devices  29.9 us (32%)
  waiting for transfers between devices  22.8 us (25%)
  other arithmetic  1.58 us (2%)
    ppermute x30, starting transfers between devices, move(): return lax.ppermute(x, 'wid', perm)  29.9 us
    pallas_call x5, Pallas kernels, call(): pl.pallas_call(body, in_specs=[pl.BlockSpec(memory_space=space) for space...  24.8 us
    ppermute x30, waiting for transfers between devices, move(): return lax.ppermute(x, 'wid', perm)  22.8 us
    pallas_call x8, Pallas kernels, plain(): pl.pallas_call(body, in_specs=[spec] * len(args), out_specs=[spec] * len(...  12.1 us
  transfers between devices with their start and end apart: 30, of which 8 were waited for; matrix products, arithmetic and copies ran while one was open for 1% of the time, Pallas kernels for 35%

profile of v2, /device:TPU:0, one launch (start us, length us, event | category | flops | bytes accessed | tf_op | source)
XLA Modules:
  0.0 91.8 jit_solution(633740325028237318)
XLA Ops:
  0.0 3.0 %collective-permute-start = (bf16[256,512]{1,0:T(8,128)(2,1)}, bf16[256,512]{1,0:T(8,128)(2,1)S(1)}, u32[]{:S(2)}, u32[]{:S(2)}) collective-permute-start(bf16[256,512]{1,0:T(8,128)(2,1)} %refs_0_.1), channel_id=1, source_target_pairs={{0,4},{1,5},{2,6},{3,7},{4,0},{5,1},{6,2},{7,3},{8,12},{9,13},{10,... | collective-permute-start | bytes 786440 | tf_op jit(solution)/shard_map/ppermute | solution.py:261
  3.0 0.7 collective-permute-start.5
  3.7 1.6 %collective-permute-start.15 = (bf16[256,512]{1,0:T(8,128)(2,1)}, bf16[256,512]{1,0:T(8,128)(2,1)S(1)}, u32[]{:S(2)}, u32[]{:S(2)}) collective-permute-start(bf16[256,512]{1,0:T(8,128)(2,1)} %refs_0_.1), channel_id=1, source_target_pairs={{0,2},{1,3},{2,0},{3,1},{4,6},{5,7},{6,4},{7,5},{8,10},{9,11},{10,... | collective-permute-start | bytes 786440 | tf_op jit(solution)/shard_map/ppermute | solution.py:261
  5.3 0.0 collective-permute-start.14
  5.3 0.1 stack.88.blocks
  5.4 0.1 stack.93.blocks
  5.5 0.1 stack.98.blocks
  5.5 0.1 pad_add_fusion.1.blocks
  5.6 0.1 pad_add_fusion.blocks
  5.7 3.8 %collective-permute-done.refs_0_ = bf16[256,512]{1,0:T(8,128)(2,1)S(1)} collective-permute-done((bf16[256,512]{1,0:T(8,128)(2,1)}, bf16[256,512]{1,0:T(8,128)(2,1)S(1)}, u32[]{:S(2)}, u32[]{:S(2)}) %collective-permute-start) | collective-permute-done | bytes 262176 | tf_op jit(solution)/shard_map/ppermute | solution.py:261
  9.5 1.7 %collective-permute-start.12 = (bf16[256,512]{1,0:T(8,128)(2,1)S(1)}, bf16[256,512]{1,0:T(8,128)(2,1)S(1)}, u32[]{:S(2)}, u32[]{:S(2)}) collective-permute-start(bf16[256,512]{1,0:T(8,128)(2,1)S(1)} %collective-permute-done.refs_0_), channel_id=1, source_target_pairs={{0,2},{1,3},{2,0},{3,1},{4,6},{5,7},{6,4},{7,5},{8,10},{9,11},{10,... | collective-permute-start | bytes 786440 | tf_op jit(solution)/shard_map/ppermute | solution.py:261
  11.2 0.7 collective-permute-start.1
  11.9 1.3 %collective-permute-start.6 = (bf16[256,512]{1,0:T(8,128)(2,1)S(1)}, bf16[256,512]{1,0:T(8,128)(2,1)S(1)}, u32[]{:S(2)}, u32[]{:S(2)}) collective-permute-start(bf16[256,512]{1,0:T(8,128)(2,1)S(1)} %collective-permute-done.5), channel_id=1, source_target_pairs={{4,0},{5,1},{6,2},{7,3},{8,12},{9,13},{10,14},{11,15},{20,16},{21,... | collective-permute-start | bytes 786440 | tf_op jit(solution)/shard_map/ppermute | solution.py:261
  13.2 0.0 collective-permute-done.15.refs_2_
  13.2 0.1 collective-permute-start.16
  13.3 4.4 %shard_map.67 = (f32[256,1024]{1,0:T(8,128)S(1)}, f32[256,1024]{1,0:T(8,128)S(1)}, bf16[2048,1024]{1,0:T(8,128)(2,1)S(1)}, bf16[2048,1024]{1,0:T(8,128)(2,1)S(1)}) custom-call(s32[4]{0:T(128)S(1)} %pad_add_fusion.1.blocks, bf16[256,1024]{1,0:T(8,128)(2,1)} %gate.1, bf16[256,1024]{1,0:T(8,128)(2,1)} %up.1, bf16[8192,1024]{1,0:T(8,128)(2,1)} %w_gate.1, ...), custom_call_target="tpu_custom_call" | custom-call | flops 4000000000 | tf_op jit(solution)/shard_map/pallas_call | solution.py:22
  17.7 4.7 %collective-permute-done.6 = bf16[256,512]{1,0:T(8,128)(2,1)S(1)} collective-permute-done((bf16[256,512]{1,0:T(8,128)(2,1)S(1)}, bf16[256,512]{1,0:T(8,128)(2,1)S(1)}, u32[]{:S(2)}, u32[]{:S(2)}) %collective-permute-start.6) | collective-permute-done | bytes 262176 | tf_op jit(solution)/shard_map/ppermute | solution.py:261
  22.4 0.0 collective-permute-start.11
  22.4 0.1 add.169.refs_0_
  22.5 0.6 collective-permute-start.8
  23.1 0.2 collective-permute-start.7
  23.3 0.3 collective-permute-start.13
  23.6 1.3 %collective-permute-start.2 = (bf16[256,512]{1,0:T(8,128)(2,1)S(1)}, bf16[256,512]{1,0:T(8,128)(2,1)S(1)}, u32[]{:S(2)}, u32[]{:S(2)}) collective-permute-start(bf16[256,512]{1,0:T(8,128)(2,1)S(1)} %collective-permute-done.1), channel_id=1, source_target_pairs={{4,0},{5,1},{6,2},{7,3},{8,12},{9,13},{10,14},{11,15},{20,16},{21,... | collective-permute-start | bytes 786440 | tf_op jit(solution)/shard_map/ppermute | solution.py:261
  24.9 5.5 %shard_map.64 = (f32[256,1024]{1,0:T(8,128)S(1)}, bf16[2048,1024]{1,0:T(8,128)(2,1)S(1)}, bf16[2048,1024]{1,0:T(8,128)(2,1)S(1)}) custom-call(s32[8]{0:T(128)S(1)} %stack.98.blocks, bf16[256,512]{1,0:T(8,128)(2,1)S(1)} %copy-done, bf16[256,512]{1,0:T(8,128)(2,1)S(1)} %collective-permute-done.14.refs_1_, ...), custom_call_target="tpu_custom_call" | custom-call | flops 5000000000 | tf_op jit(solution)/shard_map/pallas_call | solution.py:22
  30.4 3.5 %collective-permute-done.2 = bf16[256,512]{1,0:T(8,128)(2,1)S(1)} collective-permute-done((bf16[256,512]{1,0:T(8,128)(2,1)S(1)}, bf16[256,512]{1,0:T(8,128)(2,1)S(1)}, u32[]{:S(2)}, u32[]{:S(2)}) %collective-permute-start.2) | collective-permute-done | bytes 262176 | tf_op jit(solution)/shard_map/ppermute | solution.py:261
  33.9 0.1 add.159.refs_4_
  34.0 0.1 collective-permute-start.10
  34.1 1.6 %collective-permute-start.3 = (bf16[256,512]{1,0:T(8,128)(2,1)S(1)}, bf16[256,512]{1,0:T(8,128)(2,1)S(1)}, u32[]{:S(2)}, u32[]{:S(2)}) collective-permute-start(bf16[256,512]{1,0:T(8,128)(2,1)S(1)} %add.159.refs_4_), channel_id=1, source_target_pairs={{0,2},{1,3},{2,0},{3,1},{4,6},{5,7},{6,4},{7,5},{8,10},{9,11},{10,... | collective-permute-start | bytes 786440 | tf_op jit(solution)/shard_map/ppermute | solution.py:261
  35.7 0.2 collective-permute-start.9
  35.9 5.5 %shard_map.65 = (f32[256,1024]{1,0:T(8,128)S(1)}, bf16[2048,1024]{1,0:T(8,128)(2,1)S(1)}, bf16[2048,1024]{1,0:T(8,128)(2,1)S(1)}) custom-call(s32[8]{0:T(128)S(1)} %stack.93.blocks, bf16[256,512]{1,0:T(8,128)(2,1)S(1)} %collective-permute-done.refs_0_, bf16[256,512]{1,0:T(8,128)(2,1)S(1)} %collective-permute-done.11.refs_1_, ...), custom_call_target="tpu_custom_call" | custom-call | flops 5000000000 | tf_op jit(solution)/shard_map/pallas_call | solution.py:22
  41.4 1.4 %collective-permute-done.3.refs_0_ = bf16[256,512]{1,0:T(8,128)(2,1)S(1)} collective-permute-done((bf16[256,512]{1,0:T(8,128)(2,1)S(1)}, bf16[256,512]{1,0:T(8,128)(2,1)S(1)}, u32[]{:S(2)}, u32[]{:S(2)}) %collective-permute-start.3) | collective-permute-done | bytes 262176 | tf_op jit(solution)/shard_map/ppermute | solution.py:261
  42.8 6.3 %shard_map.66 = (f32[256,1024]{1,0:T(8,128)S(1)}, bf16[2048,1024]{1,0:T(8,128)(2,1)S(1)}, bf16[2048,1024]{1,0:T(8,128)(2,1)S(1)}) custom-call(s32[10]{0:T(128)S(1)} %stack.88.blocks, bf16[256,512]{1,0:T(8,128)(2,1)S(1)} %add.169.refs_0_, bf16[256,512]{1,0:T(8,128)(2,1)S(1)} %collective-permute-done.7.refs_1_, ...), custom_call_target="tpu_custom_call" | custom-call | flops 5000000000 | tf_op jit(solution)/shard_map/pallas_call | solution.py:22
  49.1 3.1 %shard_map.68 = (bf16[256,1024]{1,0:T(8,128)(2,1)S(1)}, bf16[256,1024]{1,0:T(8,128)(2,1)S(1)}) custom-call(s32[2]{0:T(128)S(1)} %pad_add_fusion.blocks, bf16[256,512]{1,0:T(8,128)(2,1)S(1)} %collective-permute-done.3.refs_0_, bf16[256,512]{1,0:T(8,128)(2,1)S(1)} %collective-permute-done.4.refs_1_, bf16[1024,8192]{1,0:T(8,128)(2,1)} %refs_2_.1, ...), custom_call_target="tpu_custom_call" | custom-call | flops 3000000000 | tf_op jit(solution)/shard_map/pallas_call | solution.py:22
  52.2 1.5 %shard_map.75 = bf16[256,1024]{1,0:T(8,128)(2,1)S(1)} custom-call(bf16[256,1024]{1,0:T(8,128)(2,1)S(1)} %get-tuple-element.33.grad_gate, bf16[256,1024]{1,0:T(8,128)(2,1)S(1)} %get-tuple-element.34.grad_up, bf16[2048,1024]{1,0:T(8,128)(2,1)S(1)} %get-tuple-element.47.w_gate, bf16[2048,1024]{1,0:T(8,128)(2,1)S(1)} %get-tuple-element.48.w_up), custom_call_target="tpu_custom_call" | custom-call | flops 2000000000 | tf_op jit(solution)/shard_map/pallas_call | solution.py:215
  53.7 0.6 collective-permute-start.25
  54.3 1.5 %shard_map.71 = bf16[256,1024]{1,0:T(8,128)(2,1)S(1)} custom-call(bf16[256,1024]{1,0:T(8,128)(2,1)S(1)} %get-tuple-element.33.grad_gate, bf16[256,1024]{1,0:T(8,128)(2,1)S(1)} %get-tuple-element.34.grad_up, bf16[2048,1024]{1,0:T(8,128)(2,1)S(1)} %get-tuple-element.39.w_gate, bf16[2048,1024]{1,0:T(8,128)(2,1)S(1)} %get-tuple-element.40.w_up), custom_call_target="tpu_custom_call" | custom-call | flops 2000000000 | tf_op jit(solution)/shard_map/pallas_call | solution.py:215
  55.8 0.1 collective-permute-start.19
  55.9 1.5 %shard_map.73 = bf16[256,1024]{1,0:T(8,128)(2,1)S(1)} custom-call(bf16[256,1024]{1,0:T(8,128)(2,1)S(1)} %get-tuple-element.33.grad_gate, bf16[256,1024]{1,0:T(8,128)(2,1)S(1)} %get-tuple-element.34.grad_up, bf16[2048,1024]{1,0:T(8,128)(2,1)S(1)} %get-tuple-element.43.w_gate, bf16[2048,1024]{1,0:T(8,128)(2,1)S(1)} %get-tuple-element.44.w_up), custom_call_target="tpu_custom_call" | custom-call | flops 2000000000 | tf_op jit(solution)/shard_map/pallas_call | solution.py:215
  57.4 0.6 collective-permute-start.23
  57.9 1.5 %shard_map.76 = (f32[256,512]{1,0:T(8,128)S(1)}, bf16[256,512]{1,0:T(8,128)(2,1)S(1)}) custom-call(bf16[256,1024]{1,0:T(8,128)(2,1)S(1)} %get-tuple-element.33.grad_gate, bf16[256,1024]{1,0:T(8,128)(2,1)S(1)} %get-tuple-element.34.grad_up, bf16[2048,1024]{1,0:T(8,128)(2,1)S(1)} %get-tuple-element.47.w_gate, bf16[2048,1024]{1,0:T(8,128)(2,1)S(1)} %get-tuple-element.48.w_up, ...), custom_call_target="tpu_custom_call" | custom-call | flops 2000000000 | tf_op jit(solution)/shard_map/pallas_call | solution.py:215
  59.5 1.6 %collective-permute-start.26 = (bf16[256,512]{1,0:T(8,128)(2,1)S(1)}, bf16[256,512]{1,0:T(8,128)(2,1)S(1)}, u32[]{:S(2)}, u32[]{:S(2)}) collective-permute-start(bf16[256,512]{1,0:T(8,128)(2,1)S(1)} %get-tuple-element.50), channel_id=1, source_target_pairs={{0,2},{1,3},{2,0},{3,1},{4,6},{5,7},{6,4},{7,5},{8,10},{9,11},{10,... | collective-permute-start | bytes 786440 | tf_op jit(solution)/shard_map/ppermute | solution.py:261
  61.1 1.5 %shard_map.69 = bf16[256,1024]{1,0:T(8,128)(2,1)S(1)} custom-call(bf16[256,1024]{1,0:T(8,128)(2,1)S(1)} %get-tuple-element.33.grad_gate, bf16[256,1024]{1,0:T(8,128)(2,1)S(1)} %get-tuple-element.34.grad_up, bf16[2048,1024]{1,0:T(8,128)(2,1)S(1)} %get-tuple-element.35.w_gate, bf16[2048,1024]{1,0:T(8,128)(2,1)S(1)} %get-tuple-element.36.w_up), custom_call_target="tpu_custom_call" | custom-call | flops 2000000000 | tf_op jit(solution)/shard_map/pallas_call | solution.py:215
  62.6 0.1 collective-permute-start.17
  62.7 1.6 %shard_map.72 = (f32[256,512]{1,0:T(8,128)S(1)}, bf16[256,512]{1,0:T(8,128)(2,1)S(1)}) custom-call(bf16[256,1024]{1,0:T(8,128)(2,1)S(1)} %get-tuple-element.33.grad_gate, bf16[256,1024]{1,0:T(8,128)(2,1)S(1)} %get-tuple-element.34.grad_up, bf16[2048,1024]{1,0:T(8,128)(2,1)S(1)} %get-tuple-element.39.w_gate, bf16[2048,1024]{1,0:T(8,128)(2,1)S(1)} %get-tuple-element.40.w_up, ...), custom_call_target="tpu_custom_call" | custom-call | flops 2000000000 | tf_op jit(solution)/shard_map/pallas_call | solution.py:215
  64.2 0.6 collective-permute-start.20
  64.8 3.4 %collective-permute-done.26 = bf16[256,512]{1,0:T(8,128)(2,1)S(1)} collective-permute-done((bf16[256,512]{1,0:T(8,128)(2,1)S(1)}, bf16[256,512]{1,0:T(8,128)(2,1)S(1)}, u32[]{:S(2)}, u32[]{:S(2)}) %collective-permute-start.26) | collective-permute-done | bytes 262176 | tf_op jit(solution)/shard_map/ppermute | solution.py:261
  68.1 0.1 fusion.1
  68.2 1.4 %collective-permute-start.27 = (bf16[256,512]{1,0:T(8,128)(2,1)S(1)}, bf16[256,512]{1,0:T(8,128)(2,1)S(1)}, u32[]{:S(2)}, u32[]{:S(2)}) collective-permute-start(bf16[256,512]{1,0:T(8,128)(2,1)S(1)} %fusion.1), channel_id=1, source_target_pairs={{0,4},{1,5},{2,6},{3,7},{12,8},{13,9},{14,10},{15,11},{16,20},{17,... | collective-permute-start | bytes 786440 | tf_op jit(solution)/shard_map/ppermute | solution.py:261
  69.7 1.5 %shard_map.74 = (f32[256,512]{1,0:T(8,128)S(1)}, bf16[256,512]{1,0:T(8,128)(2,1)S(1)}) custom-call(bf16[256,1024]{1,0:T(8,128)(2,1)S(1)} %get-tuple-element.33.grad_gate, bf16[256,1024]{1,0:T(8,128)(2,1)S(1)} %get-tuple-element.34.grad_up, bf16[2048,1024]{1,0:T(8,128)(2,1)S(1)} %get-tuple-element.43.w_gate, bf16[2048,1024]{1,0:T(8,128)(2,1)S(1)} %get-tuple-element.44.w_up, ...), custom_call_target="tpu_custom_call" | custom-call | flops 2000000000 | tf_op jit(solution)/shard_map/pallas_call | solution.py:215
  71.2 2.2 %collective-permute-start.24 = (bf16[256,512]{1,0:T(8,128)(2,1)S(1)}, bf16[256,512]{1,0:T(8,128)(2,1)S(1)}, u32[]{:S(2)}, u32[]{:S(2)}) collective-permute-start(bf16[256,512]{1,0:T(8,128)(2,1)S(1)} %get-tuple-element.46), channel_id=1, source_target_pairs={{0,2},{1,3},{2,0},{3,1},{4,6},{5,7},{6,4},{7,5},{8,10},{9,11},{10,... | collective-permute-start | bytes 786440 | tf_op jit(solution)/shard_map/ppermute | solution.py:261
  73.4 0.3 collective-permute-done.20
  73.8 0.1 fusion
  73.8 1.4 %collective-permute-start.21 = (bf16[256,512]{1,0:T(8,128)(2,1)S(1)}, bf16[256,512]{1,0:T(8,128)(2,1)S(1)}, u32[]{:S(2)}, u32[]{:S(2)}) collective-permute-start(bf16[256,512]{1,0:T(8,128)(2,1)S(1)} %fusion), channel_id=1, source_target_pairs={{0,4},{1,5},{2,6},{3,7},{12,8},{13,9},{14,10},{15,11},{16,20},{17,... | collective-permute-start | bytes 786440 | tf_op jit(solution)/shard_map/ppermute | solution.py:261
  75.3 0.1 add_convert_fusion.2
  75.4 0.7 collective-permute-start.28
  76.1 1.5 %shard_map.70 = (f32[256,512]{1,0:T(8,128)S(1)}, bf16[256,512]{1,0:T(8,128)(2,1)S(1)}) custom-call(bf16[256,1024]{1,0:T(8,128)(2,1)S(1)} %get-tuple-element.33.grad_gate, bf16[256,1024]{1,0:T(8,128)(2,1)S(1)} %get-tuple-element.34.grad_up, bf16[2048,1024]{1,0:T(8,128)(2,1)S(1)} %get-tuple-element.35.w_gate, bf16[2048,1024]{1,0:T(8,128)(2,1)S(1)} %get-tuple-element.36.w_up, ...), custom_call_target="tpu_custom_call" | custom-call | flops 2000000000 | tf_op jit(solution)/shard_map/pallas_call | solution.py:215
  77.7 2.0 %collective-permute-start.18 = (bf16[256,512]{1,0:T(8,128)(2,1)S(1)}, bf16[256,512]{1,0:T(8,128)(2,1)S(1)}, u32[]{:S(2)}, u32[]{:S(2)}) collective-permute-start(bf16[256,512]{1,0:T(8,128)(2,1)S(1)} %get-tuple-element.38), channel_id=1, source_target_pairs={{0,2},{1,3},{2,0},{3,1},{4,6},{5,7},{6,4},{7,5},{8,10},{9,11},{10,... | collective-permute-start | bytes 786440 | tf_op jit(solution)/shard_map/ppermute | solution.py:261
  79.7 0.8 collective-permute-done.21
  80.5 0.1 add_convert_fusion.3
  80.6 0.7 collective-permute-start.22
  81.3 0.1 add_convert_fusion.1
  81.4 4.8 %collective-permute-start.29 = (bf16[256,512]{1,0:T(8,128)(2,1)S(1)}, bf16[256,512]{1,0:T(8,128)(2,1)S(1)}, u32[]{:S(2)}, u32[]{:S(2)}) collective-permute-start(bf16[256,512]{1,0:T(8,128)(2,1)S(1)} %add_convert_fusion.1), channel_id=1, source_target_pairs={{0,4},{1,5},{2,6},{3,7},{4,0},{5,1},{6,2},{7,3},{8,12},{9,13},{10,... | collective-permute-start | bytes 786440 | tf_op jit(solution)/shard_map/ppermute | solution.py:261
  86.2 4.7 %collective-permute-done.29 = bf16[256,512]{1,0:T(8,128)(2,1)S(1)} collective-permute-done((bf16[256,512]{1,0:T(8,128)(2,1)S(1)}, bf16[256,512]{1,0:T(8,128)(2,1)S(1)}, u32[]{:S(2)}, u32[]{:S(2)}) %collective-permute-start.29) | collective-permute-done | bytes 262176 | tf_op jit(solution)/shard_map/ppermute | solution.py:261
  90.9 0.8 add_convert_fusion
  (24 shorter events, 0.1 us)
Async XLA Ops:
  0.0 9.5 %collective-permute-start = (bf16[256,512]{1,0:T(8,128)(2,1)}, bf16[256,512]{1,0:T(8,128)(2,1)S(1)}, u32[]{:S(2)}, u32[]{:S(2)}) collective-permute-start(bf16[256,512]{1,0:T(8,128)(2,1)} %refs_0_.1), channel_id=1, source_target_pairs={{0,4},{1,5},{2,6},{3,7},{4,0},{5,1},{6,2},{7,3},{8,12},{9,13},{10,... | collective-permute-start | bytes 786440 | tf_op jit(solution)/shard_map/ppermute | solution.py:261
  3.0 8.9 %collective-permute-start.5 = (bf16[256,512]{1,0:T(8,128)(2,1)}, bf16[256,512]{1,0:T(8,128)(2,1)S(1)}, u32[]{:S(2)}, u32[]{:S(2)}) collective-permute-start(bf16[256,512]{1,0:T(8,128)(2,1)} %refs_0_.1), channel_id=1, source_target_pairs={{4,8},{5,9},{6,10},{7,11},{8,4},{9,5},{10,6},{11,7},{20,24},{21,25... | collective-permute-start | bytes 786440 | tf_op jit(solution)/shard_map/ppermute | solution.py:261
  3.7 9.5 %collective-permute-start.15 = (bf16[256,512]{1,0:T(8,128)(2,1)}, bf16[256,512]{1,0:T(8,128)(2,1)S(1)}, u32[]{:S(2)}, u32[]{:S(2)}) collective-permute-start(bf16[256,512]{1,0:T(8,128)(2,1)} %refs_0_.1), channel_id=1, source_target_pairs={{0,2},{1,3},{2,0},{3,1},{4,6},{5,7},{6,4},{7,5},{8,10},{9,11},{10,... | collective-permute-start | bytes 786440 | tf_op jit(solution)/shard_map/ppermute | solution.py:261
  5.3 17.2 %collective-permute-start.14 = (bf16[256,512]{1,0:T(8,128)(2,1)}, bf16[256,512]{1,0:T(8,128)(2,1)S(1)}, u32[]{:S(2)}, u32[]{:S(2)}) collective-permute-start(bf16[256,512]{1,0:T(8,128)(2,1)} %refs_0_.1), channel_id=1, source_target_pairs={{0,1},{1,0},{2,3},{3,2},{4,5},{5,4},{6,7},{7,6},{8,9},{9,8},{10,11... | collective-permute-start | bytes 786440 | tf_op jit(solution)/shard_map/ppermute | solution.py:261
  5.7 19.2 %copy-start = (bf16[256,512]{1,0:T(8,128)(2,1)S(1)}, bf16[256,512]{1,0:T(8,128)(2,1)}, u32[]{:S(2)}) copy-start(bf16[256,512]{1,0:T(8,128)(2,1)} %refs_0_.1) | copy-start | bytes 786436
  9.5 13.6 %collective-permute-start.12 = (bf16[256,512]{1,0:T(8,128)(2,1)S(1)}, bf16[256,512]{1,0:T(8,128)(2,1)S(1)}, u32[]{:S(2)}, u32[]{:S(2)}) collective-permute-start(bf16[256,512]{1,0:T(8,128)(2,1)S(1)} %collective-permute-done.refs_0_), channel_id=1, source_target_pairs={{0,2},{1,3},{2,0},{3,1},{4,6},{5,7},{6,4},{7,5},{8,10},{9,11},{10,... | collective-permute-start | bytes 786440 | tf_op jit(solution)/shard_map/ppermute | solution.py:261
  11.2 12.1 %collective-permute-start.1 = (bf16[256,512]{1,0:T(8,128)(2,1)S(1)}, bf16[256,512]{1,0:T(8,128)(2,1)S(1)}, u32[]{:S(2)}, u32[]{:S(2)}) collective-permute-start(bf16[256,512]{1,0:T(8,128)(2,1)S(1)} %collective-permute-done.refs_0_), channel_id=1, source_target_pairs={{4,8},{5,9},{6,10},{7,11},{8,4},{9,5},{10,6},{11,7},{20,24},{21,25... | collective-permute-start | bytes 786440 | tf_op jit(solution)/shard_map/ppermute | solution.py:261
  11.9 10.5 %collective-permute-start.6 = (bf16[256,512]{1,0:T(8,128)(2,1)S(1)}, bf16[256,512]{1,0:T(8,128)(2,1)S(1)}, u32[]{:S(2)}, u32[]{:S(2)}) collective-permute-start(bf16[256,512]{1,0:T(8,128)(2,1)S(1)} %collective-permute-done.5), channel_id=1, source_target_pairs={{4,0},{5,1},{6,2},{7,3},{8,12},{9,13},{10,14},{11,15},{20,16},{21,... | collective-permute-start | bytes 786440 | tf_op jit(solution)/shard_map/ppermute | solution.py:261
  13.2 10.4 %collective-permute-start.16 = (bf16[256,512]{1,0:T(8,128)(2,1)S(1)}, bf16[256,512]{1,0:T(8,128)(2,1)S(1)}, u32[]{:S(2)}, u32[]{:S(2)}) collective-permute-start(bf16[256,512]{1,0:T(8,128)(2,1)S(1)} %collective-permute-done.15.refs_2_), channel_id=1, source_target_pairs={{0,1},{1,0},{2,3},{3,2},{4,5},{5,4},{6,7},{7,6},{8,9},{9,8},{10,11... | collective-permute-start | bytes 786440 | tf_op jit(solution)/shard_map/ppermute | solution.py:261
  22.4 11.7 %collective-permute-start.11 = (bf16[256,512]{1,0:T(8,128)(2,1)S(1)}, bf16[256,512]{1,0:T(8,128)(2,1)S(1)}, u32[]{:S(2)}, u32[]{:S(2)}) collective-permute-start(bf16[256,512]{1,0:T(8,128)(2,1)S(1)} %collective-permute-done.refs_0_), channel_id=1, source_target_pairs={{0,1},{1,0},{2,3},{3,2},{4,5},{5,4},{6,7},{7,6},{8,9},{9,8},{10,11... | collective-permute-start | bytes 786440 | tf_op jit(solution)/shard_map/ppermute | solution.py:261
  22.5 13.2 %collective-permute-start.8 = (bf16[256,512]{1,0:T(8,128)(2,1)S(1)}, bf16[256,512]{1,0:T(8,128)(2,1)S(1)}, u32[]{:S(2)}, u32[]{:S(2)}) collective-permute-start(bf16[256,512]{1,0:T(8,128)(2,1)S(1)} %add.169.refs_0_), channel_id=1, source_target_pairs={{0,2},{1,3},{2,0},{3,1},{4,6},{5,7},{6,4},{7,5},{8,10},{9,11},{10,... | collective-permute-start | bytes 786440 | tf_op jit(solution)/shard_map/ppermute | solution.py:261
  23.1 19.7 %collective-permute-start.7 = (bf16[256,512]{1,0:T(8,128)(2,1)S(1)}, bf16[256,512]{1,0:T(8,128)(2,1)S(1)}, u32[]{:S(2)}, u32[]{:S(2)}) collective-permute-start(bf16[256,512]{1,0:T(8,128)(2,1)S(1)} %add.169.refs_0_), channel_id=1, source_target_pairs={{0,1},{1,0},{2,3},{3,2},{4,5},{5,4},{6,7},{7,6},{8,9},{9,8},{10,11... | collective-permute-start | bytes 786440 | tf_op jit(solution)/shard_map/ppermute | solution.py:261
  23.3 12.5 %collective-permute-start.13 = (bf16[256,512]{1,0:T(8,128)(2,1)S(1)}, bf16[256,512]{1,0:T(8,128)(2,1)S(1)}, u32[]{:S(2)}, u32[]{:S(2)}) collective-permute-start(bf16[256,512]{1,0:T(8,128)(2,1)S(1)} %collective-permute-done.12.refs_2_), channel_id=1, source_target_pairs={{0,1},{1,0},{2,3},{3,2},{4,5},{5,4},{6,7},{7,6},{8,9},{9,8},{10,11... | collective-permute-start | bytes 786440 | tf_op jit(solution)/shard_map/ppermute | solution.py:261
  23.6 10.3 %collective-permute-start.2 = (bf16[256,512]{1,0:T(8,128)(2,1)S(1)}, bf16[256,512]{1,0:T(8,128)(2,1)S(1)}, u32[]{:S(2)}, u32[]{:S(2)}) collective-permute-start(bf16[256,512]{1,0:T(8,128)(2,1)S(1)} %collective-permute-done.1), channel_id=1, source_target_pairs={{4,0},{5,1},{6,2},{7,3},{8,12},{9,13},{10,14},{11,15},{20,16},{21,... | collective-permute-start | bytes 786440 | tf_op jit(solution)/shard_map/ppermute | solution.py:261
  34.0 8.8 %collective-permute-start.10 = (bf16[256,512]{1,0:T(8,128)(2,1)S(1)}, bf16[256,512]{1,0:T(8,128)(2,1)S(1)}, u32[]{:S(2)}, u32[]{:S(2)}) collective-permute-start(bf16[256,512]{1,0:T(8,128)(2,1)S(1)} %add.159.refs_4_), channel_id=1, source_target_pairs={{0,1},{1,0},{2,3},{3,2},{4,5},{5,4},{6,7},{7,6},{8,9},{9,8},{10,11... | collective-permute-start | bytes 786440 | tf_op jit(solution)/shard_map/ppermute | solution.py:261
  34.1 8.7 %collective-permute-start.3 = (bf16[256,512]{1,0:T(8,128)(2,1)S(1)}, bf16[256,512]{1,0:T(8,128)(2,1)S(1)}, u32[]{:S(2)}, u32[]{:S(2)}) collective-permute-start(bf16[256,512]{1,0:T(8,128)(2,1)S(1)} %add.159.refs_4_), channel_id=1, source_target_pairs={{0,2},{1,3},{2,0},{3,1},{4,6},{5,7},{6,4},{7,5},{8,10},{9,11},{10,... | collective-permute-start | bytes 786440 | tf_op jit(solution)/shard_map/ppermute | solution.py:261
  35.7 7.1 %collective-permute-start.9 = (bf16[256,512]{1,0:T(8,128)(2,1)S(1)}, bf16[256,512]{1,0:T(8,128)(2,1)S(1)}, u32[]{:S(2)}, u32[]{:S(2)}) collective-permute-start(bf16[256,512]{1,0:T(8,128)(2,1)S(1)} %collective-permute-done.8.refs_2_), channel_id=1, source_target_pairs={{0,1},{1,0},{2,3},{3,2},{4,5},{5,4},{6,7},{7,6},{8,9},{9,8},{10,11... | collective-permute-start | bytes 786440 | tf_op jit(solution)/shard_map/ppermute | solution.py:261
  42.8 6.3 %collective-permute-start.4 = (bf16[256,512]{1,0:T(8,128)(2,1)S(1)}, bf16[256,512]{1,0:T(8,128)(2,1)S(1)}, u32[]{:S(2)}, u32[]{:S(2)}) collective-permute-start(bf16[256,512]{1,0:T(8,128)(2,1)S(1)} %collective-permute-done.3.refs_0_), channel_id=1, source_target_pairs={{0,1},{1,0},{2,3},{3,2},{4,5},{5,4},{6,7},{7,6},{8,9},{9,8},{10,11... | collective-permute-start | bytes 786440 | tf_op jit(solution)/shard_map/ppermute | solution.py:261
  53.7 4.2 %collective-permute-start.25 = (bf16[256,1024]{1,0:T(8,128)(2,1)S(1)}, bf16[256,1024]{1,0:T(8,128)(2,1)S(1)}, u32[]{:S(2)}, u32[]{:S(2)}) collective-permute-start(bf16[256,1024]{1,0:T(8,128)(2,1)S(1)} %shard_map.75), channel_id=1, source_target_pairs={{0,1},{1,0},{2,3},{3,2},{4,5},{5,4},{6,7},{7,6},{8,9},{9,8},{10,11... | collective-permute-start | bytes 1572872 | tf_op jit(solution)/shard_map/ppermute | solution.py:261
  55.8 6.8 %collective-permute-start.19 = (bf16[256,1024]{1,0:T(8,128)(2,1)S(1)}, bf16[256,1024]{1,0:T(8,128)(2,1)S(1)}, u32[]{:S(2)}, u32[]{:S(2)}) collective-permute-start(bf16[256,1024]{1,0:T(8,128)(2,1)S(1)} %shard_map.71), channel_id=1, source_target_pairs={{0,1},{1,0},{2,3},{3,2},{4,5},{5,4},{6,7},{7,6},{8,9},{9,8},{10,11... | collective-permute-start | bytes 1572872 | tf_op jit(solution)/shard_map/ppermute | solution.py:261
  57.4 12.3 %collective-permute-start.23 = (bf16[256,1024]{1,0:T(8,128)(2,1)S(1)}, bf16[256,1024]{1,0:T(8,128)(2,1)S(1)}, u32[]{:S(2)}, u32[]{:S(2)}) collective-permute-start(bf16[256,1024]{1,0:T(8,128)(2,1)S(1)} %shard_map.73), channel_id=1, source_target_pairs={{0,1},{1,0},{2,3},{3,2},{4,5},{5,4},{6,7},{7,6},{8,9},{9,8},{10,11... | collective-permute-start | bytes 1572872 | tf_op jit(solution)/shard_map/ppermute | solution.py:261
  59.5 8.7 %collective-permute-start.26 = (bf16[256,512]{1,0:T(8,128)(2,1)S(1)}, bf16[256,512]{1,0:T(8,128)(2,1)S(1)}, u32[]{:S(2)}, u32[]{:S(2)}) collective-permute-start(bf16[256,512]{1,0:T(8,128)(2,1)S(1)} %get-tuple-element.50), channel_id=1, source_target_pairs={{0,2},{1,3},{2,0},{3,1},{4,6},{5,7},{6,4},{7,5},{8,10},{9,11},{10,... | collective-permute-start | bytes 786440 | tf_op jit(solution)/shard_map/ppermute | solution.py:261
  62.6 13.5 %collective-permute-start.17 = (bf16[256,1024]{1,0:T(8,128)(2,1)S(1)}, bf16[256,1024]{1,0:T(8,128)(2,1)S(1)}, u32[]{:S(2)}, u32[]{:S(2)}) collective-permute-start(bf16[256,1024]{1,0:T(8,128)(2,1)S(1)} %shard_map.69), channel_id=1, source_target_pairs={{0,1},{1,0},{2,3},{3,2},{4,5},{5,4},{6,7},{7,6},{8,9},{9,8},{10,11... | collective-permute-start | bytes 1572872 | tf_op jit(solution)/shard_map/ppermute | solution.py:261
  64.2 9.6 %collective-permute-start.20 = (bf16[256,512]{1,0:T(8,128)(2,1)S(1)}, bf16[256,512]{1,0:T(8,128)(2,1)S(1)}, u32[]{:S(2)}, u32[]{:S(2)}) collective-permute-start(bf16[256,512]{1,0:T(8,128)(2,1)S(1)} %get-tuple-element.42), channel_id=1, source_target_pairs={{0,2},{1,3},{2,0},{3,1},{4,6},{5,7},{6,4},{7,5},{8,10},{9,11},{10,... | collective-permute-start | bytes 786440 | tf_op jit(solution)/shard_map/ppermute | solution.py:261
  68.2 7.1 %collective-permute-start.27 = (bf16[256,512]{1,0:T(8,128)(2,1)S(1)}, bf16[256,512]{1,0:T(8,128)(2,1)S(1)}, u32[]{:S(2)}, u32[]{:S(2)}) collective-permute-start(bf16[256,512]{1,0:T(8,128)(2,1)S(1)} %fusion.1), channel_id=1, source_target_pairs={{0,4},{1,5},{2,6},{3,7},{12,8},{13,9},{14,10},{15,11},{16,20},{17,... | collective-permute-start | bytes 786440 | tf_op jit(solution)/shard_map/ppermute | solution.py:261
  71.2 10.1 %collective-permute-start.24 = (bf16[256,512]{1,0:T(8,128)(2,1)S(1)}, bf16[256,512]{1,0:T(8,128)(2,1)S(1)}, u32[]{:S(2)}, u32[]{:S(2)}) collective-permute-start(bf16[256,512]{1,0:T(8,128)(2,1)S(1)} %get-tuple-element.46), channel_id=1, source_target_pairs={{0,2},{1,3},{2,0},{3,1},{4,6},{5,7},{6,4},{7,5},{8,10},{9,11},{10,... | collective-permute-start | bytes 786440 | tf_op jit(solution)/shard_map/ppermute | solution.py:261
  73.8 6.7 %collective-permute-start.21 = (bf16[256,512]{1,0:T(8,128)(2,1)S(1)}, bf16[256,512]{1,0:T(8,128)(2,1)S(1)}, u32[]{:S(2)}, u32[]{:S(2)}) collective-permute-start(bf16[256,512]{1,0:T(8,128)(2,1)S(1)} %fusion), channel_id=1, source_target_pairs={{0,4},{1,5},{2,6},{3,7},{12,8},{13,9},{14,10},{15,11},{16,20},{17,... | collective-permute-start | bytes 786440 | tf_op jit(solution)/shard_map/ppermute | solution.py:261
  75.4 5.9 %collective-permute-start.28 = (bf16[256,512]{1,0:T(8,128)(2,1)S(1)}, bf16[256,512]{1,0:T(8,128)(2,1)S(1)}, u32[]{:S(2)}, u32[]{:S(2)}) collective-permute-start(bf16[256,512]{1,0:T(8,128)(2,1)S(1)} %add_convert_fusion.2), channel_id=1, source_target_pairs={{4,8},{5,9},{6,10},{7,11},{8,4},{9,5},{10,6},{11,7},{20,24},{21,25... | collective-permute-start | bytes 786440 | tf_op jit(solution)/shard_map/ppermute | solution.py:261
  77.7 8.6 %collective-permute-start.18 = (bf16[256,512]{1,0:T(8,128)(2,1)S(1)}, bf16[256,512]{1,0:T(8,128)(2,1)S(1)}, u32[]{:S(2)}, u32[]{:S(2)}) collective-permute-start(bf16[256,512]{1,0:T(8,128)(2,1)S(1)} %get-tuple-element.38), channel_id=1, source_target_pairs={{0,2},{1,3},{2,0},{3,1},{4,6},{5,7},{6,4},{7,5},{8,10},{9,11},{10,... | collective-permute-start | bytes 786440 | tf_op jit(solution)/shard_map/ppermute | solution.py:261
  80.6 5.6 %collective-permute-start.22 = (bf16[256,512]{1,0:T(8,128)(2,1)S(1)}, bf16[256,512]{1,0:T(8,128)(2,1)S(1)}, u32[]{:S(2)}, u32[]{:S(2)}) collective-permute-start(bf16[256,512]{1,0:T(8,128)(2,1)S(1)} %add_convert_fusion.3), channel_id=1, source_target_pairs={{4,8},{5,9},{6,10},{7,11},{8,4},{9,5},{10,6},{11,7},{20,24},{21,25... | collective-permute-start | bytes 786440 | tf_op jit(solution)/shard_map/ppermute | solution.py:261
  81.4 9.5 %collective-permute-start.29 = (bf16[256,512]{1,0:T(8,128)(2,1)S(1)}, bf16[256,512]{1,0:T(8,128)(2,1)S(1)}, u32[]{:S(2)}, u32[]{:S(2)}) collective-permute-start(bf16[256,512]{1,0:T(8,128)(2,1)S(1)} %add_convert_fusion.1), channel_id=1, source_target_pairs={{0,4},{1,5},{2,6},{3,7},{4,0},{5,1},{6,2},{7,3},{8,12},{9,13},{10,... | collective-permute-start | bytes 786440 | tf_op jit(solution)/shard_map/ppermute | solution.py:261

commit v3 on v0

v3 whole, which is shorter than its diff:
```python
import functools

import jax
import jax.numpy as jnp
from jax import lax
from jax.experimental import pallas as pl
from jax.experimental.pallas import tpu as pltpu
from jax.sharding import PartitionSpec as P

BF16, F32 = jnp.bfloat16, jnp.float32
TILE = 256
VMEM = 10 * 2**20
COST = 2e8


def contract_last(left, right):
    return lax.dot_general(
        left, right, (((1,), (1,)), ((), ())), preferred_element_type=F32
    )


OWN, NEAR, MID, FAR = range(4)


def shard(place, row, pair):
    return lax.axis_index("wid") ^ (4 * place + 2 * row + pair)


def call(body, ins, outs, args, scratch, micros):
    return pl.pallas_call(
        body,
        in_specs=[pl.BlockSpec(memory_space=space) for space in ins],
        out_specs=[pl.BlockSpec(memory_space=pltpu.VMEM) for _ in outs],
        out_shape=outs,
        scratch_shapes=scratch,
        compiler_params=pltpu.CompilerParams(vmem_limit_bytes=VMEM),
        cost_estimate=pl.CostEstimate(flops=int(micros * COST), bytes_accessed=0, transcendentals=0),
    )(*args)


def factors_body(gate, up, to_gate_ref, to_up_ref, gate_ref, up_ref, sem):
    copies = [
        pltpu.make_async_copy(source, to, sem.at[k])
        for k, (source, to) in enumerate([(gate, gate_ref), (up, up_ref)])
    ]
    for copy in copies:
        copy.start()
    for copy in copies:
        copy.wait()

    def step(i, carry):
        at = pl.ds(pl.multiple_of(i * 32, 32), 32)
        gate = gate_ref[at].astype(F32)
        up = up_ref[at].astype(F32)
        sig = jax.nn.sigmoid(gate)
        to_gate_ref[at] = up * sig * (1.0 + gate * (1.0 - sig))
        to_up_ref[at] = gate * sig
        return carry

    lax.fori_loop(0, gate_ref.shape[0] // 32, step, 0)


def factors(gate, up):
    tok, ff = gate.shape
    outs = [jax.ShapeDtypeStruct((tok, ff), F32)] * 2
    scratch = [pltpu.VMEM((tok, ff), BF16)] * 2 + [pltpu.SemaphoreType.DMA((2,))]
    return call(factors_body, [pl.ANY] * 2, outs, (gate, up), scratch, 1.0)


def hidden_body(shards, first, last, soon, *refs):
    refs, parts = list(refs), len(shards)
    blocks = [shard(*which) for which in shards]
    pieces, w_down, rest = refs[:parts], refs[parts], refs[parts + 1 :]
    piece_sem, weight_sem = rest.pop(), rest.pop()
    held, weights = rest.pop(), rest.pop()
    width = pieces[0].shape[1]
    before = None if first else rest.pop(0)
    if soon:
        del rest[2 * last : 2 * last + soon]
    count = w_down.shape[0] // TILE

    def arrival(j):
        return pltpu.make_async_copy(pieces[j], held.at[:, pl.ds(j * width, width)], piece_sem.at[j])

    def weight(i, j):
        at = pl.ds(pl.multiple_of(i * TILE, TILE), TILE)
        source = pl.ds(pl.multiple_of(blocks[j] * width, width), width)
        return pltpu.make_async_copy(
            w_down.at[at, source], weights.at[at, pl.ds(j * width, width)], weight_sem.at[i, j]
        )

    def start(i, carry):
        for j in range(parts):
            weight(i, j).start()
        return carry

    for j in range(parts):
        arrival(j).start()
    lax.fori_loop(0, count, start, 0)
    for j in range(parts):
        arrival(j).wait()

    def step(i, carry):
        for j in range(parts):
            weight(i, j).wait()
        at = pl.ds(pl.multiple_of(i * TILE, TILE), TILE)
        total = contract_last(held[...], weights[at])
        if not first:
            total = total + before[:, at]
        if last:
            to_gate, to_up, grad_gate, grad_up = rest
            grad_gate[:, at] = (total * to_gate[:, at]).astype(BF16)
            grad_up[:, at] = (total * to_up[:, at]).astype(BF16)
        else:
            rest[0][:, at] = total
        return carry

    lax.fori_loop(0, count, step, 0)


def hidden(pieces, w_down, total=None, scale=None, soon=()):
    shards, pieces = zip(*pieces)
    tok, width = pieces[0].shape
    ff = w_down.shape[0]
    parts = len(pieces)
    ins, args = [pl.ANY] * (parts + 1), (*pieces, w_down)
    if total is not None:
        ins, args = ins + [pltpu.VMEM], (*args, total)
    if scale is not None:
        ins, args = ins + [pltpu.VMEM] * 2, (*args, *scale)
        outs = [jax.ShapeDtypeStruct((tok, ff), BF16)] * 2
    else:
        outs = [jax.ShapeDtypeStruct((tok, ff), F32)]
    ins, args = ins + [pltpu.VMEM] * len(soon), (*args, *soon)
    scratch = [
        pltpu.VMEM((ff, parts * width), BF16),
        pltpu.VMEM((tok, parts * width), BF16),
        pltpu.SemaphoreType.DMA((ff // TILE, parts)),
        pltpu.SemaphoreType.DMA((parts,)),
    ]
    body = functools.partial(hidden_body, shards, total is None, scale is not None, len(soon))
    return call(body, ins, outs, args, scratch, 3.0)


def partial_sum(block, width, grad_gate, grad_up, w_gate, w_up):
    at = pl.ds(pl.multiple_of(block * width, width), width)
    return contract_last(grad_gate[...], w_gate[at]) + contract_last(grad_up[...], w_up[at])


def each_row(width, body):
    def step(i, carry):
        body(i, pl.ds(pl.multiple_of(i * width, width), width))
        return carry

    lax.fori_loop(0, 2, step, 0)


def sums_body(kept, sent, width, grad_gate, grad_up, w_gate, w_up, *refs):
    given = (grad_gate, grad_up, w_gate, w_up)
    refs = list(refs)
    if kept is not None:
        got, keep, cross = refs.pop(0), refs.pop(0), refs.pop(0)

        def keep_row(i, at):
            total = partial_sum(shard(kept, 1 - i, 0), width, *given) + got[:, at].astype(F32)

            @pl.when(i == 0)
            def _():
                cross[...] = total.astype(BF16)

            @pl.when(i == 1)
            def _():
                keep[...] = total

        each_row(width, keep_row)
    if sent is not None:
        out = refs.pop(0)

        def send_row(i, at):
            out[:, at] = partial_sum(shard(sent, 1 - i, 1), width, *given).astype(BF16)

        each_row(width, send_row)


def sums(grads, weights, width, kept=None, got=None, sent=None):
    tok = grads[0].shape[0]
    args, outs = (*grads, *weights), []
    if kept is not None:
        args = (*args, got)
        outs += [jax.ShapeDtypeStruct((tok, width), F32), jax.ShapeDtypeStruct((tok, width), BF16)]
    if sent is not None:
        outs += [jax.ShapeDtypeStruct((tok, 2 * width), BF16)]
    body = functools.partial(sums_body, kept, sent, width)
    return call(body, [pltpu.VMEM] * len(args), outs, args, [], 1.5 * len(outs) / 2)


def after(x, *earlier):
    return lax.optimization_barrier((x, *earlier))[0]


def staged(grad_out, gate_saved, up_saved, w_gate, w_up, w_down):
    n = 16
    width = grad_out.shape[1]

    def move(x, bits):
        return lax.ppermute(x, "wid", [(i, i ^ bits) for i in range(n)])

    pair, row, near_, mid_ = 1, 2, 4, 8
    half = grad_out.shape[0] // 2
    in_hbm = functools.partial(pltpu.with_memory_space_constraint, memory_space=pltpu.HBM)
    gate_saved, up_saved, w_down = map(in_hbm, (gate_saved, up_saved, w_down))
    weights = [pltpu.with_memory_space_constraint(w, pltpu.VMEM) for w in (w_gate, w_up)]

    scale = factors(gate_saved, up_saved)
    own_row = move(grad_out, row)
    near = move(grad_out, near_)
    mid_a = move(grad_out[:half], mid_)
    own_pair = move(grad_out, pair)

    near = after(near, scale[0])
    near_row = move(near, row)
    mid_b = move(after(grad_out[half:], near), mid_)
    far_a = move(mid_a, near_)
    near_pair = move(near, pair)
    own_both = move(own_row, pair)
    (total,) = hidden(
        [((OWN, 0, 0), in_hbm(grad_out)), ((OWN, 0, 1), own_pair), ((OWN, 1, 0), own_row), ((NEAR, 0, 0), near)], w_down
    )

    mid_b, near_row = after(mid_b, total, near_row), after(near_row, mid_b)
    mid = jnp.concatenate([mid_a, mid_b])
    mid_row = move(mid, row)
    far_b = move(mid_b, near_)
    mid_pair = move(mid, pair)
    near_both = move(near_row, pair)
    (total,) = hidden(
        [((OWN, 1, 1), own_both), ((NEAR, 0, 1), near_pair), ((NEAR, 1, 0), near_row), ((MID, 0, 0), mid)], w_down, total
    )

    far_b = after(far_b, total)
    far = jnp.concatenate([far_a, far_b])
    far_row = move(far, row)
    far_pair = move(far, pair)
    mid_both = move(mid_row, pair)
    (total,) = hidden(
        [
            ((NEAR, 1, 1), near_both),
            ((MID, 0, 1), mid_pair),
            ((MID, 1, 0), mid_row),
            ((FAR, 0, 0), far),
            ((MID, 1, 1), mid_both),
            ((FAR, 0, 1), far_pair),
        ],
        w_down,
        total,
        soon=weights,
    )

    far_row = after(far_row, total)
    far_both = move(far_row, pair)
    grads = hidden([((FAR, 1, 0), far_row), ((FAR, 1, 1), far_both)], w_down, total, scale)

    step = functools.partial(sums, grads, weights, width)
    (sent_far,) = step(sent=FAR)
    (sent_mid,) = step(sent=MID)
    far, cross_far = step(kept=FAR, got=move(sent_far, pair))
    mid, cross_mid, sent_near = step(kept=MID, got=move(sent_mid, pair), sent=NEAR)
    far = far + move(cross_far, row).astype(F32)

    near, cross_near, sent_own = step(kept=NEAR, got=move(sent_near, pair), sent=OWN)
    mid = mid + after(move(cross_mid, row), cross_near).astype(F32) + move(far.astype(BF16), near_).astype(F32)

    own, cross_own = step(kept=OWN, got=move(sent_own, pair))
    mid = mid.astype(BF16)
    mid_a, near_row = move(mid[:half], mid_), move(cross_near, row)
    mid_a, near_row = after(mid_a, near_row, cross_own), after(near_row, mid_a, cross_own)
    near = near + near_row.astype(F32)

    near = move(near.astype(BF16), near_)
    mid_b = move(mid[half:], mid_)
    own = own + move(cross_own, row).astype(F32) + jnp.concatenate([mid_a, mid_b]).astype(F32)
    return (after(own) + near.astype(F32)).astype(BF16)


def local(grad_out, gate_saved, up_saved, w_gate, w_up, w_down):
    grad_hidden = contract_last(lax.all_gather(grad_out, "wid", axis=1, tiled=True), w_down)
    gate = gate_saved.astype(F32)
    up = up_saved.astype(F32)
    sig = jax.nn.sigmoid(gate)
    grad_gate = (grad_hidden * up * sig * (1.0 + gate * (1.0 - sig))).astype(BF16)
    grad_up = (grad_hidden * gate * sig).astype(BF16)
    summed = lax.psum_scatter(
        contract_last(w_gate, grad_gate) + contract_last(w_up, grad_up),
        "wid",
        scatter_dimension=0,
        tiled=True,
    )
    return summed.astype(BF16).T


def solution(mesh):
    in_specs = (
        P("grp", "wid"),
        P("grp", "wid"),
        P("grp", "wid"),
        P(None, "wid"),
        P(None, "wid"),
        P("wid", None),
    )
    out_specs = P("grp", "wid")
    body = staged if mesh.shape["wid"] == 16 else local
    return jax.shard_map(body, mesh=mesh, in_specs=in_specs, out_specs=out_specs, check_vma=False)
```

time: 219 us -> 85.2 us (0.39)
  waiting for transfers between devices: 162 us -> 28.1 us
  matrix products: 41.1 us -> 0 us
  Pallas kernels: 0 us -> 28.8 us
  starting transfers between devices: 0.04 us -> 25.5 us
  between operations: 13.4 us -> 0.35 us
    reduce_scatter x1 -> x0, waiting for transfers between devices: 103 us -> none  [local(): lax.psum_scatter(contract_last(w_gate, grad_gate) + contract_last(w_up, g...]
    all_gather x1 -> x0, waiting for transfers between devices: 58.2 us -> none  [local(): lax.all_gather(grad_out, 'wid', axis=1, tiled=True)]
    dot_general x3 -> x0, matrix products: 41.1 us -> none  [contract_last(): lax.dot_general(left, right, (((1,), (1,)), ((), ())), preferred_element_...]
    pallas_call x0 -> x11, Pallas kernels: none -> 28.8 us  [call(): pl.pallas_call(body, in_specs=[pl.BlockSpec(memory_space=space) for space...]
    ppermute x0 -> x29, waiting for transfers between devices: none -> 28.1 us  [move(): return lax.ppermute(x, 'wid', [(i, i ^ bits) for i in range(n)])]
    ppermute x0 -> x29, starting transfers between devices: none -> 25.5 us  [move(): return lax.ppermute(x, 'wid', [(i, i ^ bits) for i in range(n)])]
  transfers between devices with their start and end apart: 2 -> 29, of which waited for: 2 -> 11; matrix products, arithmetic and copies ran while one was open for 0% -> 2% of each run, Pallas kernels for 0% -> 29%
where the time goes in v3:
time: 85.2 us; the launch traced here: 85 us
  Pallas kernels  28.8 us (34%)
  waiting for transfers between devices  28.1 us (33%)
  starting transfers between devices  25.5 us (30%)
  local copies, waits for them, and re-layouts  1.21 us (1%)
  other arithmetic  1.12 us (1%)
    pallas_call x11, Pallas kernels, call(): pl.pallas_call(body, in_specs=[pl.BlockSpec(memory_space=space) for space...  28.8 us
    ppermute x29, waiting for transfers between devices, move(): return lax.ppermute(x, 'wid', [(i, i ^ bits) for i in range(n)])  28.1 us
    ppermute x29, starting transfers between devices, move(): return lax.ppermute(x, 'wid', [(i, i ^ bits) for i in range(n)])  25.5 us
  transfers between devices with their start and end apart: 29, of which 11 were waited for; matrix products, arithmetic and copies ran while one was open for 2% of the time, Pallas kernels for 29%

profile of v3, /device:TPU:0, one launch (start us, length us, event | category | flops | bytes accessed | tf_op | source)
XLA Modules:
  0.0 85.0 jit_solution(14574351320875569567)
XLA Ops:
  0.0 3.0 %collective-permute-start.2 = (bf16[256,512]{1,0:T(8,128)(2,1)}, bf16[256,512]{1,0:T(8,128)(2,1)S(1)}, u32[]{:S(2)}, u32[]{:S(2)}) collective-permute-start(bf16[256,512]{1,0:T(8,128)(2,1)} %refs_0_.1), channel_id=1, source_target_pairs={{0,4},{1,5},{2,6},{3,7},{4,0},{5,1},{6,2},{7,3},{8,12},{9,13},{10,... | collective-permute-start | bytes 786440 | tf_op jit(solution)/shard_map/ppermute | solution.py:206
  3.0 1.5 %collective-permute-start.5 = (bf16[256,512]{1,0:T(8,128)(2,1)}, bf16[256,512]{1,0:T(8,128)(2,1)S(1)}, u32[]{:S(2)}, u32[]{:S(2)}) collective-permute-start(bf16[256,512]{1,0:T(8,128)(2,1)} %refs_0_.1), channel_id=1, source_target_pairs={{0,2},{1,3},{2,0},{3,1},{4,6},{5,7},{6,4},{7,5},{8,10},{9,11},{10,... | collective-permute-start | bytes 786440 | tf_op jit(solution)/shard_map/ppermute | solution.py:206
  4.5 0.0 collective-permute-start.4
  4.5 1.0 %fusion.1 = (bf16[128,512]{1,0:T(8,128)(2,1)S(1)}, bf16[128,512]{1,0:T(8,128)(2,1)S(1)}) fusion(bf16[256,512]{1,0:T(8,128)(2,1)} %refs_0_.1), kind=kLoop, calls=%fused_computation.10 | loop fusion | bytes 524288 | tf_op jit(solution)/shard_map/slice | solution.py:222
  5.5 2.7 %collective-permute-start = (bf16[128,512]{1,0:T(8,128)(2,1)S(1)}, bf16[128,512]{1,0:T(8,128)(2,1)S(1)}, u32[]{:S(2)}, u32[]{:S(2)}) collective-permute-start(bf16[128,512]{1,0:T(8,128)(2,1)S(1)} %get-tuple-element.54), channel_id=1, source_target_pairs={{0,8},{1,9},{2,10},{3,11},{4,12},{5,13},{6,14},{7,15},{8,0},{9,1},... | collective-permute-start | bytes 393224 | tf_op jit(solution)/shard_map/ppermute | solution.py:206
  8.2 1.8 %shard_map.64 = (f32[256,1024]{1,0:T(8,128)S(1)}, f32[256,1024]{1,0:T(8,128)S(1)}) custom-call(bf16[256,1024]{1,0:T(8,128)(2,1)} %gate.1, bf16[256,1024]{1,0:T(8,128)(2,1)} %up.1), custom_call_target="tpu_custom_call" | custom-call | flops 200000000 | tf_op jit(solution)/shard_map/pallas_call | solution.py:30
  10.0 0.0 collective-permute-done.2.refs_3_
  10.0 4.0 %collective-permute-start.6 = (bf16[256,512]{1,0:T(8,128)(2,1)S(1)}, bf16[256,512]{1,0:T(8,128)(2,1)S(1)}, u32[]{:S(2)}, u32[]{:S(2)}) collective-permute-start(bf16[256,512]{1,0:T(8,128)(2,1)S(1)} %collective-permute-done.2.refs_3_), channel_id=1, source_target_pairs={{0,2},{1,3},{2,0},{3,1},{4,6},{5,7},{6,4},{7,5},{8,10},{9,11},{10,... | collective-permute-start | bytes 786440 | tf_op jit(solution)/shard_map/ppermute | solution.py:206
  14.0 1.2 %collective-permute-done = bf16[128,512]{1,0:T(8,128)(2,1)S(1)} collective-permute-done((bf16[128,512]{1,0:T(8,128)(2,1)S(1)}, bf16[128,512]{1,0:T(8,128)(2,1)S(1)}, u32[]{:S(2)}, u32[]{:S(2)}) %collective-permute-start) | collective-permute-done | bytes 131104 | tf_op jit(solution)/shard_map/ppermute | solution.py:206
  15.2 3.1 %collective-permute-start.3 = (bf16[128,512]{1,0:T(8,128)(2,1)S(1)}, bf16[128,512]{1,0:T(8,128)(2,1)S(1)}, u32[]{:S(2)}, u32[]{:S(2)}) collective-permute-start(bf16[128,512]{1,0:T(8,128)(2,1)S(1)} %get-tuple-element.30), channel_id=1, source_target_pairs={{0,8},{1,9},{2,10},{3,11},{4,12},{5,13},{6,14},{7,15},{8,0},{9,1},... | collective-permute-start | bytes 393224 | tf_op jit(solution)/shard_map/ppermute | solution.py:206
  18.3 0.0 slice-start
  18.3 0.0 slice-start.1
  18.3 0.0 copy-start
  18.4 0.1 collective-permute-start.9
  18.4 0.0 collective-permute-done.4.refs_1_
  18.5 0.5 collective-permute-start.8
  18.9 3.7 %shard_map.65.refs_5_ = f32[256,1024]{1,0:T(8,128)S(1)} custom-call(bf16[256,512]{1,0:T(8,128)(2,1)} %refs_0_.1, bf16[256,512]{1,0:T(8,128)(2,1)S(1)} %collective-permute-done.4.refs_1_, bf16[256,512]{1,0:T(8,128)(2,1)S(1)} %collective-permute-done.5.refs_2_, bf16[256,512]{1,0:T(8,128)(2,1)S(1)} %collective-permute-done.2.refs_3_, bf16[1024,8192]{1,0:T(8,128)(2,1)} %refs_2_.1), custom_call_target="tpu_custom_call" | custom-call | flops 600000000 | tf_op jit(solution)/shard_map/pallas_call | solution.py:30
  22.6 1.6 %collective-permute-done.3 = bf16[128,512]{1,0:T(8,128)(2,1)S(1)} collective-permute-done((bf16[128,512]{1,0:T(8,128)(2,1)S(1)}, bf16[128,512]{1,0:T(8,128)(2,1)S(1)}, u32[]{:S(2)}, u32[]{:S(2)}) %collective-permute-start.3) | collective-permute-done | bytes 131104 | tf_op jit(solution)/shard_map/ppermute | solution.py:206
  24.3 0.3 collective-permute-start.7
  24.6 0.6 collective-permute-start.13
  25.2 0.0 collective-permute-done.1
  25.2 0.0 slice-start.2
  25.2 0.1 collective-permute-start.12
  25.3 0.5 collective-permute-start.11
  25.8 4.2 %shard_map.66.refs_7_ = f32[256,1024]{1,0:T(8,128)S(1)} custom-call(bf16[256,512]{1,0:T(8,128)(2,1)S(1)} %collective-permute-done.8.refs_0_, bf16[256,512]{1,0:T(8,128)(2,1)S(1)} %collective-permute-done.9.refs_1_, bf16[256,512]{1,0:T(8,128)(2,1)S(1)} %collective-permute-done.6.refs_2_, bf16[256,512]{1,0:T(8,128)(2,1)S(1)} %constant_dynamic-update-slice_fusion.refs_3_, ...), custom_call_target="tpu_custom_call" | custom-call | flops 600000000 | tf_op jit(solution)/shard_map/pallas_call | solution.py:30
  30.0 0.2 collective-permute-start.15
  30.2 1.5 %collective-permute-done.13.refs_2_ = bf16[256,512]{1,0:T(8,128)(2,1)S(1)} collective-permute-done((bf16[256,512]{1,0:T(8,128)(2,1)S(1)}, bf16[256,512]{1,0:T(8,128)(2,1)S(1)}, u32[]{:S(2)}, u32[]{:S(2)}) %collective-permute-start.13) | collective-permute-done | bytes 262176 | tf_op jit(solution)/shard_map/ppermute | solution.py:206
  31.7 0.5 collective-permute-start.10
  32.2 1.0 %collective-permute-done.14.refs_4_ = bf16[256,512]{1,0:T(8,128)(2,1)S(1)} collective-permute-done((bf16[256,512]{1,0:T(8,128)(2,1)S(1)}, bf16[256,512]{1,0:T(8,128)(2,1)S(1)}, u32[]{:S(2)}, u32[]{:S(2)}) %collective-permute-start.14) | collective-permute-done | bytes 262176 | tf_op jit(solution)/shard_map/ppermute | solution.py:206
  33.2 0.0 slice-start.4
  33.2 0.0 slice-start.5
  33.3 0.0 slice-start.6
  33.3 4.4 %shard_map.67.refs_3_ = f32[256,1024]{1,0:T(8,128)S(1)} custom-call(bf16[256,512]{1,0:T(8,128)(2,1)S(1)} %collective-permute-done.11.refs_0_, bf16[256,512]{1,0:T(8,128)(2,1)S(1)} %collective-permute-done.12.refs_1_, bf16[256,512]{1,0:T(8,128)(2,1)S(1)} %collective-permute-done.13.refs_2_, bf16[256,512]{1,0:T(8,128)(2,1)S(1)} %constant_dynamic-update-slice_fusion.2.refs_3_, ...), custom_call_target="tpu_custom_call" | custom-call | flops 600000000 | tf_op jit(solution)/shard_map/pallas_call | solution.py:30
  37.6 2.7 %collective-permute-done.10.refs_0_ = bf16[256,512]{1,0:T(8,128)(2,1)S(1)} collective-permute-done((bf16[256,512]{1,0:T(8,128)(2,1)S(1)}, bf16[256,512]{1,0:T(8,128)(2,1)S(1)}, u32[]{:S(2)}, u32[]{:S(2)}) %collective-permute-start.10) | collective-permute-done | bytes 262176 | tf_op jit(solution)/shard_map/ppermute | solution.py:206
  40.4 1.5 %collective-permute-done.16.refs_1_ = bf16[256,512]{1,0:T(8,128)(2,1)S(1)} collective-permute-done((bf16[256,512]{1,0:T(8,128)(2,1)S(1)}, bf16[256,512]{1,0:T(8,128)(2,1)S(1)}, u32[]{:S(2)}, u32[]{:S(2)}) %collective-permute-start.16) | collective-permute-done | bytes 262176 | tf_op jit(solution)/shard_map/ppermute | solution.py:206
  41.9 2.7 %shard_map.68 = (bf16[256,1024]{1,0:T(8,128)(2,1)S(1)}, bf16[256,1024]{1,0:T(8,128)(2,1)S(1)}) custom-call(bf16[256,512]{1,0:T(8,128)(2,1)S(1)} %collective-permute-done.10.refs_0_, bf16[256,512]{1,0:T(8,128)(2,1)S(1)} %collective-permute-done.16.refs_1_, bf16[1024,8192]{1,0:T(8,128)(2,1)} %refs_2_.1, f32[256,1024]{1,0:T(8,128)S(1)} %shard_map.67.refs_3_, ...), custom_call_target="tpu_custom_call" | custom-call | flops 600000000 | tf_op jit(solution)/shard_map/pallas_call | solution.py:30
  44.6 0.1 slice-done.7
  44.7 1.5 %shard_map.73 = bf16[256,1024]{1,0:T(8,128)(2,1)S(1)} custom-call(bf16[256,1024]{1,0:T(8,128)(2,1)S(1)} %get-tuple-element.36.grad_gate, bf16[256,1024]{1,0:T(8,128)(2,1)S(1)} %get-tuple-element.37.grad_up, bf16[8192,1024]{1,0:T(8,128)(2,1)S(1)} %bitcast.1, bf16[8192,1024]{1,0:T(8,128)(2,1)S(1)} %bitcast.3), custom_call_target="tpu_custom_call" | custom-call | flops 150000000 | tf_op jit(solution)/shard_map/pallas_call | solution.py:30
  46.2 0.2 collective-permute-start.22
  46.4 1.5 %shard_map.69 = bf16[256,1024]{1,0:T(8,128)(2,1)S(1)} custom-call(bf16[256,1024]{1,0:T(8,128)(2,1)S(1)} %get-tuple-element.36.grad_gate, bf16[256,1024]{1,0:T(8,128)(2,1)S(1)} %get-tuple-element.37.grad_up, bf16[8192,1024]{1,0:T(8,128)(2,1)S(1)} %bitcast.1, bf16[8192,1024]{1,0:T(8,128)(2,1)S(1)} %bitcast.3), custom_call_target="tpu_custom_call" | custom-call | flops 150000000 | tf_op jit(solution)/shard_map/pallas_call | solution.py:30
  47.9 0.4 collective-permute-start.17
  48.4 1.6 %shard_map.74 = (f32[256,512]{1,0:T(8,128)S(1)}, bf16[256,512]{1,0:T(8,128)(2,1)S(1)}) custom-call(bf16[256,1024]{1,0:T(8,128)(2,1)S(1)} %get-tuple-element.36.grad_gate, bf16[256,1024]{1,0:T(8,128)(2,1)S(1)} %get-tuple-element.37.grad_up, bf16[8192,1024]{1,0:T(8,128)(2,1)S(1)} %bitcast.1, bf16[8192,1024]{1,0:T(8,128)(2,1)S(1)} %bitcast.3, ...), custom_call_target="tpu_custom_call" | custom-call | flops 300000000 | tf_op jit(solution)/shard_map/pallas_call | solution.py:30
  49.9 0.6 collective-permute-start.23
  50.5 3.0 %shard_map.70 = (f32[256,512]{1,0:T(8,128)S(1)}, bf16[256,512]{1,0:T(8,128)(2,1)S(1)}, bf16[256,1024]{1,0:T(8,128)(2,1)S(1)}) custom-call(bf16[256,1024]{1,0:T(8,128)(2,1)S(1)} %get-tuple-element.36.grad_gate, bf16[256,1024]{1,0:T(8,128)(2,1)S(1)} %get-tuple-element.37.grad_up, bf16[8192,1024]{1,0:T(8,128)(2,1)S(1)} %bitcast.1, ...), custom_call_target="tpu_custom_call" | custom-call | flops 450000000 | tf_op jit(solution)/shard_map/pallas_call | solution.py:30
  53.6 0.1 collective-permute-start.18
  53.6 1.6 %collective-permute-start.21 = (bf16[256,512]{1,0:T(8,128)(2,1)S(1)}, bf16[256,512]{1,0:T(8,128)(2,1)S(1)}, u32[]{:S(2)}, u32[]{:S(2)}) collective-permute-start(bf16[256,512]{1,0:T(8,128)(2,1)S(1)} %get-tuple-element.43), channel_id=1, source_target_pairs={{0,2},{1,3},{2,0},{3,1},{4,6},{5,7},{6,4},{7,5},{8,10},{9,11},{10,... | collective-permute-start | bytes 786440 | tf_op jit(solution)/shard_map/ppermute | solution.py:206
  55.2 3.9 %collective-permute-done.23 = bf16[256,512]{1,0:T(8,128)(2,1)S(1)} collective-permute-done((bf16[256,512]{1,0:T(8,128)(2,1)S(1)}, bf16[256,512]{1,0:T(8,128)(2,1)S(1)}, u32[]{:S(2)}, u32[]{:S(2)}) %collective-permute-start.23) | collective-permute-done | bytes 262176 | tf_op jit(solution)/shard_map/ppermute | solution.py:206
  59.2 0.1 add_convert_fusion.3
  59.2 1.6 %collective-permute-start.24 = (bf16[256,512]{1,0:T(8,128)(2,1)S(1)}, bf16[256,512]{1,0:T(8,128)(2,1)S(1)}, u32[]{:S(2)}, u32[]{:S(2)}) collective-permute-start(bf16[256,512]{1,0:T(8,128)(2,1)S(1)} %add_convert_fusion.3), channel_id=1, source_target_pairs={{0,4},{1,5},{2,6},{3,7},{4,0},{5,1},{6,2},{7,3},{8,12},{9,13},{10,... | collective-permute-start | bytes 786440 | tf_op jit(solution)/shard_map/ppermute | solution.py:206
  60.9 3.0 %shard_map.71 = (f32[256,512]{1,0:T(8,128)S(1)}, bf16[256,512]{1,0:T(8,128)(2,1)S(1)}, bf16[256,1024]{1,0:T(8,128)(2,1)S(1)}) custom-call(bf16[256,1024]{1,0:T(8,128)(2,1)S(1)} %get-tuple-element.36.grad_gate, bf16[256,1024]{1,0:T(8,128)(2,1)S(1)} %get-tuple-element.37.grad_up, bf16[8192,1024]{1,0:T(8,128)(2,1)S(1)} %bitcast.1, ...), custom_call_target="tpu_custom_call" | custom-call | flops 450000000 | tf_op jit(solution)/shard_map/pallas_call | solution.py:30
  63.9 0.3 collective-permute-start.26
  64.2 1.8 %collective-permute-done.24 = bf16[256,512]{1,0:T(8,128)(2,1)S(1)} collective-permute-done((bf16[256,512]{1,0:T(8,128)(2,1)S(1)}, bf16[256,512]{1,0:T(8,128)(2,1)S(1)}, u32[]{:S(2)}, u32[]{:S(2)}) %collective-permute-start.24) | collective-permute-done | bytes 262176 | tf_op jit(solution)/shard_map/ppermute | solution.py:206
  66.0 0.1 add_convert_fusion.2
  66.1 2.5 %collective-permute-start.25 = (bf16[128,512]{1,0:T(8,128)(2,1)S(1)}, bf16[128,512]{1,0:T(8,128)(2,1)S(1)}, u32[]{:S(2)}, u32[]{:S(2)}) collective-permute-start(bf16[128,512]{1,0:T(8,128)(2,1)S(1)} %get-tuple-element.51), channel_id=1, source_target_pairs={{0,8},{1,9},{2,10},{3,11},{4,12},{5,13},{6,14},{7,15},{8,0},{9,1},... | collective-permute-start | bytes 393224 | tf_op jit(solution)/shard_map/ppermute | solution.py:206
  68.6 1.6 %shard_map.72 = (f32[256,512]{1,0:T(8,128)S(1)}, bf16[256,512]{1,0:T(8,128)(2,1)S(1)}) custom-call(bf16[256,1024]{1,0:T(8,128)(2,1)S(1)} %get-tuple-element.36.grad_gate, bf16[256,1024]{1,0:T(8,128)(2,1)S(1)} %get-tuple-element.37.grad_up, bf16[8192,1024]{1,0:T(8,128)(2,1)S(1)} %bitcast.1, bf16[8192,1024]{1,0:T(8,128)(2,1)S(1)} %bitcast.3, ...), custom_call_target="tpu_custom_call" | custom-call | flops 300000000 | tf_op jit(solution)/shard_map/pallas_call | solution.py:30
  70.2 0.4 collective-permute-start.20
  70.6 0.7 collective-permute-start.27
  71.3 6.5 %collective-permute-done.25 = bf16[128,512]{1,0:T(8,128)(2,1)S(1)} collective-permute-done((bf16[128,512]{1,0:T(8,128)(2,1)S(1)}, bf16[128,512]{1,0:T(8,128)(2,1)S(1)}, u32[]{:S(2)}, u32[]{:S(2)}) %collective-permute-start.25) | collective-permute-done | bytes 131104 | tf_op jit(solution)/shard_map/ppermute | solution.py:206
  77.8 0.1 add_convert_fusion.1
  77.8 0.1 collective-permute-start.28
  77.9 1.8 %collective-permute-done.27 = bf16[128,512]{1,0:T(8,128)(2,1)S(1)} collective-permute-done((bf16[128,512]{1,0:T(8,128)(2,1)S(1)}, bf16[128,512]{1,0:T(8,128)(2,1)S(1)}, u32[]{:S(2)}, u32[]{:S(2)}) %collective-permute-start.27) | collective-permute-done | bytes 131104 | tf_op jit(solution)/shard_map/ppermute | solution.py:206
  79.8 0.1 convert_add_fusion
  79.9 4.4 %collective-permute-done.28 = bf16[256,512]{1,0:T(8,128)(2,1)S(1)} collective-permute-done((bf16[256,512]{1,0:T(8,128)(2,1)S(1)}, bf16[256,512]{1,0:T(8,128)(2,1)S(1)}, u32[]{:S(2)}, u32[]{:S(2)}) %collective-permute-start.28) | collective-permute-done | bytes 262176 | tf_op jit(solution)/shard_map/ppermute | solution.py:206
  84.3 0.8 add_convert_fusion
  (36 shorter events, 0.1 us)
Async XLA Ops:
  0.0 10.0 %collective-permute-start.2 = (bf16[256,512]{1,0:T(8,128)(2,1)}, bf16[256,512]{1,0:T(8,128)(2,1)S(1)}, u32[]{:S(2)}, u32[]{:S(2)}) collective-permute-start(bf16[256,512]{1,0:T(8,128)(2,1)} %refs_0_.1), channel_id=1, source_target_pairs={{0,4},{1,5},{2,6},{3,7},{4,0},{5,1},{6,2},{7,3},{8,12},{9,13},{10,... | collective-permute-start | bytes 786440 | tf_op jit(solution)/shard_map/ppermute | solution.py:206
  3.0 15.3 %collective-permute-start.5 = (bf16[256,512]{1,0:T(8,128)(2,1)}, bf16[256,512]{1,0:T(8,128)(2,1)S(1)}, u32[]{:S(2)}, u32[]{:S(2)}) collective-permute-start(bf16[256,512]{1,0:T(8,128)(2,1)} %refs_0_.1), channel_id=1, source_target_pairs={{0,2},{1,3},{2,0},{3,1},{4,6},{5,7},{6,4},{7,5},{8,10},{9,11},{10,... | collective-permute-start | bytes 786440 | tf_op jit(solution)/shard_map/ppermute | solution.py:206
  4.5 13.9 %collective-permute-start.4 = (bf16[256,512]{1,0:T(8,128)(2,1)}, bf16[256,512]{1,0:T(8,128)(2,1)S(1)}, u32[]{:S(2)}, u32[]{:S(2)}) collective-permute-start(bf16[256,512]{1,0:T(8,128)(2,1)} %refs_0_.1), channel_id=1, source_target_pairs={{0,1},{1,0},{2,3},{3,2},{4,5},{5,4},{6,7},{7,6},{8,9},{9,8},{10,11... | collective-permute-start | bytes 786440 | tf_op jit(solution)/shard_map/ppermute | solution.py:206
  5.5 9.7 %collective-permute-start = (bf16[128,512]{1,0:T(8,128)(2,1)S(1)}, bf16[128,512]{1,0:T(8,128)(2,1)S(1)}, u32[]{:S(2)}, u32[]{:S(2)}) collective-permute-start(bf16[128,512]{1,0:T(8,128)(2,1)S(1)} %get-tuple-element.54), channel_id=1, source_target_pairs={{0,8},{1,9},{2,10},{3,11},{4,12},{5,13},{6,14},{7,15},{8,0},{9,1},... | collective-permute-start | bytes 393224 | tf_op jit(solution)/shard_map/ppermute | solution.py:206
  10.0 14.3 %collective-permute-start.6 = (bf16[256,512]{1,0:T(8,128)(2,1)S(1)}, bf16[256,512]{1,0:T(8,128)(2,1)S(1)}, u32[]{:S(2)}, u32[]{:S(2)}) collective-permute-start(bf16[256,512]{1,0:T(8,128)(2,1)S(1)} %collective-permute-done.2.refs_3_), channel_id=1, source_target_pairs={{0,2},{1,3},{2,0},{3,1},{4,6},{5,7},{6,4},{7,5},{8,10},{9,11},{10,... | collective-permute-start | bytes 786440 | tf_op jit(solution)/shard_map/ppermute | solution.py:206
  15.2 10.0 %collective-permute-start.1 = (bf16[128,512]{1,0:T(8,128)(2,1)S(1)}, bf16[128,512]{1,0:T(8,128)(2,1)S(1)}, u32[]{:S(2)}, u32[]{:S(2)}) collective-permute-start(bf16[128,512]{1,0:T(8,128)(2,1)S(1)} %collective-permute-done), channel_id=1, source_target_pairs={{0,4},{1,5},{2,6},{3,7},{4,0},{5,1},{6,2},{7,3},{8,12},{9,13},{10,... | collective-permute-start | bytes 393224 | tf_op jit(solution)/shard_map/ppermute | solution.py:206
  15.2 9.0 %collective-permute-start.3 = (bf16[128,512]{1,0:T(8,128)(2,1)S(1)}, bf16[128,512]{1,0:T(8,128)(2,1)S(1)}, u32[]{:S(2)}, u32[]{:S(2)}) collective-permute-start(bf16[128,512]{1,0:T(8,128)(2,1)S(1)} %get-tuple-element.30), channel_id=1, source_target_pairs={{0,8},{1,9},{2,10},{3,11},{4,12},{5,13},{6,14},{7,15},{8,0},{9,1},... | collective-permute-start | bytes 393224 | tf_op jit(solution)/shard_map/ppermute | solution.py:206
  18.3 14.9 %slice-start = ((s8[16777216]{0:T(1024)(128)(4,1)}), s8[4194304]{0:T(1024)(128)(4,1)S(1)}, s32[]{:S(2)}) async-start(s8[16777216]{0:T(1024)(128)(4,1)} %bitcast), calls=%async_computation | async-start | bytes 8388608
  18.3 14.9 %slice-start.1 = ((s8[16777216]{0:T(1024)(128)(4,1)}), s8[4194304]{0:T(1024)(128)(4,1)S(1)}, s32[]{:S(2)}) async-start(s8[16777216]{0:T(1024)(128)(4,1)} %bitcast), calls=%async_computation.1 | async-start | bytes 8388608
  18.3 14.9 %copy-start = (bf16[8192,1024]{1,0:T(8,128)(2,1)S(1)}, bf16[8192,1024]{1,0:T(8,128)(2,1)}, u32[]{:S(2)}) copy-start(bf16[8192,1024]{1,0:T(8,128)(2,1)} %w_up.11) | copy-start | bytes 50331652
  18.4 6.9 %collective-permute-start.9 = (bf16[256,512]{1,0:T(8,128)(2,1)S(1)}, bf16[256,512]{1,0:T(8,128)(2,1)S(1)}, u32[]{:S(2)}, u32[]{:S(2)}) collective-permute-start(bf16[256,512]{1,0:T(8,128)(2,1)S(1)} %collective-permute-done.2.refs_3_), channel_id=1, source_target_pairs={{0,1},{1,0},{2,3},{3,2},{4,5},{5,4},{6,7},{7,6},{8,9},{9,8},{10,11... | collective-permute-start | bytes 786440 | tf_op jit(solution)/shard_map/ppermute | solution.py:206
  18.5 7.4 %collective-permute-start.8 = (bf16[256,512]{1,0:T(8,128)(2,1)S(1)}, bf16[256,512]{1,0:T(8,128)(2,1)S(1)}, u32[]{:S(2)}, u32[]{:S(2)}) collective-permute-start(bf16[256,512]{1,0:T(8,128)(2,1)S(1)} %collective-permute-done.5.refs_2_), channel_id=1, source_target_pairs={{0,1},{1,0},{2,3},{3,2},{4,5},{5,4},{6,7},{7,6},{8,9},{9,8},{10,11... | collective-permute-start | bytes 786440 | tf_op jit(solution)/shard_map/ppermute | solution.py:206
  24.3 5.7 %collective-permute-start.7 = (bf16[128,512]{1,0:T(8,128)(2,1)S(1)}, bf16[128,512]{1,0:T(8,128)(2,1)S(1)}, u32[]{:S(2)}, u32[]{:S(2)}) collective-permute-start(bf16[128,512]{1,0:T(8,128)(2,1)S(1)} %collective-permute-done.3), channel_id=1, source_target_pairs={{0,4},{1,5},{2,6},{3,7},{4,0},{5,1},{6,2},{7,3},{8,12},{9,13},{10,... | collective-permute-start | bytes 393224 | tf_op jit(solution)/shard_map/ppermute | solution.py:206
  24.6 7.0 %collective-permute-start.13 = (bf16[256,512]{1,0:T(8,128)(2,1)S(1)}, bf16[256,512]{1,0:T(8,128)(2,1)S(1)}, u32[]{:S(2)}, u32[]{:S(2)}) collective-permute-start(bf16[256,512]{1,0:T(8,128)(2,1)S(1)} %constant_dynamic-update-slice_fusion.refs_3_), channel_id=1, source_target_pairs={{0,2},{1,3},{2,0},{3,1},{4,6},{5,7},{6,4},{7,5},{8,10},{9,11},{10,... | collective-permute-start | bytes 786440 | tf_op jit(solution)/shard_map/ppermute | solution.py:206
  25.2 8.0 %slice-start.2 = ((s8[16777216]{0:T(1024)(128)(4,1)}), s8[4194304]{0:T(1024)(128)(4,1)S(1)}, s32[]{:S(2)}) async-start(s8[16777216]{0:T(1024)(128)(4,1)} %bitcast), calls=%async_computation.2 | async-start | bytes 8388608
  25.2 8.0 %slice-start.3 = ((s8[16777216]{0:T(1024)(128)(4,1)}), s8[4194304]{0:T(1024)(128)(4,1)S(1)}, s32[]{:S(2)}) async-start(s8[16777216]{0:T(1024)(128)(4,1)} %bitcast), calls=%async_computation.3 | async-start | bytes 8388608
  25.2 6.9 %collective-permute-start.12 = (bf16[256,512]{1,0:T(8,128)(2,1)S(1)}, bf16[256,512]{1,0:T(8,128)(2,1)S(1)}, u32[]{:S(2)}, u32[]{:S(2)}) collective-permute-start(bf16[256,512]{1,0:T(8,128)(2,1)S(1)} %constant_dynamic-update-slice_fusion.refs_3_), channel_id=1, source_target_pairs={{0,1},{1,0},{2,3},{3,2},{4,5},{5,4},{6,7},{7,6},{8,9},{9,8},{10,11... | collective-permute-start | bytes 786440 | tf_op jit(solution)/shard_map/ppermute | solution.py:206
  25.3 6.9 %collective-permute-start.11 = (bf16[256,512]{1,0:T(8,128)(2,1)S(1)}, bf16[256,512]{1,0:T(8,128)(2,1)S(1)}, u32[]{:S(2)}, u32[]{:S(2)}) collective-permute-start(bf16[256,512]{1,0:T(8,128)(2,1)S(1)} %collective-permute-done.6.refs_2_), channel_id=1, source_target_pairs={{0,1},{1,0},{2,3},{3,2},{4,5},{5,4},{6,7},{7,6},{8,9},{9,8},{10,11... | collective-permute-start | bytes 786440 | tf_op jit(solution)/shard_map/ppermute | solution.py:206
  30.0 2.1 %collective-permute-start.15 = (bf16[256,512]{1,0:T(8,128)(2,1)S(1)}, bf16[256,512]{1,0:T(8,128)(2,1)S(1)}, u32[]{:S(2)}, u32[]{:S(2)}) collective-permute-start(bf16[256,512]{1,0:T(8,128)(2,1)S(1)} %constant_dynamic-update-slice_fusion.2.refs_3_), channel_id=1, source_target_pairs={{0,1},{1,0},{2,3},{3,2},{4,5},{5,4},{6,7},{7,6},{8,9},{9,8},{10,11... | collective-permute-start | bytes 786440 | tf_op jit(solution)/shard_map/ppermute | solution.py:206
  31.7 1.5 %collective-permute-start.14 = (bf16[256,512]{1,0:T(8,128)(2,1)S(1)}, bf16[256,512]{1,0:T(8,128)(2,1)S(1)}, u32[]{:S(2)}, u32[]{:S(2)}) collective-permute-start(bf16[256,512]{1,0:T(8,128)(2,1)S(1)} %collective-permute-done.13.refs_2_), channel_id=1, source_target_pairs={{0,1},{1,0},{2,3},{3,2},{4,5},{5,4},{6,7},{7,6},{8,9},{9,8},{10,11... | collective-permute-start | bytes 786440 | tf_op jit(solution)/shard_map/ppermute | solution.py:206
  31.7 8.7 %collective-permute-start.10 = (bf16[256,512]{1,0:T(8,128)(2,1)S(1)}, bf16[256,512]{1,0:T(8,128)(2,1)S(1)}, u32[]{:S(2)}, u32[]{:S(2)}) collective-permute-start(bf16[256,512]{1,0:T(8,128)(2,1)S(1)} %constant_dynamic-update-slice_fusion.2.refs_3_), channel_id=1, source_target_pairs={{0,2},{1,3},{2,0},{3,1},{4,6},{5,7},{6,4},{7,5},{8,10},{9,11},{10,... | collective-permute-start | bytes 786440 | tf_op jit(solution)/shard_map/ppermute | solution.py:206
  33.2 11.4 %slice-start.4 = ((s8[16777216]{0:T(1024)(128)(4,1)}), s8[4194304]{0:T(1024)(128)(4,1)S(1)}, s32[]{:S(2)}) async-start(s8[16777216]{0:T(1024)(128)(4,1)} %bitcast.2), calls=%async_computation.4 | async-start | bytes 8388608
  33.2 11.4 %slice-start.5 = ((s8[16777216]{0:T(1024)(128)(4,1)}), s8[4194304]{0:T(1024)(128)(4,1)S(1)}, s32[]{:S(2)}) async-start(s8[16777216]{0:T(1024)(128)(4,1)} %bitcast.2), calls=%async_computation.5 | async-start | bytes 8388608
  33.3 11.4 %slice-start.6 = ((s8[16777216]{0:T(1024)(128)(4,1)}), s8[4194304]{0:T(1024)(128)(4,1)S(1)}, s32[]{:S(2)}) async-start(s8[16777216]{0:T(1024)(128)(4,1)} %bitcast.2), calls=%async_computation.6 | async-start | bytes 8388608
  40.4 1.5 %collective-permute-start.16 = (bf16[256,512]{1,0:T(8,128)(2,1)S(1)}, bf16[256,512]{1,0:T(8,128)(2,1)S(1)}, u32[]{:S(2)}, u32[]{:S(2)}) collective-permute-start(bf16[256,512]{1,0:T(8,128)(2,1)S(1)} %collective-permute-done.10.refs_0_), channel_id=1, source_target_pairs={{0,1},{1,0},{2,3},{3,2},{4,5},{5,4},{6,7},{7,6},{8,9},{9,8},{10,11... | collective-permute-start | bytes 786440 | tf_op jit(solution)/shard_map/ppermute | solution.py:206
  41.9 2.8 %slice-start.7 = ((s8[16777216]{0:T(1024)(128)(4,1)}), s8[4194304]{0:T(1024)(128)(4,1)S(1)}, s32[]{:S(2)}) async-start(s8[16777216]{0:T(1024)(128)(4,1)} %bitcast.2), calls=%async_computation.7 | async-start | bytes 8388608
  46.2 2.1 %collective-permute-start.22 = (bf16[256,1024]{1,0:T(8,128)(2,1)S(1)}, bf16[256,1024]{1,0:T(8,128)(2,1)S(1)}, u32[]{:S(2)}, u32[]{:S(2)}) collective-permute-start(bf16[256,1024]{1,0:T(8,128)(2,1)S(1)} %shard_map.73), channel_id=1, source_target_pairs={{0,1},{1,0},{2,3},{3,2},{4,5},{5,4},{6,7},{7,6},{8,9},{9,8},{10,11... | collective-permute-start | bytes 1572872 | tf_op jit(solution)/shard_map/ppermute | solution.py:206
  47.9 2.6 %collective-permute-start.17 = (bf16[256,1024]{1,0:T(8,128)(2,1)S(1)}, bf16[256,1024]{1,0:T(8,128)(2,1)S(1)}, u32[]{:S(2)}, u32[]{:S(2)}) collective-permute-start(bf16[256,1024]{1,0:T(8,128)(2,1)S(1)} %shard_map.69), channel_id=1, source_target_pairs={{0,1},{1,0},{2,3},{3,2},{4,5},{5,4},{6,7},{7,6},{8,9},{9,8},{10,11... | collective-permute-start | bytes 1572872 | tf_op jit(solution)/shard_map/ppermute | solution.py:206
  49.9 9.2 %collective-permute-start.23 = (bf16[256,512]{1,0:T(8,128)(2,1)S(1)}, bf16[256,512]{1,0:T(8,128)(2,1)S(1)}, u32[]{:S(2)}, u32[]{:S(2)}) collective-permute-start(bf16[256,512]{1,0:T(8,128)(2,1)S(1)} %get-tuple-element.47), channel_id=1, source_target_pairs={{0,2},{1,3},{2,0},{3,1},{4,6},{5,7},{6,4},{7,5},{8,10},{9,11},{10,... | collective-permute-start | bytes 786440 | tf_op jit(solution)/shard_map/ppermute | solution.py:206
  53.6 7.3 %collective-permute-start.18 = (bf16[256,1024]{1,0:T(8,128)(2,1)S(1)}, bf16[256,1024]{1,0:T(8,128)(2,1)S(1)}, u32[]{:S(2)}, u32[]{:S(2)}) collective-permute-start(bf16[256,1024]{1,0:T(8,128)(2,1)S(1)} %get-tuple-element.38), channel_id=1, source_target_pairs={{0,1},{1,0},{2,3},{3,2},{4,5},{5,4},{6,7},{7,6},{8,9},{9,8},{10,11... | collective-permute-start | bytes 1572872 | tf_op jit(solution)/shard_map/ppermute | solution.py:206
  53.6 10.6 %collective-permute-start.21 = (bf16[256,512]{1,0:T(8,128)(2,1)S(1)}, bf16[256,512]{1,0:T(8,128)(2,1)S(1)}, u32[]{:S(2)}, u32[]{:S(2)}) collective-permute-start(bf16[256,512]{1,0:T(8,128)(2,1)S(1)} %get-tuple-element.43), channel_id=1, source_target_pairs={{0,2},{1,3},{2,0},{3,1},{4,6},{5,7},{6,4},{7,5},{8,10},{9,11},{10,... | collective-permute-start | bytes 786440 | tf_op jit(solution)/shard_map/ppermute | solution.py:206
  59.2 6.8 %collective-permute-start.24 = (bf16[256,512]{1,0:T(8,128)(2,1)S(1)}, bf16[256,512]{1,0:T(8,128)(2,1)S(1)}, u32[]{:S(2)}, u32[]{:S(2)}) collective-permute-start(bf16[256,512]{1,0:T(8,128)(2,1)S(1)} %add_convert_fusion.3), channel_id=1, source_target_pairs={{0,4},{1,5},{2,6},{3,7},{4,0},{5,1},{6,2},{7,3},{8,12},{9,13},{10,... | collective-permute-start | bytes 786440 | tf_op jit(solution)/shard_map/ppermute | solution.py:206
  63.9 13.9 %collective-permute-start.26 = (bf16[256,512]{1,0:T(8,128)(2,1)S(1)}, bf16[256,512]{1,0:T(8,128)(2,1)S(1)}, u32[]{:S(2)}, u32[]{:S(2)}) collective-permute-start(bf16[256,512]{1,0:T(8,128)(2,1)S(1)} %get-tuple-element.44), channel_id=1, source_target_pairs={{0,2},{1,3},{2,0},{3,1},{4,6},{5,7},{6,4},{7,5},{8,10},{9,11},{10,... | collective-permute-start | bytes 786440 | tf_op jit(solution)/shard_map/ppermute | solution.py:206
  64.2 4.4 %collective-permute-start.19 = (bf16[256,1024]{1,0:T(8,128)(2,1)S(1)}, bf16[256,1024]{1,0:T(8,128)(2,1)S(1)}, u32[]{:S(2)}, u32[]{:S(2)}) collective-permute-start(bf16[256,1024]{1,0:T(8,128)(2,1)S(1)} %get-tuple-element.39), channel_id=1, source_target_pairs={{0,1},{1,0},{2,3},{3,2},{4,5},{5,4},{6,7},{7,6},{8,9},{9,8},{10,11... | collective-permute-start | bytes 1572872 | tf_op jit(solution)/shard_map/ppermute | solution.py:206
  66.1 11.6 %collective-permute-start.25 = (bf16[128,512]{1,0:T(8,128)(2,1)S(1)}, bf16[128,512]{1,0:T(8,128)(2,1)S(1)}, u32[]{:S(2)}, u32[]{:S(2)}) collective-permute-start(bf16[128,512]{1,0:T(8,128)(2,1)S(1)} %get-tuple-element.51), channel_id=1, source_target_pairs={{0,8},{1,9},{2,10},{3,11},{4,12},{5,13},{6,14},{7,15},{8,0},{9,1},... | collective-permute-start | bytes 393224 | tf_op jit(solution)/shard_map/ppermute | solution.py:206
  70.2 9.6 %collective-permute-start.20 = (bf16[256,512]{1,0:T(8,128)(2,1)S(1)}, bf16[256,512]{1,0:T(8,128)(2,1)S(1)}, u32[]{:S(2)}, u32[]{:S(2)}) collective-permute-start(bf16[256,512]{1,0:T(8,128)(2,1)S(1)} %get-tuple-element.41), channel_id=1, source_target_pairs={{0,2},{1,3},{2,0},{3,1},{4,6},{5,7},{6,4},{7,5},{8,10},{9,11},{10,... | collective-permute-start | bytes 786440 | tf_op jit(solution)/shard_map/ppermute | solution.py:206
  70.6 9.2 %collective-permute-start.27 = (bf16[128,512]{1,0:T(8,128)(2,1)S(1)}, bf16[128,512]{1,0:T(8,128)(2,1)S(1)}, u32[]{:S(2)}, u32[]{:S(2)}) collective-permute-start(bf16[128,512]{1,0:T(8,128)(2,1)S(1)} %get-tuple-element.52), channel_id=1, source_target_pairs={{0,8},{1,9},{2,10},{3,11},{4,12},{5,13},{6,14},{7,15},{8,0},{9,1},... | collective-permute-start | bytes 393224 | tf_op jit(solution)/shard_map/ppermute | solution.py:206
  77.8 6.4 %collective-permute-start.28 = (bf16[256,512]{1,0:T(8,128)(2,1)S(1)}, bf16[256,512]{1,0:T(8,128)(2,1)S(1)}, u32[]{:S(2)}, u32[]{:S(2)}) collective-permute-start(bf16[256,512]{1,0:T(8,128)(2,1)S(1)} %add_convert_fusion.1), channel_id=1, source_target_pairs={{0,4},{1,5},{2,6},{3,7},{4,0},{5,1},{6,2},{7,3},{8,12},{9,13},{10,... | collective-permute-start | bytes 786440 | tf_op jit(solution)/shard_map/ppermute | solution.py:206

commit v4 on v3

--- a/solution.py
+++ b/solution.py
@@ -67,63 +67,86 @@
     return call(factors_body, [pl.ANY] * 2, outs, (gate, up), scratch, 1.0)
 
 
-def hidden_body(shards, first, last, soon, *refs):
+def blocks_of(w_down, shards, width, into, sem):
+    places = [pl.multiple_of(shard(*which) * width, width) for which in shards]
+
+    def copies(i):
+        at = pl.ds(pl.multiple_of(i * TILE, TILE), TILE)
+        return [
+            pltpu.make_async_copy(
+                w_down.at[at, pl.ds(place, width)], into.at[at, pl.ds(j * width, width)], sem.at[i, j]
+            )
+            for j, place in enumerate(places)
+        ]
+
+    return copies
+
+
+def each(copies, count, what):
+    def step(i, carry):
+        for copy in copies(i):
+            getattr(copy, what)()
+        return carry
+
+    lax.fori_loop(0, count, step, 0)
+
+
+def hidden_body(shards, given, *refs):
+    first, held, last, soon, fetch = given
     refs, parts = list(refs), len(shards)
-    blocks = [shard(*which) for which in shards]
     pieces, w_down, rest = refs[:parts], refs[parts], refs[parts + 1 :]
-    piece_sem, weight_sem = rest.pop(), rest.pop()
-    held, weights = rest.pop(), rest.pop()
+    before = None if first else rest.pop(0)
+    scale = [rest.pop(0), rest.pop(0)] if last else None
+    del rest[:soon]
+    outs = [rest.pop(0)] + ([rest.pop(0)] if last or fetch else [])
+    acts, piece_sem = rest.pop(0), rest.pop(0)
     width = pieces[0].shape[1]
-    before = None if first else rest.pop(0)
-    if soon:
-        del rest[2 * last : 2 * last + soon]
     count = w_down.shape[0] // TILE
 
-    def arrival(j):
-        return pltpu.make_async_copy(pieces[j], held.at[:, pl.ds(j * width, width)], piece_sem.at[j])
-
-    def weight(i, j):
+    arrivals = [
+        pltpu.make_async_copy(piece, acts.at[:, pl.ds(j * width, width)], piece_sem.at[j])
+        for j, piece in enumerate(pieces)
+    ]
+    for copy in arrivals:
+        copy.start()
+    if held:
+        weights = w_down
+    else:
+        weights, sem = rest.pop(0), rest.pop(0)
+        needed = blocks_of(w_down, shards, width, weights, sem)
+        each(needed, count, "start")
+    if fetch:
+        later = blocks_of(w_down, fetch, width, outs[1], rest.pop(0))
+        each(later, count, "start")
+    for copy in arrivals:
+        copy.wait()
+
+    def step(i, carry):
+        if not held:
+            for copy in needed(i):
+                copy.wait()
         at = pl.ds(pl.multiple_of(i * TILE, TILE), TILE)
-        source = pl.ds(pl.multiple_of(blocks[j] * width, width), width)
-        return pltpu.make_async_copy(
-            w_down.at[at, source], weights.at[at, pl.ds(j * width, width)], weight_sem.at[i, j]
-        )
-
-    def start(i, carry):
-        for j in range(parts):
-            weight(i, j).start()
-        return carry
-
-    for j in range(parts):
-        arrival(j).start()
-    lax.fori_loop(0, count, start, 0)
-    for j in range(parts):
-        arrival(j).wait()
-
-    def step(i, carry):
-        for j in range(parts):
-            weight(i, j).wait()
-        at = pl.ds(pl.multiple_of(i * TILE, TILE), TILE)
-        total = contract_last(held[...], weights[at])
+        total = contract_last(acts[...], weights[at])
         if not first:
             total = total + before[:, at]
         if last:
-            to_gate, to_up, grad_gate, grad_up = rest
-            grad_gate[:, at] = (total * to_gate[:, at]).astype(BF16)
-            grad_up[:, at] = (total * to_up[:, at]).astype(BF16)
+            for out, factor in zip(outs, scale):
+                out[:, at] = (total * factor[:, at]).astype(BF16)
         else:
-            rest[0][:, at] = total
+            outs[0][:, at] = total
         return carry
 
     lax.fori_loop(0, count, step, 0)
-
-
-def hidden(pieces, w_down, total=None, scale=None, soon=()):
+    if fetch:
+        each(later, count, "wait")
+
+
+def hidden(pieces, w_down, total=None, scale=None, soon=(), fetch=(), held=False):
     shards, pieces = zip(*pieces)
     tok, width = pieces[0].shape
     ff = w_down.shape[0]
     parts = len(pieces)
-    ins, args = [pl.ANY] * (parts + 1), (*pieces, w_down)
+    ins, args = [pl.ANY] * parts + [pltpu.VMEM if held else pl.ANY], (*pieces, w_down)
     if total is not None:
         ins, args = ins + [pltpu.VMEM], (*args, total)
     if scale is not None:
@@ -132,14 +155,14 @@
     else:
         outs = [jax.ShapeDtypeStruct((tok, ff), F32)]
     ins, args = ins + [pltpu.VMEM] * len(soon), (*args, *soon)
-    scratch = [
-        pltpu.VMEM((ff, parts * width), BF16),
-        pltpu.VMEM((tok, parts * width), BF16),
-        pltpu.SemaphoreType.DMA((ff // TILE, parts)),
-        pltpu.SemaphoreType.DMA((parts,)),
-    ]
-    body = functools.partial(hidden_body, shards, total is None, scale is not None, len(soon))
-    return call(body, ins, outs, args, scratch, 3.0)
+    scratch = [pltpu.VMEM((tok, parts * width), BF16), pltpu.SemaphoreType.DMA((parts,))]
+    if not held:
+        scratch += [pltpu.VMEM((ff, parts * width), BF16), pltpu.SemaphoreType.DMA((ff // TILE, parts))]
+    if fetch:
+        outs += [pltpu.VMEM((ff, len(fetch) * width), BF16)]
+        scratch += [pltpu.SemaphoreType.DMA((ff // TILE, len(fetch)))]
+    given = (total is None, held, scale is not None, len(soon), tuple(fetch))
+    return call(functools.partial(hidden_body, shards, given), ins, outs, args, scratch, 3.0)
 
 
 def partial_sum(block, width, grad_gate, grad_up, w_gate, w_up):
@@ -220,7 +243,6 @@
     near = after(near, scale[0])
     near_row = move(near, row)
     mid_b = move(after(grad_out[half:], near), mid_)
-    far_a = move(mid_a, near_)
     near_pair = move(near, pair)
     own_both = move(own_row, pair)
     (total,) = hidden(
@@ -230,35 +252,29 @@
     mid_b, near_row = after(mid_b, total, near_row), after(near_row, mid_b)
     mid = jnp.concatenate([mid_a, mid_b])
     mid_row = move(mid, row)
-    far_b = move(mid_b, near_)
+    far = move(mid, near_)
     mid_pair = move(mid, pair)
     near_both = move(near_row, pair)
     (total,) = hidden(
         [((OWN, 1, 1), own_both), ((NEAR, 0, 1), near_pair), ((NEAR, 1, 0), near_row), ((MID, 0, 0), mid)], w_down, total
     )
 
-    far_b = after(far_b, total)
-    far = jnp.concatenate([far_a, far_b])
+    far = after(far, total)
     far_row = move(far, row)
     far_pair = move(far, pair)
     mid_both = move(mid_row, pair)
+    last = [(MID, 1, 1), (FAR, 0, 1), (FAR, 1, 0), (FAR, 1, 1)]
     (total,) = hidden(
-        [
-            ((NEAR, 1, 1), near_both),
-            ((MID, 0, 1), mid_pair),
-            ((MID, 1, 0), mid_row),
-            ((FAR, 0, 0), far),
-            ((MID, 1, 1), mid_both),
-            ((FAR, 0, 1), far_pair),
-        ],
+        [((NEAR, 1, 1), near_both), ((MID, 0, 1), mid_pair), ((MID, 1, 0), mid_row), ((FAR, 0, 0), far)],
         w_down,
         total,
         soon=weights,
+
     )
 
     far_row = after(far_row, total)
     far_both = move(far_row, pair)
-    grads = hidden([((FAR, 1, 0), far_row), ((FAR, 1, 1), far_both)], w_down, total, scale)
+    grads = hidden(list(zip(last, (mid_both, far_pair, far_row, far_both))), w_down, total, scale)
 
     step = functools.partial(sums, grads, weights, width)
     (sent_far,) = step(sent=FAR)

time: 85.2 us -> 82 us (0.962)
  waiting for transfers between devices: 28.1 us -> 25.5 us
  starting transfers between devices: 25.5 us -> 24.6 us
    ppermute x29 -> x28, waiting for transfers between devices: 28.1 us -> 25.5 us  [move(): return lax.ppermute(x, 'wid', [(i, i ^ bits) for i in range(n)])]
    ppermute x29 -> x28, starting transfers between devices: 25.5 us -> 24.6 us  [move(): return lax.ppermute(x, 'wid', [(i, i ^ bits) for i in range(n)])]
  transfers between devices with their start and end apart: 29 -> 28, of which waited for: 11 -> 11; matrix products, arithmetic and copies ran while one was open for 2% -> 2% of each run, Pallas kernels for 29% -> 29%
where the time goes in v4:
time: 82 us; the launch traced here: 81.5 us
  Pallas kernels  28.8 us (35%)
  waiting for transfers between devices  25.5 us (31%)
  starting transfers between devices  24.6 us (30%)
  other arithmetic  1.13 us (1%)
  local copies, waits for them, and re-layouts  1.08 us (1%)
    pallas_call x11, Pallas kernels, call(): pl.pallas_call(body, in_specs=[pl.BlockSpec(memory_space=space) for space...  28.8 us
    ppermute x28, waiting for transfers between devices, move(): return lax.ppermute(x, 'wid', [(i, i ^ bits) for i in range(n)])  25.5 us
    ppermute x28, starting transfers between devices, move(): return lax.ppermute(x, 'wid', [(i, i ^ bits) for i in range(n)])  24.6 us
  transfers between devices with their start and end apart: 28, of which 11 were waited for; matrix products, arithmetic and copies ran while one was open for 2% of the time, Pallas kernels for 29%

profile of v4, /device:TPU:0, one launch (start us, length us, event | category | flops | bytes accessed | tf_op | source)
XLA Modules:
  0.0 81.5 jit_solution(3905832577081122464)
XLA Ops:
  0.0 3.0 %collective-permute-start.1 = (bf16[256,512]{1,0:T(8,128)(2,1)}, bf16[256,512]{1,0:T(8,128)(2,1)S(1)}, u32[]{:S(2)}, u32[]{:S(2)}) collective-permute-start(bf16[256,512]{1,0:T(8,128)(2,1)} %refs_0_.1), channel_id=1, source_target_pairs={{0,4},{1,5},{2,6},{3,7},{4,0},{5,1},{6,2},{7,3},{8,12},{9,13},{10,... | collective-permute-start | bytes 786440 | tf_op jit(solution)/shard_map/ppermute | solution.py:229
  3.0 1.5 %collective-permute-start.4 = (bf16[256,512]{1,0:T(8,128)(2,1)}, bf16[256,512]{1,0:T(8,128)(2,1)S(1)}, u32[]{:S(2)}, u32[]{:S(2)}) collective-permute-start(bf16[256,512]{1,0:T(8,128)(2,1)} %refs_0_.1), channel_id=1, source_target_pairs={{0,2},{1,3},{2,0},{3,1},{4,6},{5,7},{6,4},{7,5},{8,10},{9,11},{10,... | collective-permute-start | bytes 786440 | tf_op jit(solution)/shard_map/ppermute | solution.py:229
  4.5 0.0 collective-permute-start.3
  4.5 1.0 %fusion.1 = (bf16[128,512]{1,0:T(8,128)(2,1)S(1)}, bf16[128,512]{1,0:T(8,128)(2,1)S(1)}) fusion(bf16[256,512]{1,0:T(8,128)(2,1)} %refs_0_.1), kind=kLoop, calls=%fused_computation.8 | loop fusion | bytes 524288 | tf_op jit(solution)/shard_map/slice | solution.py:245
  5.5 2.7 %collective-permute-start = (bf16[128,512]{1,0:T(8,128)(2,1)S(1)}, bf16[128,512]{1,0:T(8,128)(2,1)S(1)}, u32[]{:S(2)}, u32[]{:S(2)}) collective-permute-start(bf16[128,512]{1,0:T(8,128)(2,1)S(1)} %get-tuple-element.54), channel_id=1, source_target_pairs={{0,8},{1,9},{2,10},{3,11},{4,12},{5,13},{6,14},{7,15},{8,0},{9,1},... | collective-permute-start | bytes 393224 | tf_op jit(solution)/shard_map/ppermute | solution.py:229
  8.2 1.8 %shard_map.64 = (f32[256,1024]{1,0:T(8,128)S(1)}, f32[256,1024]{1,0:T(8,128)S(1)}) custom-call(bf16[256,1024]{1,0:T(8,128)(2,1)} %gate.1, bf16[256,1024]{1,0:T(8,128)(2,1)} %up.1), custom_call_target="tpu_custom_call" | custom-call | flops 200000000 | tf_op jit(solution)/shard_map/pallas_call | solution.py:30
  10.0 4.0 %collective-permute-start.5 = (bf16[256,512]{1,0:T(8,128)(2,1)S(1)}, bf16[256,512]{1,0:T(8,128)(2,1)S(1)}, u32[]{:S(2)}, u32[]{:S(2)}) collective-permute-start(bf16[256,512]{1,0:T(8,128)(2,1)S(1)} %collective-permute-done.1.refs_3_), channel_id=1, source_target_pairs={{0,2},{1,3},{2,0},{3,1},{4,6},{5,7},{6,4},{7,5},{8,10},{9,11},{10,... | collective-permute-start | bytes 786440 | tf_op jit(solution)/shard_map/ppermute | solution.py:229
  14.0 1.0 %collective-permute-start.2 = (bf16[128,512]{1,0:T(8,128)(2,1)S(1)}, bf16[128,512]{1,0:T(8,128)(2,1)S(1)}, u32[]{:S(2)}, u32[]{:S(2)}) collective-permute-start(bf16[128,512]{1,0:T(8,128)(2,1)S(1)} %get-tuple-element.30), channel_id=1, source_target_pairs={{0,8},{1,9},{2,10},{3,11},{4,12},{5,13},{6,14},{7,15},{8,0},{9,1},... | collective-permute-start | bytes 393224 | tf_op jit(solution)/shard_map/ppermute | solution.py:229
  15.1 0.5 collective-permute-done
  15.6 0.0 slice-start
  15.6 0.0 slice-start.1
  15.6 0.0 copy-start
  15.7 0.1 collective-permute-start.10
  15.7 0.0 collective-permute-done.4.refs_2_
  15.7 0.5 collective-permute-start.9
  16.2 0.0 collective-permute-done.3.refs_1_
  16.2 3.7 %shard_map.65.refs_5_ = f32[256,1024]{1,0:T(8,128)S(1)} custom-call(bf16[256,512]{1,0:T(8,128)(2,1)} %refs_0_.1, bf16[256,512]{1,0:T(8,128)(2,1)S(1)} %collective-permute-done.3.refs_1_, bf16[256,512]{1,0:T(8,128)(2,1)S(1)} %collective-permute-done.4.refs_2_, bf16[256,512]{1,0:T(8,128)(2,1)S(1)} %collective-permute-done.1.refs_3_, bf16[1024,8192]{1,0:T(8,128)(2,1)} %refs_4_.7), custom_call_target="tpu_custom_call" | custom-call | flops 600000000 | tf_op jit(solution)/shard_map/pallas_call | solution.py:30
  19.9 1.3 %collective-permute-done.2 = bf16[128,512]{1,0:T(8,128)(2,1)S(1)} collective-permute-done((bf16[128,512]{1,0:T(8,128)(2,1)S(1)}, bf16[128,512]{1,0:T(8,128)(2,1)S(1)}, u32[]{:S(2)}, u32[]{:S(2)}) %collective-permute-start.2) | collective-permute-done | bytes 131104 | tf_op jit(solution)/shard_map/ppermute | solution.py:229
  21.3 0.0 slice-start.2
  21.3 0.0 slice-start.3
  21.3 0.6 collective-permute-start.8
  21.9 0.0 collective-permute-start.6
  21.9 0.3 collective-permute-start.14
  22.2 0.0 collective-permute-done.10.refs_1_
  22.2 0.2 collective-permute-start.13
  22.4 4.2 %shard_map.66.refs_5_ = f32[256,1024]{1,0:T(8,128)S(1)} custom-call(bf16[256,512]{1,0:T(8,128)(2,1)S(1)} %collective-permute-done.9.refs_0_, bf16[256,512]{1,0:T(8,128)(2,1)S(1)} %collective-permute-done.10.refs_1_, bf16[256,512]{1,0:T(8,128)(2,1)S(1)} %collective-permute-done.5.refs_2_, bf16[256,512]{1,0:T(8,128)(2,1)S(1)} %constant_dynamic-update-slice_fusion.refs_3_, ...), custom_call_target="tpu_custom_call" | custom-call | flops 600000000 | tf_op jit(solution)/shard_map/pallas_call | solution.py:30
  26.6 2.3 %collective-permute-done.8.refs_3_ = bf16[256,512]{1,0:T(8,128)(2,1)S(1)} collective-permute-done((bf16[256,512]{1,0:T(8,128)(2,1)S(1)}, bf16[256,512]{1,0:T(8,128)(2,1)S(1)}, u32[]{:S(2)}, u32[]{:S(2)}) %collective-permute-start.8) | collective-permute-done | bytes 262176 | tf_op jit(solution)/shard_map/ppermute | solution.py:229
  28.9 0.2 collective-permute-start.12
  29.1 1.3 %collective-permute-done.6.refs_2_ = bf16[256,512]{1,0:T(8,128)(2,1)S(1)} collective-permute-done((bf16[256,512]{1,0:T(8,128)(2,1)S(1)}, bf16[256,512]{1,0:T(8,128)(2,1)S(1)}, u32[]{:S(2)}, u32[]{:S(2)}) %collective-permute-start.6) | collective-permute-done | bytes 262176 | tf_op jit(solution)/shard_map/ppermute | solution.py:229
  30.4 0.0 slice-start.4
  30.5 0.0 slice-start.5
  30.5 0.0 slice-start.6
  30.5 3.5 %shard_map.67.refs_5_ = f32[256,1024]{1,0:T(8,128)S(1)} custom-call(bf16[256,512]{1,0:T(8,128)(2,1)S(1)} %collective-permute-done.13.refs_0_, bf16[256,512]{1,0:T(8,128)(2,1)S(1)} %collective-permute-done.14.refs_1_, bf16[256,512]{1,0:T(8,128)(2,1)S(1)} %collective-permute-done.6.refs_2_, bf16[256,512]{1,0:T(8,128)(2,1)S(1)} %collective-permute-done.8.refs_3_, ...), custom_call_target="tpu_custom_call" | custom-call | flops 600000000 | tf_op jit(solution)/shard_map/pallas_call | solution.py:30
  34.0 2.1 %collective-permute-done.12.refs_2_ = bf16[256,512]{1,0:T(8,128)(2,1)S(1)} collective-permute-done((bf16[256,512]{1,0:T(8,128)(2,1)S(1)}, bf16[256,512]{1,0:T(8,128)(2,1)S(1)}, u32[]{:S(2)}, u32[]{:S(2)}) %collective-permute-start.12) | collective-permute-done | bytes 262176 | tf_op jit(solution)/shard_map/ppermute | solution.py:229
  36.2 1.5 %collective-permute-done.15.refs_3_ = bf16[256,512]{1,0:T(8,128)(2,1)S(1)} collective-permute-done((bf16[256,512]{1,0:T(8,128)(2,1)S(1)}, bf16[256,512]{1,0:T(8,128)(2,1)S(1)}, u32[]{:S(2)}, u32[]{:S(2)}) %collective-permute-start.15) | collective-permute-done | bytes 262176 | tf_op jit(solution)/shard_map/ppermute | solution.py:229
  37.7 3.5 %shard_map.68 = (bf16[256,1024]{1,0:T(8,128)(2,1)S(1)}, bf16[256,1024]{1,0:T(8,128)(2,1)S(1)}) custom-call(bf16[256,512]{1,0:T(8,128)(2,1)S(1)} %collective-permute-done.7.refs_0_, bf16[256,512]{1,0:T(8,128)(2,1)S(1)} %collective-permute-done.11.refs_1_, bf16[256,512]{1,0:T(8,128)(2,1)S(1)} %collective-permute-done.12.refs_2_, ...), custom_call_target="tpu_custom_call" | custom-call | flops 600000000 | tf_op jit(solution)/shard_map/pallas_call | solution.py:30
  41.3 1.5 %shard_map.73 = bf16[256,1024]{1,0:T(8,128)(2,1)S(1)} custom-call(bf16[256,1024]{1,0:T(8,128)(2,1)S(1)} %get-tuple-element.36.grad_gate, bf16[256,1024]{1,0:T(8,128)(2,1)S(1)} %get-tuple-element.37.grad_up, bf16[8192,1024]{1,0:T(8,128)(2,1)S(1)} %bitcast.1, bf16[8192,1024]{1,0:T(8,128)(2,1)S(1)} %bitcast.3), custom_call_target="tpu_custom_call" | custom-call | flops 150000000 | tf_op jit(solution)/shard_map/pallas_call | solution.py:30
  42.8 0.2 collective-permute-start.21
  43.0 1.5 %shard_map.69 = bf16[256,1024]{1,0:T(8,128)(2,1)S(1)} custom-call(bf16[256,1024]{1,0:T(8,128)(2,1)S(1)} %get-tuple-element.36.grad_gate, bf16[256,1024]{1,0:T(8,128)(2,1)S(1)} %get-tuple-element.37.grad_up, bf16[8192,1024]{1,0:T(8,128)(2,1)S(1)} %bitcast.1, bf16[8192,1024]{1,0:T(8,128)(2,1)S(1)} %bitcast.3), custom_call_target="tpu_custom_call" | custom-call | flops 150000000 | tf_op jit(solution)/shard_map/pallas_call | solution.py:30
  44.5 0.4 collective-permute-start.16
  44.9 1.6 %shard_map.74 = (f32[256,512]{1,0:T(8,128)S(1)}, bf16[256,512]{1,0:T(8,128)(2,1)S(1)}) custom-call(bf16[256,1024]{1,0:T(8,128)(2,1)S(1)} %get-tuple-element.36.grad_gate, bf16[256,1024]{1,0:T(8,128)(2,1)S(1)} %get-tuple-element.37.grad_up, bf16[8192,1024]{1,0:T(8,128)(2,1)S(1)} %bitcast.1, bf16[8192,1024]{1,0:T(8,128)(2,1)S(1)} %bitcast.3, ...), custom_call_target="tpu_custom_call" | custom-call | flops 300000000 | tf_op jit(solution)/shard_map/pallas_call | solution.py:30
  46.5 0.3 collective-permute-start.22
  46.8 3.0 %shard_map.70 = (f32[256,512]{1,0:T(8,128)S(1)}, bf16[256,512]{1,0:T(8,128)(2,1)S(1)}, bf16[256,1024]{1,0:T(8,128)(2,1)S(1)}) custom-call(bf16[256,1024]{1,0:T(8,128)(2,1)S(1)} %get-tuple-element.36.grad_gate, bf16[256,1024]{1,0:T(8,128)(2,1)S(1)} %get-tuple-element.37.grad_up, bf16[8192,1024]{1,0:T(8,128)(2,1)S(1)} %bitcast.1, ...), custom_call_target="tpu_custom_call" | custom-call | flops 450000000 | tf_op jit(solution)/shard_map/pallas_call | solution.py:30
  49.9 0.1 collective-permute-start.17
  49.9 1.8 %collective-permute-start.20 = (bf16[256,512]{1,0:T(8,128)(2,1)S(1)}, bf16[256,512]{1,0:T(8,128)(2,1)S(1)}, u32[]{:S(2)}, u32[]{:S(2)}) collective-permute-start(bf16[256,512]{1,0:T(8,128)(2,1)S(1)} %get-tuple-element.43), channel_id=1, source_target_pairs={{0,2},{1,3},{2,0},{3,1},{4,6},{5,7},{6,4},{7,5},{8,10},{9,11},{10,... | collective-permute-start | bytes 786440 | tf_op jit(solution)/shard_map/ppermute | solution.py:229
  51.8 3.9 %collective-permute-done.22 = bf16[256,512]{1,0:T(8,128)(2,1)S(1)} collective-permute-done((bf16[256,512]{1,0:T(8,128)(2,1)S(1)}, bf16[256,512]{1,0:T(8,128)(2,1)S(1)}, u32[]{:S(2)}, u32[]{:S(2)}) %collective-permute-start.22) | collective-permute-done | bytes 262176 | tf_op jit(solution)/shard_map/ppermute | solution.py:229
  55.7 0.1 add_convert_fusion.3
  55.8 2.5 %collective-permute-start.23 = (bf16[256,512]{1,0:T(8,128)(2,1)S(1)}, bf16[256,512]{1,0:T(8,128)(2,1)S(1)}, u32[]{:S(2)}, u32[]{:S(2)}) collective-permute-start(bf16[256,512]{1,0:T(8,128)(2,1)S(1)} %add_convert_fusion.3), channel_id=1, source_target_pairs={{0,4},{1,5},{2,6},{3,7},{4,0},{5,1},{6,2},{7,3},{8,12},{9,13},{10,... | collective-permute-start | bytes 786440 | tf_op jit(solution)/shard_map/ppermute | solution.py:229
  58.3 3.0 %shard_map.71 = (f32[256,512]{1,0:T(8,128)S(1)}, bf16[256,512]{1,0:T(8,128)(2,1)S(1)}, bf16[256,1024]{1,0:T(8,128)(2,1)S(1)}) custom-call(bf16[256,1024]{1,0:T(8,128)(2,1)S(1)} %get-tuple-element.36.grad_gate, bf16[256,1024]{1,0:T(8,128)(2,1)S(1)} %get-tuple-element.37.grad_up, bf16[8192,1024]{1,0:T(8,128)(2,1)S(1)} %bitcast.1, ...), custom_call_target="tpu_custom_call" | custom-call | flops 450000000 | tf_op jit(solution)/shard_map/pallas_call | solution.py:30
  61.4 0.1 collective-permute-start.25
  61.4 0.1 collective-permute-start.18
  61.5 1.8 %collective-permute-done.23 = bf16[256,512]{1,0:T(8,128)(2,1)S(1)} collective-permute-done((bf16[256,512]{1,0:T(8,128)(2,1)S(1)}, bf16[256,512]{1,0:T(8,128)(2,1)S(1)}, u32[]{:S(2)}, u32[]{:S(2)}) %collective-permute-start.23) | collective-permute-done | bytes 262176 | tf_op jit(solution)/shard_map/ppermute | solution.py:229
  63.3 0.1 add_convert_fusion.2
  63.4 1.4 %collective-permute-start.24 = (bf16[128,512]{1,0:T(8,128)(2,1)S(1)}, bf16[128,512]{1,0:T(8,128)(2,1)S(1)}, u32[]{:S(2)}, u32[]{:S(2)}) collective-permute-start(bf16[128,512]{1,0:T(8,128)(2,1)S(1)} %get-tuple-element.51), channel_id=1, source_target_pairs={{0,8},{1,9},{2,10},{3,11},{4,12},{5,13},{6,14},{7,15},{8,0},{9,1},... | collective-permute-start | bytes 393224 | tf_op jit(solution)/shard_map/ppermute | solution.py:229
  64.8 1.6 %shard_map.72 = (f32[256,512]{1,0:T(8,128)S(1)}, bf16[256,512]{1,0:T(8,128)(2,1)S(1)}) custom-call(bf16[256,1024]{1,0:T(8,128)(2,1)S(1)} %get-tuple-element.36.grad_gate, bf16[256,1024]{1,0:T(8,128)(2,1)S(1)} %get-tuple-element.37.grad_up, bf16[8192,1024]{1,0:T(8,128)(2,1)S(1)} %bitcast.1, bf16[8192,1024]{1,0:T(8,128)(2,1)S(1)} %bitcast.3, ...), custom_call_target="tpu_custom_call" | custom-call | flops 300000000 | tf_op jit(solution)/shard_map/pallas_call | solution.py:30
  66.3 1.8 %collective-permute-start.19 = (bf16[256,512]{1,0:T(8,128)(2,1)S(1)}, bf16[256,512]{1,0:T(8,128)(2,1)S(1)}, u32[]{:S(2)}, u32[]{:S(2)}) collective-permute-start(bf16[256,512]{1,0:T(8,128)(2,1)S(1)} %get-tuple-element.41), channel_id=1, source_target_pairs={{0,2},{1,3},{2,0},{3,1},{4,6},{5,7},{6,4},{7,5},{8,10},{9,11},{10,... | collective-permute-start | bytes 786440 | tf_op jit(solution)/shard_map/ppermute | solution.py:229
  68.2 0.2 collective-permute-start.26
  68.4 5.3 %collective-permute-done.24 = bf16[128,512]{1,0:T(8,128)(2,1)S(1)} collective-permute-done((bf16[128,512]{1,0:T(8,128)(2,1)S(1)}, bf16[128,512]{1,0:T(8,128)(2,1)S(1)}, u32[]{:S(2)}, u32[]{:S(2)}) %collective-permute-start.24) | collective-permute-done | bytes 131104 | tf_op jit(solution)/shard_map/ppermute | solution.py:229
  73.7 0.1 add_convert_fusion.1
  73.8 1.5 %collective-permute-start.27 = (bf16[256,512]{1,0:T(8,128)(2,1)S(1)}, bf16[256,512]{1,0:T(8,128)(2,1)S(1)}, u32[]{:S(2)}, u32[]{:S(2)}) collective-permute-start(bf16[256,512]{1,0:T(8,128)(2,1)S(1)} %add_convert_fusion.1), channel_id=1, source_target_pairs={{0,4},{1,5},{2,6},{3,7},{4,0},{5,1},{6,2},{7,3},{8,12},{9,13},{10,... | collective-permute-start | bytes 786440 | tf_op jit(solution)/shard_map/ppermute | solution.py:229
  75.3 1.9 %collective-permute-done.26 = bf16[128,512]{1,0:T(8,128)(2,1)S(1)} collective-permute-done((bf16[128,512]{1,0:T(8,128)(2,1)S(1)}, bf16[128,512]{1,0:T(8,128)(2,1)S(1)}, u32[]{:S(2)}, u32[]{:S(2)}) %collective-permute-start.26) | collective-permute-done | bytes 131104 | tf_op jit(solution)/shard_map/ppermute | solution.py:229
  77.2 0.1 convert_add_fusion
  77.3 3.4 %collective-permute-done.27 = bf16[256,512]{1,0:T(8,128)(2,1)S(1)} collective-permute-done((bf16[256,512]{1,0:T(8,128)(2,1)S(1)}, bf16[256,512]{1,0:T(8,128)(2,1)S(1)}, u32[]{:S(2)}, u32[]{:S(2)}) %collective-permute-start.27) | collective-permute-done | bytes 262176 | tf_op jit(solution)/shard_map/ppermute | solution.py:229
  80.7 0.8 add_convert_fusion
  (32 shorter events, 0.1 us)
Async XLA Ops:
  0.0 10.0 %collective-permute-start.1 = (bf16[256,512]{1,0:T(8,128)(2,1)}, bf16[256,512]{1,0:T(8,128)(2,1)S(1)}, u32[]{:S(2)}, u32[]{:S(2)}) collective-permute-start(bf16[256,512]{1,0:T(8,128)(2,1)} %refs_0_.1), channel_id=1, source_target_pairs={{0,4},{1,5},{2,6},{3,7},{4,0},{5,1},{6,2},{7,3},{8,12},{9,13},{10,... | collective-permute-start | bytes 786440 | tf_op jit(solution)/shard_map/ppermute | solution.py:229
  3.0 12.7 %collective-permute-start.4 = (bf16[256,512]{1,0:T(8,128)(2,1)}, bf16[256,512]{1,0:T(8,128)(2,1)S(1)}, u32[]{:S(2)}, u32[]{:S(2)}) collective-permute-start(bf16[256,512]{1,0:T(8,128)(2,1)} %refs_0_.1), channel_id=1, source_target_pairs={{0,2},{1,3},{2,0},{3,1},{4,6},{5,7},{6,4},{7,5},{8,10},{9,11},{10,... | collective-permute-start | bytes 786440 | tf_op jit(solution)/shard_map/ppermute | solution.py:229
  4.5 11.7 %collective-permute-start.3 = (bf16[256,512]{1,0:T(8,128)(2,1)}, bf16[256,512]{1,0:T(8,128)(2,1)S(1)}, u32[]{:S(2)}, u32[]{:S(2)}) collective-permute-start(bf16[256,512]{1,0:T(8,128)(2,1)} %refs_0_.1), channel_id=1, source_target_pairs={{0,1},{1,0},{2,3},{3,2},{4,5},{5,4},{6,7},{7,6},{8,9},{9,8},{10,11... | collective-permute-start | bytes 786440 | tf_op jit(solution)/shard_map/ppermute | solution.py:229
  5.5 10.1 %collective-permute-start = (bf16[128,512]{1,0:T(8,128)(2,1)S(1)}, bf16[128,512]{1,0:T(8,128)(2,1)S(1)}, u32[]{:S(2)}, u32[]{:S(2)}) collective-permute-start(bf16[128,512]{1,0:T(8,128)(2,1)S(1)} %get-tuple-element.54), channel_id=1, source_target_pairs={{0,8},{1,9},{2,10},{3,11},{4,12},{5,13},{6,14},{7,15},{8,0},{9,1},... | collective-permute-start | bytes 393224 | tf_op jit(solution)/shard_map/ppermute | solution.py:229
  10.0 11.3 %collective-permute-start.5 = (bf16[256,512]{1,0:T(8,128)(2,1)S(1)}, bf16[256,512]{1,0:T(8,128)(2,1)S(1)}, u32[]{:S(2)}, u32[]{:S(2)}) collective-permute-start(bf16[256,512]{1,0:T(8,128)(2,1)S(1)} %collective-permute-done.1.refs_3_), channel_id=1, source_target_pairs={{0,2},{1,3},{2,0},{3,1},{4,6},{5,7},{6,4},{7,5},{8,10},{9,11},{10,... | collective-permute-start | bytes 786440 | tf_op jit(solution)/shard_map/ppermute | solution.py:229
  14.0 7.2 %collective-permute-start.2 = (bf16[128,512]{1,0:T(8,128)(2,1)S(1)}, bf16[128,512]{1,0:T(8,128)(2,1)S(1)}, u32[]{:S(2)}, u32[]{:S(2)}) collective-permute-start(bf16[128,512]{1,0:T(8,128)(2,1)S(1)} %get-tuple-element.30), channel_id=1, source_target_pairs={{0,8},{1,9},{2,10},{3,11},{4,12},{5,13},{6,14},{7,15},{8,0},{9,1},... | collective-permute-start | bytes 393224 | tf_op jit(solution)/shard_map/ppermute | solution.py:229
  15.6 14.8 %slice-start = ((s8[16777216]{0:T(1024)(128)(4,1)}), s8[4194304]{0:T(1024)(128)(4,1)S(1)}, s32[]{:S(2)}) async-start(s8[16777216]{0:T(1024)(128)(4,1)} %bitcast), calls=%async_computation | async-start | bytes 8388608
  15.6 14.8 %slice-start.1 = ((s8[16777216]{0:T(1024)(128)(4,1)}), s8[4194304]{0:T(1024)(128)(4,1)S(1)}, s32[]{:S(2)}) async-start(s8[16777216]{0:T(1024)(128)(4,1)} %bitcast), calls=%async_computation.1 | async-start | bytes 8388608
  15.6 14.8 %copy-start = (bf16[8192,1024]{1,0:T(8,128)(2,1)S(1)}, bf16[8192,1024]{1,0:T(8,128)(2,1)}, u32[]{:S(2)}) copy-start(bf16[8192,1024]{1,0:T(8,128)(2,1)} %w_up.11) | copy-start | bytes 50331652
  15.7 6.5 %collective-permute-start.10 = (bf16[256,512]{1,0:T(8,128)(2,1)S(1)}, bf16[256,512]{1,0:T(8,128)(2,1)S(1)}, u32[]{:S(2)}, u32[]{:S(2)}) collective-permute-start(bf16[256,512]{1,0:T(8,128)(2,1)S(1)} %collective-permute-done.1.refs_3_), channel_id=1, source_target_pairs={{0,1},{1,0},{2,3},{3,2},{4,5},{5,4},{6,7},{7,6},{8,9},{9,8},{10,11... | collective-permute-start | bytes 786440 | tf_op jit(solution)/shard_map/ppermute | solution.py:229
  15.7 6.7 %collective-permute-start.9 = (bf16[256,512]{1,0:T(8,128)(2,1)S(1)}, bf16[256,512]{1,0:T(8,128)(2,1)S(1)}, u32[]{:S(2)}, u32[]{:S(2)}) collective-permute-start(bf16[256,512]{1,0:T(8,128)(2,1)S(1)} %collective-permute-done.4.refs_2_), channel_id=1, source_target_pairs={{0,1},{1,0},{2,3},{3,2},{4,5},{5,4},{6,7},{7,6},{8,9},{9,8},{10,11... | collective-permute-start | bytes 786440 | tf_op jit(solution)/shard_map/ppermute | solution.py:229
  21.3 9.2 %slice-start.2 = ((s8[16777216]{0:T(1024)(128)(4,1)}), s8[4194304]{0:T(1024)(128)(4,1)S(1)}, s32[]{:S(2)}) async-start(s8[16777216]{0:T(1024)(128)(4,1)} %bitcast), calls=%async_computation.2 | async-start | bytes 8388608
  21.3 9.2 %slice-start.3 = ((s8[16777216]{0:T(1024)(128)(4,1)}), s8[4194304]{0:T(1024)(128)(4,1)S(1)}, s32[]{:S(2)}) async-start(s8[16777216]{0:T(1024)(128)(4,1)} %bitcast), calls=%async_computation.3 | async-start | bytes 8388608
  21.3 7.6 %collective-permute-start.8 = (bf16[256,512]{1,0:T(8,128)(2,1)S(1)}, bf16[256,512]{1,0:T(8,128)(2,1)S(1)}, u32[]{:S(2)}, u32[]{:S(2)}) collective-permute-start(bf16[256,512]{1,0:T(8,128)(2,1)S(1)} %constant_dynamic-update-slice_fusion.refs_3_), channel_id=1, source_target_pairs={{0,4},{1,5},{2,6},{3,7},{4,0},{5,1},{6,2},{7,3},{8,12},{9,13},{10,... | collective-permute-start | bytes 786440 | tf_op jit(solution)/shard_map/ppermute | solution.py:229
  21.9 8.5 %collective-permute-start.6 = (bf16[256,512]{1,0:T(8,128)(2,1)S(1)}, bf16[256,512]{1,0:T(8,128)(2,1)S(1)}, u32[]{:S(2)}, u32[]{:S(2)}) collective-permute-start(bf16[256,512]{1,0:T(8,128)(2,1)S(1)} %constant_dynamic-update-slice_fusion.refs_3_), channel_id=1, source_target_pairs={{0,2},{1,3},{2,0},{3,1},{4,6},{5,7},{6,4},{7,5},{8,10},{9,11},{10,... | collective-permute-start | bytes 786440 | tf_op jit(solution)/shard_map/ppermute | solution.py:229
  21.9 8.5 %collective-permute-start.14 = (bf16[256,512]{1,0:T(8,128)(2,1)S(1)}, bf16[256,512]{1,0:T(8,128)(2,1)S(1)}, u32[]{:S(2)}, u32[]{:S(2)}) collective-permute-start(bf16[256,512]{1,0:T(8,128)(2,1)S(1)} %constant_dynamic-update-slice_fusion.refs_3_), channel_id=1, source_target_pairs={{0,1},{1,0},{2,3},{3,2},{4,5},{5,4},{6,7},{7,6},{8,9},{9,8},{10,11... | collective-permute-start | bytes 786440 | tf_op jit(solution)/shard_map/ppermute | solution.py:229
  22.2 8.2 %collective-permute-start.13 = (bf16[256,512]{1,0:T(8,128)(2,1)S(1)}, bf16[256,512]{1,0:T(8,128)(2,1)S(1)}, u32[]{:S(2)}, u32[]{:S(2)}) collective-permute-start(bf16[256,512]{1,0:T(8,128)(2,1)S(1)} %collective-permute-done.5.refs_2_), channel_id=1, source_target_pairs={{0,1},{1,0},{2,3},{3,2},{4,5},{5,4},{6,7},{7,6},{8,9},{9,8},{10,11... | collective-permute-start | bytes 786440 | tf_op jit(solution)/shard_map/ppermute | solution.py:229
  28.9 7.2 %collective-permute-start.12 = (bf16[256,512]{1,0:T(8,128)(2,1)S(1)}, bf16[256,512]{1,0:T(8,128)(2,1)S(1)}, u32[]{:S(2)}, u32[]{:S(2)}) collective-permute-start(bf16[256,512]{1,0:T(8,128)(2,1)S(1)} %collective-permute-done.8.refs_3_), channel_id=1, source_target_pairs={{0,2},{1,3},{2,0},{3,1},{4,6},{5,7},{6,4},{7,5},{8,10},{9,11},{10,... | collective-permute-start | bytes 786440 | tf_op jit(solution)/shard_map/ppermute | solution.py:229
  29.1 7.1 %collective-permute-start.11 = (bf16[256,512]{1,0:T(8,128)(2,1)S(1)}, bf16[256,512]{1,0:T(8,128)(2,1)S(1)}, u32[]{:S(2)}, u32[]{:S(2)}) collective-permute-start(bf16[256,512]{1,0:T(8,128)(2,1)S(1)} %collective-permute-done.8.refs_3_), channel_id=1, source_target_pairs={{0,1},{1,0},{2,3},{3,2},{4,5},{5,4},{6,7},{7,6},{8,9},{9,8},{10,11... | collective-permute-start | bytes 786440 | tf_op jit(solution)/shard_map/ppermute | solution.py:229
  30.4 5.8 %collective-permute-start.7 = (bf16[256,512]{1,0:T(8,128)(2,1)S(1)}, bf16[256,512]{1,0:T(8,128)(2,1)S(1)}, u32[]{:S(2)}, u32[]{:S(2)}) collective-permute-start(bf16[256,512]{1,0:T(8,128)(2,1)S(1)} %collective-permute-done.6.refs_2_), channel_id=1, source_target_pairs={{0,1},{1,0},{2,3},{3,2},{4,5},{5,4},{6,7},{7,6},{8,9},{9,8},{10,11... | collective-permute-start | bytes 786440 | tf_op jit(solution)/shard_map/ppermute | solution.py:229
  30.4 10.8 %slice-start.4 = ((s8[16777216]{0:T(1024)(128)(4,1)}), s8[4194304]{0:T(1024)(128)(4,1)S(1)}, s32[]{:S(2)}) async-start(s8[16777216]{0:T(1024)(128)(4,1)} %bitcast.2), calls=%async_computation.4 | async-start | bytes 8388608
  30.5 10.8 %slice-start.5 = ((s8[16777216]{0:T(1024)(128)(4,1)}), s8[4194304]{0:T(1024)(128)(4,1)S(1)}, s32[]{:S(2)}) async-start(s8[16777216]{0:T(1024)(128)(4,1)} %bitcast.2), calls=%async_computation.5 | async-start | bytes 8388608
  30.5 10.8 %slice-start.6 = ((s8[16777216]{0:T(1024)(128)(4,1)}), s8[4194304]{0:T(1024)(128)(4,1)S(1)}, s32[]{:S(2)}) async-start(s8[16777216]{0:T(1024)(128)(4,1)} %bitcast.2), calls=%async_computation.6 | async-start | bytes 8388608
  36.2 1.5 %collective-permute-start.15 = (bf16[256,512]{1,0:T(8,128)(2,1)S(1)}, bf16[256,512]{1,0:T(8,128)(2,1)S(1)}, u32[]{:S(2)}, u32[]{:S(2)}) collective-permute-start(bf16[256,512]{1,0:T(8,128)(2,1)S(1)} %collective-permute-done.12.refs_2_), channel_id=1, source_target_pairs={{0,1},{1,0},{2,3},{3,2},{4,5},{5,4},{6,7},{7,6},{8,9},{9,8},{10,11... | collective-permute-start | bytes 786440 | tf_op jit(solution)/shard_map/ppermute | solution.py:229
  37.7 3.6 %slice-start.7 = ((s8[16777216]{0:T(1024)(128)(4,1)}), s8[4194304]{0:T(1024)(128)(4,1)S(1)}, s32[]{:S(2)}) async-start(s8[16777216]{0:T(1024)(128)(4,1)} %bitcast.2), calls=%async_computation.7 | async-start | bytes 8388608
  42.8 2.1 %collective-permute-start.21 = (bf16[256,1024]{1,0:T(8,128)(2,1)S(1)}, bf16[256,1024]{1,0:T(8,128)(2,1)S(1)}, u32[]{:S(2)}, u32[]{:S(2)}) collective-permute-start(bf16[256,1024]{1,0:T(8,128)(2,1)S(1)} %shard_map.73), channel_id=1, source_target_pairs={{0,1},{1,0},{2,3},{3,2},{4,5},{5,4},{6,7},{7,6},{8,9},{9,8},{10,11... | collective-permute-start | bytes 1572872 | tf_op jit(solution)/shard_map/ppermute | solution.py:229
  44.5 2.4 %collective-permute-start.16 = (bf16[256,1024]{1,0:T(8,128)(2,1)S(1)}, bf16[256,1024]{1,0:T(8,128)(2,1)S(1)}, u32[]{:S(2)}, u32[]{:S(2)}) collective-permute-start(bf16[256,1024]{1,0:T(8,128)(2,1)S(1)} %shard_map.69), channel_id=1, source_target_pairs={{0,1},{1,0},{2,3},{3,2},{4,5},{5,4},{6,7},{7,6},{8,9},{9,8},{10,11... | collective-permute-start | bytes 1572872 | tf_op jit(solution)/shard_map/ppermute | solution.py:229
  46.5 9.2 %collective-permute-start.22 = (bf16[256,512]{1,0:T(8,128)(2,1)S(1)}, bf16[256,512]{1,0:T(8,128)(2,1)S(1)}, u32[]{:S(2)}, u32[]{:S(2)}) collective-permute-start(bf16[256,512]{1,0:T(8,128)(2,1)S(1)} %get-tuple-element.47), channel_id=1, source_target_pairs={{0,2},{1,3},{2,0},{3,1},{4,6},{5,7},{6,4},{7,5},{8,10},{9,11},{10,... | collective-permute-start | bytes 786440 | tf_op jit(solution)/shard_map/ppermute | solution.py:229
  49.9 8.4 %collective-permute-start.17 = (bf16[256,1024]{1,0:T(8,128)(2,1)S(1)}, bf16[256,1024]{1,0:T(8,128)(2,1)S(1)}, u32[]{:S(2)}, u32[]{:S(2)}) collective-permute-start(bf16[256,1024]{1,0:T(8,128)(2,1)S(1)} %get-tuple-element.38), channel_id=1, source_target_pairs={{0,1},{1,0},{2,3},{3,2},{4,5},{5,4},{6,7},{7,6},{8,9},{9,8},{10,11... | collective-permute-start | bytes 1572872 | tf_op jit(solution)/shard_map/ppermute | solution.py:229
  49.9 11.5 %collective-permute-start.20 = (bf16[256,512]{1,0:T(8,128)(2,1)S(1)}, bf16[256,512]{1,0:T(8,128)(2,1)S(1)}, u32[]{:S(2)}, u32[]{:S(2)}) collective-permute-start(bf16[256,512]{1,0:T(8,128)(2,1)S(1)} %get-tuple-element.43), channel_id=1, source_target_pairs={{0,2},{1,3},{2,0},{3,1},{4,6},{5,7},{6,4},{7,5},{8,10},{9,11},{10,... | collective-permute-start | bytes 786440 | tf_op jit(solution)/shard_map/ppermute | solution.py:229
  55.8 7.5 %collective-permute-start.23 = (bf16[256,512]{1,0:T(8,128)(2,1)S(1)}, bf16[256,512]{1,0:T(8,128)(2,1)S(1)}, u32[]{:S(2)}, u32[]{:S(2)}) collective-permute-start(bf16[256,512]{1,0:T(8,128)(2,1)S(1)} %add_convert_fusion.3), channel_id=1, source_target_pairs={{0,4},{1,5},{2,6},{3,7},{4,0},{5,1},{6,2},{7,3},{8,12},{9,13},{10,... | collective-permute-start | bytes 786440 | tf_op jit(solution)/shard_map/ppermute | solution.py:229
  61.4 12.4 %collective-permute-start.25 = (bf16[256,512]{1,0:T(8,128)(2,1)S(1)}, bf16[256,512]{1,0:T(8,128)(2,1)S(1)}, u32[]{:S(2)}, u32[]{:S(2)}) collective-permute-start(bf16[256,512]{1,0:T(8,128)(2,1)S(1)} %get-tuple-element.44), channel_id=1, source_target_pairs={{0,2},{1,3},{2,0},{3,1},{4,6},{5,7},{6,4},{7,5},{8,10},{9,11},{10,... | collective-permute-start | bytes 786440 | tf_op jit(solution)/shard_map/ppermute | solution.py:229
  61.4 3.3 %collective-permute-start.18 = (bf16[256,1024]{1,0:T(8,128)(2,1)S(1)}, bf16[256,1024]{1,0:T(8,128)(2,1)S(1)}, u32[]{:S(2)}, u32[]{:S(2)}) collective-permute-start(bf16[256,1024]{1,0:T(8,128)(2,1)S(1)} %get-tuple-element.39), channel_id=1, source_target_pairs={{0,1},{1,0},{2,3},{3,2},{4,5},{5,4},{6,7},{7,6},{8,9},{9,8},{10,11... | collective-permute-start | bytes 1572872 | tf_op jit(solution)/shard_map/ppermute | solution.py:229
  63.4 10.3 %collective-permute-start.24 = (bf16[128,512]{1,0:T(8,128)(2,1)S(1)}, bf16[128,512]{1,0:T(8,128)(2,1)S(1)}, u32[]{:S(2)}, u32[]{:S(2)}) collective-permute-start(bf16[128,512]{1,0:T(8,128)(2,1)S(1)} %get-tuple-element.51), channel_id=1, source_target_pairs={{0,8},{1,9},{2,10},{3,11},{4,12},{5,13},{6,14},{7,15},{8,0},{9,1},... | collective-permute-start | bytes 393224 | tf_op jit(solution)/shard_map/ppermute | solution.py:229
  66.3 10.9 %collective-permute-start.19 = (bf16[256,512]{1,0:T(8,128)(2,1)S(1)}, bf16[256,512]{1,0:T(8,128)(2,1)S(1)}, u32[]{:S(2)}, u32[]{:S(2)}) collective-permute-start(bf16[256,512]{1,0:T(8,128)(2,1)S(1)} %get-tuple-element.41), channel_id=1, source_target_pairs={{0,2},{1,3},{2,0},{3,1},{4,6},{5,7},{6,4},{7,5},{8,10},{9,11},{10,... | collective-permute-start | bytes 786440 | tf_op jit(solution)/shard_map/ppermute | solution.py:229
  68.2 9.1 %collective-permute-start.26 = (bf16[128,512]{1,0:T(8,128)(2,1)S(1)}, bf16[128,512]{1,0:T(8,128)(2,1)S(1)}, u32[]{:S(2)}, u32[]{:S(2)}) collective-permute-start(bf16[128,512]{1,0:T(8,128)(2,1)S(1)} %get-tuple-element.52), channel_id=1, source_target_pairs={{0,8},{1,9},{2,10},{3,11},{4,12},{5,13},{6,14},{7,15},{8,0},{9,1},... | collective-permute-start | bytes 393224 | tf_op jit(solution)/shard_map/ppermute | solution.py:229
  73.8 6.9 %collective-permute-start.27 = (bf16[256,512]{1,0:T(8,128)(2,1)S(1)}, bf16[256,512]{1,0:T(8,128)(2,1)S(1)}, u32[]{:S(2)}, u32[]{:S(2)}) collective-permute-start(bf16[256,512]{1,0:T(8,128)(2,1)S(1)} %add_convert_fusion.1), channel_id=1, source_target_pairs={{0,4},{1,5},{2,6},{3,7},{4,0},{5,1},{6,2},{7,3},{8,12},{9,13},{10,... | collective-permute-start | bytes 786440 | tf_op jit(solution)/shard_map/ppermute | solution.py:229

commit v5 on v4

--- a/solution.py
+++ b/solution.py
@@ -178,18 +178,21 @@
     lax.fori_loop(0, 2, step, 0)
 
 
-def sums_body(kept, sent, width, grad_gate, grad_up, w_gate, w_up, *refs):
+def sums_body(kept, arrived, sent, width, grad_gate, grad_up, w_gate, w_up, *refs):
     given = (grad_gate, grad_up, w_gate, w_up)
     refs = list(refs)
     if kept is not None:
-        got, keep, cross = refs.pop(0), refs.pop(0), refs.pop(0)
+        got = refs.pop(0) if arrived else None
+        keep, cross = refs.pop(0), refs.pop(0)
 
         def keep_row(i, at):
-            total = partial_sum(shard(kept, 1 - i, 0), width, *given) + got[:, at].astype(F32)
+            total = partial_sum(shard(kept, 1 - i, 0), width, *given)
+            if arrived:
+                total = total + got[:, at].astype(F32)
 
             @pl.when(i == 0)
             def _():
-                cross[...] = total.astype(BF16)
+                cross[...] = total.astype(cross.dtype)
 
             @pl.when(i == 1)
             def _():
@@ -209,11 +212,11 @@
     tok = grads[0].shape[0]
     args, outs = (*grads, *weights), []
     if kept is not None:
-        args = (*args, got)
-        outs += [jax.ShapeDtypeStruct((tok, width), F32), jax.ShapeDtypeStruct((tok, width), BF16)]
+        args = args if got is None else (*args, got)
+        outs += [jax.ShapeDtypeStruct((tok, width), dtype) for dtype in (F32, F32 if got is None else BF16)]
     if sent is not None:
         outs += [jax.ShapeDtypeStruct((tok, 2 * width), BF16)]
-    body = functools.partial(sums_body, kept, sent, width)
+    body = functools.partial(sums_body, kept, got is not None, sent, width)
     return call(body, [pltpu.VMEM] * len(args), outs, args, [], 1.5 * len(outs) / 2)
 
 
@@ -237,20 +240,18 @@
     scale = factors(gate_saved, up_saved)
     own_row = move(grad_out, row)
     near = move(grad_out, near_)
-    mid_a = move(grad_out[:half], mid_)
+    mid = move(grad_out, mid_)
     own_pair = move(grad_out, pair)
 
     near = after(near, scale[0])
     near_row = move(near, row)
-    mid_b = move(after(grad_out[half:], near), mid_)
     near_pair = move(near, pair)
     own_both = move(own_row, pair)
     (total,) = hidden(
         [((OWN, 0, 0), in_hbm(grad_out)), ((OWN, 0, 1), own_pair), ((OWN, 1, 0), own_row), ((NEAR, 0, 0), near)], w_down
     )
 
-    mid_b, near_row = after(mid_b, total, near_row), after(near_row, mid_b)
-    mid = jnp.concatenate([mid_a, mid_b])
+    mid = after(mid, total)
     mid_row = move(mid, row)
     far = move(mid, near_)
     mid_pair = move(mid, pair)
@@ -278,8 +279,10 @@
 
     step = functools.partial(sums, grads, weights, width)
     (sent_far,) = step(sent=FAR)
-    (sent_mid,) = step(sent=MID)
-    far, cross_far = step(kept=FAR, got=move(sent_far, pair))
+    far, cross_far = step(kept=FAR)
+    got_far = move(sent_far, pair).astype(F32)
+    far, cross_far = far + got_far[:, width:], (cross_far + got_far[:, :width]).astype(BF16)
+    (sent_mid,) = sums([after(grad, cross_far) for grad in grads], weights, width, sent=MID)
     mid, cross_mid, sent_near = step(kept=MID, got=move(sent_mid, pair), sent=NEAR)
     far = far + move(cross_far, row).astype(F32)
 

time: 82 us -> 79.8 us (0.973)
  starting transfers between devices: 24.6 us -> 20.4 us
  waiting for transfers between devices: 25.5 us -> 28.3 us
  local copies, waits for them, and re-layouts: 1.08 us -> 0.07 us
    ppermute x28 -> x27, starting transfers between devices: 24.6 us -> 20.4 us  [move(): return lax.ppermute(x, 'wid', [(i, i ^ bits) for i in range(n)])]
    ppermute x28 -> x27, waiting for transfers between devices: 25.5 us -> 28.3 us  [move(): return lax.ppermute(x, 'wid', [(i, i ^ bits) for i in range(n)])]
    slice x1 -> x0, local copies, waits for them, and re-layouts: 0.99 us -> none  [staged(): mid_b = move(after(grad_out[half:], near), mid_)]
  transfers between devices with their start and end apart: 28 -> 27, of which waited for: 11 -> 13; matrix products, arithmetic and copies ran while one was open for 2% -> 1% of each run, Pallas kernels for 29% -> 28%
where the time goes in v5:
time: 79.8 us; the launch traced here: 79.6 us
  Pallas kernels  29.2 us (37%)
  waiting for transfers between devices  28.3 us (35%)
  starting transfers between devices  20.4 us (26%)
  other arithmetic  1.38 us (2%)
    pallas_call x11, Pallas kernels, call(): pl.pallas_call(body, in_specs=[pl.BlockSpec(memory_space=space) for space...  29.2 us
    ppermute x27, waiting for transfers between devices, move(): return lax.ppermute(x, 'wid', [(i, i ^ bits) for i in range(n)])  28.3 us
    ppermute x27, starting transfers between devices, move(): return lax.ppermute(x, 'wid', [(i, i ^ bits) for i in range(n)])  20.4 us
  transfers between devices with their start and end apart: 27, of which 13 were waited for; matrix products, arithmetic and copies ran while one was open for 1% of the time, Pallas kernels for 28%

profile of v5, /device:TPU:0, one launch (start us, length us, event | category | flops | bytes accessed | tf_op | source)
XLA Modules:
  0.0 79.6 jit_solution(8201718551100567028)
XLA Ops:
  0.0 3.0 %collective-permute-start.3 = (bf16[256,512]{1,0:T(8,128)(2,1)}, bf16[256,512]{1,0:T(8,128)(2,1)S(1)}, u32[]{:S(2)}, u32[]{:S(2)}) collective-permute-start(bf16[256,512]{1,0:T(8,128)(2,1)} %refs_0_.1), channel_id=1, source_target_pairs={{0,4},{1,5},{2,6},{3,7},{4,0},{5,1},{6,2},{7,3},{8,12},{9,13},{10,... | collective-permute-start | bytes 786440 | tf_op jit(solution)/shard_map/ppermute | solution.py:232
  3.0 1.5 %collective-permute-start.2 = (bf16[256,512]{1,0:T(8,128)(2,1)}, bf16[256,512]{1,0:T(8,128)(2,1)S(1)}, u32[]{:S(2)}, u32[]{:S(2)}) collective-permute-start(bf16[256,512]{1,0:T(8,128)(2,1)} %refs_0_.1), channel_id=1, source_target_pairs={{0,2},{1,3},{2,0},{3,1},{4,6},{5,7},{6,4},{7,5},{8,10},{9,11},{10,... | collective-permute-start | bytes 786440 | tf_op jit(solution)/shard_map/ppermute | solution.py:232
  4.5 0.0 collective-permute-start.1
  4.5 2.6 %collective-permute-start = (bf16[256,512]{1,0:T(8,128)(2,1)}, bf16[256,512]{1,0:T(8,128)(2,1)S(1)}, u32[]{:S(2)}, u32[]{:S(2)}) collective-permute-start(bf16[256,512]{1,0:T(8,128)(2,1)} %refs_0_.1), channel_id=1, source_target_pairs={{0,8},{1,9},{2,10},{3,11},{4,12},{5,13},{6,14},{7,15},{8,0},{9,1},... | collective-permute-start | bytes 786440 | tf_op jit(solution)/shard_map/ppermute | solution.py:232
  7.1 1.8 %shard_map.64 = (f32[256,1024]{1,0:T(8,128)S(1)}, f32[256,1024]{1,0:T(8,128)S(1)}) custom-call(bf16[256,1024]{1,0:T(8,128)(2,1)} %gate.1, bf16[256,1024]{1,0:T(8,128)(2,1)} %up.1), custom_call_target="tpu_custom_call" | custom-call | flops 200000000 | tf_op jit(solution)/shard_map/pallas_call | solution.py:30
  8.9 3.1 %collective-permute-done.3.refs_3_ = bf16[256,512]{1,0:T(8,128)(2,1)S(1)} collective-permute-done((bf16[256,512]{1,0:T(8,128)(2,1)}, bf16[256,512]{1,0:T(8,128)(2,1)S(1)}, u32[]{:S(2)}, u32[]{:S(2)}) %collective-permute-start.3) | collective-permute-done | bytes 262176 | tf_op jit(solution)/shard_map/ppermute | solution.py:232
  12.1 3.2 %collective-permute-start.9 = (bf16[256,512]{1,0:T(8,128)(2,1)S(1)}, bf16[256,512]{1,0:T(8,128)(2,1)S(1)}, u32[]{:S(2)}, u32[]{:S(2)}) collective-permute-start(bf16[256,512]{1,0:T(8,128)(2,1)S(1)} %collective-permute-done.3.refs_3_), channel_id=1, source_target_pairs={{0,2},{1,3},{2,0},{3,1},{4,6},{5,7},{6,4},{7,5},{8,10},{9,11},{10,... | collective-permute-start | bytes 786440 | tf_op jit(solution)/shard_map/ppermute | solution.py:232
  15.3 0.5 collective-permute-start.7
  15.8 4.1 %shard_map.65.refs_5_ = f32[256,1024]{1,0:T(8,128)S(1)} custom-call(bf16[256,512]{1,0:T(8,128)(2,1)} %refs_0_.1, bf16[256,512]{1,0:T(8,128)(2,1)S(1)} %collective-permute-done.1.refs_1_, bf16[256,512]{1,0:T(8,128)(2,1)S(1)} %collective-permute-done.2.refs_2_, bf16[256,512]{1,0:T(8,128)(2,1)S(1)} %collective-permute-done.3.refs_3_, bf16[1024,8192]{1,0:T(8,128)(2,1)} %refs_4_.7), custom_call_target="tpu_custom_call" | custom-call | flops 600000000 | tf_op jit(solution)/shard_map/pallas_call | solution.py:30
  19.9 0.0 slice-start.2
  19.9 0.1 collective-permute-done.refs_3_
  20.0 0.5 collective-permute-start.4
  20.5 0.0 collective-permute-done.9.refs_2_
  20.6 0.0 collective-permute-start.13
  20.6 0.0 collective-permute-done.8.refs_1_
  20.6 0.5 collective-permute-start.12
  21.1 0.0 collective-permute-done.7.refs_0_
  21.1 4.1 %shard_map.66.refs_5_ = f32[256,1024]{1,0:T(8,128)S(1)} custom-call(bf16[256,512]{1,0:T(8,128)(2,1)S(1)} %collective-permute-done.7.refs_0_, bf16[256,512]{1,0:T(8,128)(2,1)S(1)} %collective-permute-done.8.refs_1_, bf16[256,512]{1,0:T(8,128)(2,1)S(1)} %collective-permute-done.9.refs_2_, bf16[256,512]{1,0:T(8,128)(2,1)S(1)} %collective-permute-done.refs_3_, ...), custom_call_target="tpu_custom_call" | custom-call | flops 600000000 | tf_op jit(solution)/shard_map/pallas_call | solution.py:30
  25.2 2.9 %collective-permute-done.6.refs_3_ = bf16[256,512]{1,0:T(8,128)(2,1)S(1)} collective-permute-done((bf16[256,512]{1,0:T(8,128)(2,1)S(1)}, bf16[256,512]{1,0:T(8,128)(2,1)S(1)}, u32[]{:S(2)}, u32[]{:S(2)}) %collective-permute-start.6) | collective-permute-done | bytes 262176 | tf_op jit(solution)/shard_map/ppermute | solution.py:232
  28.1 0.4 collective-permute-start.11
  28.5 0.0 collective-permute-start.10
  28.5 0.0 collective-permute-done.4.refs_2_
  28.5 0.5 collective-permute-start.5
  29.0 0.0 collective-permute-done.13.refs_1_
  29.0 0.0 collective-permute-done.12.refs_0_
  29.1 0.0 slice-start.4
  29.1 0.0 slice-start.5
  29.1 0.0 slice-start.6
  29.1 3.5 %shard_map.67.refs_5_ = f32[256,1024]{1,0:T(8,128)S(1)} custom-call(bf16[256,512]{1,0:T(8,128)(2,1)S(1)} %collective-permute-done.12.refs_0_, bf16[256,512]{1,0:T(8,128)(2,1)S(1)} %collective-permute-done.13.refs_1_, bf16[256,512]{1,0:T(8,128)(2,1)S(1)} %collective-permute-done.4.refs_2_, bf16[256,512]{1,0:T(8,128)(2,1)S(1)} %collective-permute-done.6.refs_3_, ...), custom_call_target="tpu_custom_call" | custom-call | flops 600000000 | tf_op jit(solution)/shard_map/pallas_call | solution.py:30
  32.6 2.6 %collective-permute-done.11.refs_2_ = bf16[256,512]{1,0:T(8,128)(2,1)S(1)} collective-permute-done((bf16[256,512]{1,0:T(8,128)(2,1)S(1)}, bf16[256,512]{1,0:T(8,128)(2,1)S(1)}, u32[]{:S(2)}, u32[]{:S(2)}) %collective-permute-start.11) | collective-permute-done | bytes 262176 | tf_op jit(solution)/shard_map/ppermute | solution.py:232
  35.2 1.5 %collective-permute-done.14.refs_3_ = bf16[256,512]{1,0:T(8,128)(2,1)S(1)} collective-permute-done((bf16[256,512]{1,0:T(8,128)(2,1)S(1)}, bf16[256,512]{1,0:T(8,128)(2,1)S(1)}, u32[]{:S(2)}, u32[]{:S(2)}) %collective-permute-start.14) | collective-permute-done | bytes 262176 | tf_op jit(solution)/shard_map/ppermute | solution.py:232
  36.7 3.5 %shard_map.68 = (bf16[256,1024]{1,0:T(8,128)(2,1)S(1)}, bf16[256,1024]{1,0:T(8,128)(2,1)S(1)}) custom-call(bf16[256,512]{1,0:T(8,128)(2,1)S(1)} %collective-permute-done.5.refs_0_, bf16[256,512]{1,0:T(8,128)(2,1)S(1)} %collective-permute-done.10.refs_1_, bf16[256,512]{1,0:T(8,128)(2,1)S(1)} %collective-permute-done.11.refs_2_, ...), custom_call_target="tpu_custom_call" | custom-call | flops 600000000 | tf_op jit(solution)/shard_map/pallas_call | solution.py:30
  40.3 1.5 %shard_map.70 = bf16[256,1024]{1,0:T(8,128)(2,1)S(1)} custom-call(bf16[256,1024]{1,0:T(8,128)(2,1)S(1)} %get-tuple-element.37.grad_gate, bf16[256,1024]{1,0:T(8,128)(2,1)S(1)} %get-tuple-element.38.grad_up, bf16[8192,1024]{1,0:T(8,128)(2,1)S(1)} %bitcast.1, bf16[8192,1024]{1,0:T(8,128)(2,1)S(1)} %bitcast.3), custom_call_target="tpu_custom_call" | custom-call | flops 150000000 | tf_op jit(solution)/shard_map/pallas_call | solution.py:30
  41.8 0.2 collective-permute-start.15
  42.0 1.5 %shard_map.69 = (f32[256,512]{1,0:T(8,128)S(1)}, f32[256,512]{1,0:T(8,128)S(1)}) custom-call(bf16[256,1024]{1,0:T(8,128)(2,1)S(1)} %get-tuple-element.37.grad_gate, bf16[256,1024]{1,0:T(8,128)(2,1)S(1)} %get-tuple-element.38.grad_up, bf16[8192,1024]{1,0:T(8,128)(2,1)S(1)} %bitcast.1, bf16[8192,1024]{1,0:T(8,128)(2,1)S(1)} %bitcast.3), custom_call_target="tpu_custom_call" | custom-call | flops 300000000 | tf_op jit(solution)/shard_map/pallas_call | solution.py:30
  43.6 0.2 collective-permute-done.15
  43.8 0.1 convert_element_type.39
  43.9 0.1 fusion.2
  44.0 1.5 %shard_map.71 = bf16[256,1024]{1,0:T(8,128)(2,1)S(1)} custom-call(bf16[256,1024]{1,0:T(8,128)(2,1)S(1)} %get-tuple-element.37.grad_gate, bf16[256,1024]{1,0:T(8,128)(2,1)S(1)} %get-tuple-element.38.grad_up, bf16[8192,1024]{1,0:T(8,128)(2,1)S(1)} %bitcast.1, bf16[8192,1024]{1,0:T(8,128)(2,1)S(1)} %bitcast.3), custom_call_target="tpu_custom_call" | custom-call | flops 150000000 | tf_op jit(solution)/shard_map/pallas_call | solution.py:30
  45.5 0.2 collective-permute-start.16
  45.7 0.3 collective-permute-start.21
  46.1 1.4 %collective-permute-done.16.refs_0_ = bf16[256,1024]{1,0:T(8,128)(2,1)S(1)} collective-permute-done((bf16[256,1024]{1,0:T(8,128)(2,1)S(1)}, bf16[256,1024]{1,0:T(8,128)(2,1)S(1)}, u32[]{:S(2)}, u32[]{:S(2)}) %collective-permute-start.16) | collective-permute-done | bytes 524320 | tf_op jit(solution)/shard_map/ppermute | solution.py:232
  47.5 3.0 %shard_map.72 = (f32[256,512]{1,0:T(8,128)S(1)}, bf16[256,512]{1,0:T(8,128)(2,1)S(1)}, bf16[256,1024]{1,0:T(8,128)(2,1)S(1)}) custom-call(bf16[256,1024]{1,0:T(8,128)(2,1)S(1)} %get-tuple-element.37.grad_gate, bf16[256,1024]{1,0:T(8,128)(2,1)S(1)} %get-tuple-element.38.grad_up, bf16[8192,1024]{1,0:T(8,128)(2,1)S(1)} %bitcast.1, ...), custom_call_target="tpu_custom_call" | custom-call | flops 450000000 | tf_op jit(solution)/shard_map/pallas_call | solution.py:30
  50.5 0.2 collective-permute-start.17
  50.8 0.3 collective-permute-start.20
  51.1 3.8 %collective-permute-done.21 = bf16[256,512]{1,0:T(8,128)(2,1)S(1)} collective-permute-done((bf16[256,512]{1,0:T(8,128)(2,1)S(1)}, bf16[256,512]{1,0:T(8,128)(2,1)S(1)}, u32[]{:S(2)}, u32[]{:S(2)}) %collective-permute-start.21) | collective-permute-done | bytes 262176 | tf_op jit(solution)/shard_map/ppermute | solution.py:232
  54.9 0.1 fusion.1
  55.0 0.7 collective-permute-start.22
  55.7 3.0 %shard_map.73 = (f32[256,512]{1,0:T(8,128)S(1)}, bf16[256,512]{1,0:T(8,128)(2,1)S(1)}, bf16[256,1024]{1,0:T(8,128)(2,1)S(1)}) custom-call(bf16[256,1024]{1,0:T(8,128)(2,1)S(1)} %get-tuple-element.37.grad_gate, bf16[256,1024]{1,0:T(8,128)(2,1)S(1)} %get-tuple-element.38.grad_up, bf16[8192,1024]{1,0:T(8,128)(2,1)S(1)} %bitcast.1, ...), custom_call_target="tpu_custom_call" | custom-call | flops 450000000 | tf_op jit(solution)/shard_map/pallas_call | solution.py:30
  58.7 0.6 collective-permute-start.24
  59.3 0.6 collective-permute-done.20
  59.9 2.3 %collective-permute-done.22 = bf16[256,512]{1,0:T(8,128)(2,1)S(1)} collective-permute-done((bf16[256,512]{1,0:T(8,128)(2,1)S(1)}, bf16[256,512]{1,0:T(8,128)(2,1)S(1)}, u32[]{:S(2)}, u32[]{:S(2)}) %collective-permute-start.22) | collective-permute-done | bytes 262176 | tf_op jit(solution)/shard_map/ppermute | solution.py:232
  62.2 0.1 add_convert_fusion.2
  62.4 2.0 %collective-permute-start.23 = (bf16[128,512]{1,0:T(8,128)(2,1)S(1)}, bf16[128,512]{1,0:T(8,128)(2,1)S(1)}, u32[]{:S(2)}, u32[]{:S(2)}) collective-permute-start(bf16[128,512]{1,0:T(8,128)(2,1)S(1)} %get-tuple-element.51), channel_id=1, source_target_pairs={{0,8},{1,9},{2,10},{3,11},{4,12},{5,13},{6,14},{7,15},{8,0},{9,1},... | collective-permute-start | bytes 393224 | tf_op jit(solution)/shard_map/ppermute | solution.py:232
  64.4 1.6 %shard_map.74 = (f32[256,512]{1,0:T(8,128)S(1)}, bf16[256,512]{1,0:T(8,128)(2,1)S(1)}) custom-call(bf16[256,1024]{1,0:T(8,128)(2,1)S(1)} %get-tuple-element.37.grad_gate, bf16[256,1024]{1,0:T(8,128)(2,1)S(1)} %get-tuple-element.38.grad_up, bf16[8192,1024]{1,0:T(8,128)(2,1)S(1)} %bitcast.1, bf16[8192,1024]{1,0:T(8,128)(2,1)S(1)} %bitcast.3, ...), custom_call_target="tpu_custom_call" | custom-call | flops 300000000 | tf_op jit(solution)/shard_map/pallas_call | solution.py:30
  66.0 0.4 collective-permute-start.19
  66.3 1.0 %collective-permute-start.25 = (bf16[128,512]{1,0:T(8,128)(2,1)S(1)}, bf16[128,512]{1,0:T(8,128)(2,1)S(1)}, u32[]{:S(2)}, u32[]{:S(2)}) collective-permute-start(bf16[128,512]{1,0:T(8,128)(2,1)S(1)} %get-tuple-element.52), channel_id=1, source_target_pairs={{0,8},{1,9},{2,10},{3,11},{4,12},{5,13},{6,14},{7,15},{8,0},{9,1},... | collective-permute-start | bytes 393224 | tf_op jit(solution)/shard_map/ppermute | solution.py:232
  67.3 5.0 %collective-permute-done.23 = bf16[128,512]{1,0:T(8,128)(2,1)S(1)} collective-permute-done((bf16[128,512]{1,0:T(8,128)(2,1)S(1)}, bf16[128,512]{1,0:T(8,128)(2,1)S(1)}, u32[]{:S(2)}, u32[]{:S(2)}) %collective-permute-start.23) | collective-permute-done | bytes 131104 | tf_op jit(solution)/shard_map/ppermute | solution.py:232
  72.3 0.1 add_convert_fusion.1
  72.4 1.6 %collective-permute-start.26 = (bf16[256,512]{1,0:T(8,128)(2,1)S(1)}, bf16[256,512]{1,0:T(8,128)(2,1)S(1)}, u32[]{:S(2)}, u32[]{:S(2)}) collective-permute-start(bf16[256,512]{1,0:T(8,128)(2,1)S(1)} %add_convert_fusion.1), channel_id=1, source_target_pairs={{0,4},{1,5},{2,6},{3,7},{4,0},{5,1},{6,2},{7,3},{8,12},{9,13},{10,... | collective-permute-start | bytes 786440 | tf_op jit(solution)/shard_map/ppermute | solution.py:232
  74.0 1.5 %collective-permute-done.25 = bf16[128,512]{1,0:T(8,128)(2,1)S(1)} collective-permute-done((bf16[128,512]{1,0:T(8,128)(2,1)S(1)}, bf16[128,512]{1,0:T(8,128)(2,1)S(1)}, u32[]{:S(2)}, u32[]{:S(2)}) %collective-permute-start.25) | collective-permute-done | bytes 131104 | tf_op jit(solution)/shard_map/ppermute | solution.py:232
  75.5 0.1 convert_add_fusion
  75.6 3.3 %collective-permute-done.26 = bf16[256,512]{1,0:T(8,128)(2,1)S(1)} collective-permute-done((bf16[256,512]{1,0:T(8,128)(2,1)S(1)}, bf16[256,512]{1,0:T(8,128)(2,1)S(1)}, u32[]{:S(2)}, u32[]{:S(2)}) %collective-permute-start.26) | collective-permute-done | bytes 262176 | tf_op jit(solution)/shard_map/ppermute | solution.py:232
  78.8 0.8 add_convert_fusion
  (29 shorter events, 0.1 us)
Async XLA Ops:
  0.0 12.0 %collective-permute-start.3 = (bf16[256,512]{1,0:T(8,128)(2,1)}, bf16[256,512]{1,0:T(8,128)(2,1)S(1)}, u32[]{:S(2)}, u32[]{:S(2)}) collective-permute-start(bf16[256,512]{1,0:T(8,128)(2,1)} %refs_0_.1), channel_id=1, source_target_pairs={{0,4},{1,5},{2,6},{3,7},{4,0},{5,1},{6,2},{7,3},{8,12},{9,13},{10,... | collective-permute-start | bytes 786440 | tf_op jit(solution)/shard_map/ppermute | solution.py:232
  3.0 12.3 %collective-permute-start.2 = (bf16[256,512]{1,0:T(8,128)(2,1)}, bf16[256,512]{1,0:T(8,128)(2,1)S(1)}, u32[]{:S(2)}, u32[]{:S(2)}) collective-permute-start(bf16[256,512]{1,0:T(8,128)(2,1)} %refs_0_.1), channel_id=1, source_target_pairs={{0,2},{1,3},{2,0},{3,1},{4,6},{5,7},{6,4},{7,5},{8,10},{9,11},{10,... | collective-permute-start | bytes 786440 | tf_op jit(solution)/shard_map/ppermute | solution.py:232
  4.5 11.2 %collective-permute-start.1 = (bf16[256,512]{1,0:T(8,128)(2,1)}, bf16[256,512]{1,0:T(8,128)(2,1)S(1)}, u32[]{:S(2)}, u32[]{:S(2)}) collective-permute-start(bf16[256,512]{1,0:T(8,128)(2,1)} %refs_0_.1), channel_id=1, source_target_pairs={{0,1},{1,0},{2,3},{3,2},{4,5},{5,4},{6,7},{7,6},{8,9},{9,8},{10,11... | collective-permute-start | bytes 786440 | tf_op jit(solution)/shard_map/ppermute | solution.py:232
  4.5 15.5 %collective-permute-start = (bf16[256,512]{1,0:T(8,128)(2,1)}, bf16[256,512]{1,0:T(8,128)(2,1)S(1)}, u32[]{:S(2)}, u32[]{:S(2)}) collective-permute-start(bf16[256,512]{1,0:T(8,128)(2,1)} %refs_0_.1), channel_id=1, source_target_pairs={{0,8},{1,9},{2,10},{3,11},{4,12},{5,13},{6,14},{7,15},{8,0},{9,1},... | collective-permute-start | bytes 786440 | tf_op jit(solution)/shard_map/ppermute | solution.py:232
  12.1 17.0 %slice-start = ((s8[16777216]{0:T(1024)(128)(4,1)}), s8[4194304]{0:T(1024)(128)(4,1)S(1)}, s32[]{:S(2)}) async-start(s8[16777216]{0:T(1024)(128)(4,1)} %bitcast), calls=%async_computation | async-start | bytes 8388608
  12.1 17.0 %slice-start.1 = ((s8[16777216]{0:T(1024)(128)(4,1)}), s8[4194304]{0:T(1024)(128)(4,1)S(1)}, s32[]{:S(2)}) async-start(s8[16777216]{0:T(1024)(128)(4,1)} %bitcast), calls=%async_computation.1 | async-start | bytes 8388608
  12.1 17.0 %copy-start = (bf16[8192,1024]{1,0:T(8,128)(2,1)S(1)}, bf16[8192,1024]{1,0:T(8,128)(2,1)}, u32[]{:S(2)}) copy-start(bf16[8192,1024]{1,0:T(8,128)(2,1)} %w_up.11) | copy-start | bytes 50331652
  12.1 8.5 %collective-permute-start.9 = (bf16[256,512]{1,0:T(8,128)(2,1)S(1)}, bf16[256,512]{1,0:T(8,128)(2,1)S(1)}, u32[]{:S(2)}, u32[]{:S(2)}) collective-permute-start(bf16[256,512]{1,0:T(8,128)(2,1)S(1)} %collective-permute-done.3.refs_3_), channel_id=1, source_target_pairs={{0,2},{1,3},{2,0},{3,1},{4,6},{5,7},{6,4},{7,5},{8,10},{9,11},{10,... | collective-permute-start | bytes 786440 | tf_op jit(solution)/shard_map/ppermute | solution.py:232
  15.3 5.3 %collective-permute-start.8 = (bf16[256,512]{1,0:T(8,128)(2,1)S(1)}, bf16[256,512]{1,0:T(8,128)(2,1)S(1)}, u32[]{:S(2)}, u32[]{:S(2)}) collective-permute-start(bf16[256,512]{1,0:T(8,128)(2,1)S(1)} %collective-permute-done.3.refs_3_), channel_id=1, source_target_pairs={{0,1},{1,0},{2,3},{3,2},{4,5},{5,4},{6,7},{7,6},{8,9},{9,8},{10,11... | collective-permute-start | bytes 786440 | tf_op jit(solution)/shard_map/ppermute | solution.py:232
  15.3 5.8 %collective-permute-start.7 = (bf16[256,512]{1,0:T(8,128)(2,1)S(1)}, bf16[256,512]{1,0:T(8,128)(2,1)S(1)}, u32[]{:S(2)}, u32[]{:S(2)}) collective-permute-start(bf16[256,512]{1,0:T(8,128)(2,1)S(1)} %collective-permute-done.2.refs_2_), channel_id=1, source_target_pairs={{0,1},{1,0},{2,3},{3,2},{4,5},{5,4},{6,7},{7,6},{8,9},{9,8},{10,11... | collective-permute-start | bytes 786440 | tf_op jit(solution)/shard_map/ppermute | solution.py:232
  19.9 9.1 %slice-start.2 = ((s8[16777216]{0:T(1024)(128)(4,1)}), s8[4194304]{0:T(1024)(128)(4,1)S(1)}, s32[]{:S(2)}) async-start(s8[16777216]{0:T(1024)(128)(4,1)} %bitcast), calls=%async_computation.2 | async-start | bytes 8388608
  19.9 9.1 %slice-start.3 = ((s8[16777216]{0:T(1024)(128)(4,1)}), s8[4194304]{0:T(1024)(128)(4,1)S(1)}, s32[]{:S(2)}) async-start(s8[16777216]{0:T(1024)(128)(4,1)} %bitcast), calls=%async_computation.3 | async-start | bytes 8388608
  20.0 8.0 %collective-permute-start.6 = (bf16[256,512]{1,0:T(8,128)(2,1)S(1)}, bf16[256,512]{1,0:T(8,128)(2,1)S(1)}, u32[]{:S(2)}, u32[]{:S(2)}) collective-permute-start(bf16[256,512]{1,0:T(8,128)(2,1)S(1)} %collective-permute-done.refs_3_), channel_id=1, source_target_pairs={{0,4},{1,5},{2,6},{3,7},{4,0},{5,1},{6,2},{7,3},{8,12},{9,13},{10,... | collective-permute-start | bytes 786440 | tf_op jit(solution)/shard_map/ppermute | solution.py:232
  20.0 8.4 %collective-permute-start.4 = (bf16[256,512]{1,0:T(8,128)(2,1)S(1)}, bf16[256,512]{1,0:T(8,128)(2,1)S(1)}, u32[]{:S(2)}, u32[]{:S(2)}) collective-permute-start(bf16[256,512]{1,0:T(8,128)(2,1)S(1)} %collective-permute-done.refs_3_), channel_id=1, source_target_pairs={{0,2},{1,3},{2,0},{3,1},{4,6},{5,7},{6,4},{7,5},{8,10},{9,11},{10,... | collective-permute-start | bytes 786440 | tf_op jit(solution)/shard_map/ppermute | solution.py:232
  20.6 8.4 %collective-permute-start.13 = (bf16[256,512]{1,0:T(8,128)(2,1)S(1)}, bf16[256,512]{1,0:T(8,128)(2,1)S(1)}, u32[]{:S(2)}, u32[]{:S(2)}) collective-permute-start(bf16[256,512]{1,0:T(8,128)(2,1)S(1)} %collective-permute-done.refs_3_), channel_id=1, source_target_pairs={{0,1},{1,0},{2,3},{3,2},{4,5},{5,4},{6,7},{7,6},{8,9},{9,8},{10,11... | collective-permute-start | bytes 786440 | tf_op jit(solution)/shard_map/ppermute | solution.py:232
  20.6 8.4 %collective-permute-start.12 = (bf16[256,512]{1,0:T(8,128)(2,1)S(1)}, bf16[256,512]{1,0:T(8,128)(2,1)S(1)}, u32[]{:S(2)}, u32[]{:S(2)}) collective-permute-start(bf16[256,512]{1,0:T(8,128)(2,1)S(1)} %collective-permute-done.9.refs_2_), channel_id=1, source_target_pairs={{0,1},{1,0},{2,3},{3,2},{4,5},{5,4},{6,7},{7,6},{8,9},{9,8},{10,11... | collective-permute-start | bytes 786440 | tf_op jit(solution)/shard_map/ppermute | solution.py:232
  28.1 7.1 %collective-permute-start.11 = (bf16[256,512]{1,0:T(8,128)(2,1)S(1)}, bf16[256,512]{1,0:T(8,128)(2,1)S(1)}, u32[]{:S(2)}, u32[]{:S(2)}) collective-permute-start(bf16[256,512]{1,0:T(8,128)(2,1)S(1)} %collective-permute-done.6.refs_3_), channel_id=1, source_target_pairs={{0,2},{1,3},{2,0},{3,1},{4,6},{5,7},{6,4},{7,5},{8,10},{9,11},{10,... | collective-permute-start | bytes 786440 | tf_op jit(solution)/shard_map/ppermute | solution.py:232
  28.5 6.7 %collective-permute-start.10 = (bf16[256,512]{1,0:T(8,128)(2,1)S(1)}, bf16[256,512]{1,0:T(8,128)(2,1)S(1)}, u32[]{:S(2)}, u32[]{:S(2)}) collective-permute-start(bf16[256,512]{1,0:T(8,128)(2,1)S(1)} %collective-permute-done.6.refs_3_), channel_id=1, source_target_pairs={{0,1},{1,0},{2,3},{3,2},{4,5},{5,4},{6,7},{7,6},{8,9},{9,8},{10,11... | collective-permute-start | bytes 786440 | tf_op jit(solution)/shard_map/ppermute | solution.py:232
  28.5 6.7 %collective-permute-start.5 = (bf16[256,512]{1,0:T(8,128)(2,1)S(1)}, bf16[256,512]{1,0:T(8,128)(2,1)S(1)}, u32[]{:S(2)}, u32[]{:S(2)}) collective-permute-start(bf16[256,512]{1,0:T(8,128)(2,1)S(1)} %collective-permute-done.4.refs_2_), channel_id=1, source_target_pairs={{0,1},{1,0},{2,3},{3,2},{4,5},{5,4},{6,7},{7,6},{8,9},{9,8},{10,11... | collective-permute-start | bytes 786440 | tf_op jit(solution)/shard_map/ppermute | solution.py:232
  29.1 11.2 %slice-start.4 = ((s8[16777216]{0:T(1024)(128)(4,1)}), s8[4194304]{0:T(1024)(128)(4,1)S(1)}, s32[]{:S(2)}) async-start(s8[16777216]{0:T(1024)(128)(4,1)} %bitcast.2), calls=%async_computation.4 | async-start | bytes 8388608
  29.1 11.2 %slice-start.5 = ((s8[16777216]{0:T(1024)(128)(4,1)}), s8[4194304]{0:T(1024)(128)(4,1)S(1)}, s32[]{:S(2)}) async-start(s8[16777216]{0:T(1024)(128)(4,1)} %bitcast.2), calls=%async_computation.5 | async-start | bytes 8388608
  29.1 11.2 %slice-start.6 = ((s8[16777216]{0:T(1024)(128)(4,1)}), s8[4194304]{0:T(1024)(128)(4,1)S(1)}, s32[]{:S(2)}) async-start(s8[16777216]{0:T(1024)(128)(4,1)} %bitcast.2), calls=%async_computation.6 | async-start | bytes 8388608
  35.2 1.5 %collective-permute-start.14 = (bf16[256,512]{1,0:T(8,128)(2,1)S(1)}, bf16[256,512]{1,0:T(8,128)(2,1)S(1)}, u32[]{:S(2)}, u32[]{:S(2)}) collective-permute-start(bf16[256,512]{1,0:T(8,128)(2,1)S(1)} %collective-permute-done.11.refs_2_), channel_id=1, source_target_pairs={{0,1},{1,0},{2,3},{3,2},{4,5},{5,4},{6,7},{7,6},{8,9},{9,8},{10,11... | collective-permute-start | bytes 786440 | tf_op jit(solution)/shard_map/ppermute | solution.py:232
  36.7 3.6 %slice-start.7 = ((s8[16777216]{0:T(1024)(128)(4,1)}), s8[4194304]{0:T(1024)(128)(4,1)S(1)}, s32[]{:S(2)}) async-start(s8[16777216]{0:T(1024)(128)(4,1)} %bitcast.2), calls=%async_computation.7 | async-start | bytes 8388608
  41.8 2.0 %collective-permute-start.15 = (bf16[256,1024]{1,0:T(8,128)(2,1)S(1)}, bf16[256,1024]{1,0:T(8,128)(2,1)S(1)}, u32[]{:S(2)}, u32[]{:S(2)}) collective-permute-start(bf16[256,1024]{1,0:T(8,128)(2,1)S(1)} %shard_map.70), channel_id=1, source_target_pairs={{0,1},{1,0},{2,3},{3,2},{4,5},{5,4},{6,7},{7,6},{8,9},{9,8},{10,11... | collective-permute-start | bytes 1572872 | tf_op jit(solution)/shard_map/ppermute | solution.py:232
  45.5 2.0 %collective-permute-start.16 = (bf16[256,1024]{1,0:T(8,128)(2,1)S(1)}, bf16[256,1024]{1,0:T(8,128)(2,1)S(1)}, u32[]{:S(2)}, u32[]{:S(2)}) collective-permute-start(bf16[256,1024]{1,0:T(8,128)(2,1)S(1)} %shard_map.71), channel_id=1, source_target_pairs={{0,1},{1,0},{2,3},{3,2},{4,5},{5,4},{6,7},{7,6},{8,9},{9,8},{10,11... | collective-permute-start | bytes 1572872 | tf_op jit(solution)/shard_map/ppermute | solution.py:232
  45.7 9.1 %collective-permute-start.21 = (bf16[256,512]{1,0:T(8,128)(2,1)S(1)}, bf16[256,512]{1,0:T(8,128)(2,1)S(1)}, u32[]{:S(2)}, u32[]{:S(2)}) collective-permute-start(bf16[256,512]{1,0:T(8,128)(2,1)S(1)} %fusion.2), channel_id=1, source_target_pairs={{0,2},{1,3},{2,0},{3,1},{4,6},{5,7},{6,4},{7,5},{8,10},{9,11},{10,... | collective-permute-start | bytes 786440 | tf_op jit(solution)/shard_map/ppermute | solution.py:232
  50.5 5.1 %collective-permute-start.17 = (bf16[256,1024]{1,0:T(8,128)(2,1)S(1)}, bf16[256,1024]{1,0:T(8,128)(2,1)S(1)}, u32[]{:S(2)}, u32[]{:S(2)}) collective-permute-start(bf16[256,1024]{1,0:T(8,128)(2,1)S(1)} %get-tuple-element.39), channel_id=1, source_target_pairs={{0,1},{1,0},{2,3},{3,2},{4,5},{5,4},{6,7},{7,6},{8,9},{9,8},{10,11... | collective-permute-start | bytes 1572872 | tf_op jit(solution)/shard_map/ppermute | solution.py:232
  50.8 9.1 %collective-permute-start.20 = (bf16[256,512]{1,0:T(8,128)(2,1)S(1)}, bf16[256,512]{1,0:T(8,128)(2,1)S(1)}, u32[]{:S(2)}, u32[]{:S(2)}) collective-permute-start(bf16[256,512]{1,0:T(8,128)(2,1)S(1)} %get-tuple-element.44), channel_id=1, source_target_pairs={{0,2},{1,3},{2,0},{3,1},{4,6},{5,7},{6,4},{7,5},{8,10},{9,11},{10,... | collective-permute-start | bytes 786440 | tf_op jit(solution)/shard_map/ppermute | solution.py:232
  55.0 7.2 %collective-permute-start.22 = (bf16[256,512]{1,0:T(8,128)(2,1)S(1)}, bf16[256,512]{1,0:T(8,128)(2,1)S(1)}, u32[]{:S(2)}, u32[]{:S(2)}) collective-permute-start(bf16[256,512]{1,0:T(8,128)(2,1)S(1)} %fusion.1), channel_id=1, source_target_pairs={{0,4},{1,5},{2,6},{3,7},{4,0},{5,1},{6,2},{7,3},{8,12},{9,13},{10,... | collective-permute-start | bytes 786440 | tf_op jit(solution)/shard_map/ppermute | solution.py:232
  58.7 13.6 %collective-permute-start.24 = (bf16[256,512]{1,0:T(8,128)(2,1)S(1)}, bf16[256,512]{1,0:T(8,128)(2,1)S(1)}, u32[]{:S(2)}, u32[]{:S(2)}) collective-permute-start(bf16[256,512]{1,0:T(8,128)(2,1)S(1)} %get-tuple-element.45), channel_id=1, source_target_pairs={{0,2},{1,3},{2,0},{3,1},{4,6},{5,7},{6,4},{7,5},{8,10},{9,11},{10,... | collective-permute-start | bytes 786440 | tf_op jit(solution)/shard_map/ppermute | solution.py:232
  59.9 4.5 %collective-permute-start.18 = (bf16[256,1024]{1,0:T(8,128)(2,1)S(1)}, bf16[256,1024]{1,0:T(8,128)(2,1)S(1)}, u32[]{:S(2)}, u32[]{:S(2)}) collective-permute-start(bf16[256,1024]{1,0:T(8,128)(2,1)S(1)} %get-tuple-element.40), channel_id=1, source_target_pairs={{0,1},{1,0},{2,3},{3,2},{4,5},{5,4},{6,7},{7,6},{8,9},{9,8},{10,11... | collective-permute-start | bytes 1572872 | tf_op jit(solution)/shard_map/ppermute | solution.py:232
  62.4 9.9 %collective-permute-start.23 = (bf16[128,512]{1,0:T(8,128)(2,1)S(1)}, bf16[128,512]{1,0:T(8,128)(2,1)S(1)}, u32[]{:S(2)}, u32[]{:S(2)}) collective-permute-start(bf16[128,512]{1,0:T(8,128)(2,1)S(1)} %get-tuple-element.51), channel_id=1, source_target_pairs={{0,8},{1,9},{2,10},{3,11},{4,12},{5,13},{6,14},{7,15},{8,0},{9,1},... | collective-permute-start | bytes 393224 | tf_op jit(solution)/shard_map/ppermute | solution.py:232
  66.0 9.5 %collective-permute-start.19 = (bf16[256,512]{1,0:T(8,128)(2,1)S(1)}, bf16[256,512]{1,0:T(8,128)(2,1)S(1)}, u32[]{:S(2)}, u32[]{:S(2)}) collective-permute-start(bf16[256,512]{1,0:T(8,128)(2,1)S(1)} %get-tuple-element.42), channel_id=1, source_target_pairs={{0,2},{1,3},{2,0},{3,1},{4,6},{5,7},{6,4},{7,5},{8,10},{9,11},{10,... | collective-permute-start | bytes 786440 | tf_op jit(solution)/shard_map/ppermute | solution.py:232
  66.3 9.1 %collective-permute-start.25 = (bf16[128,512]{1,0:T(8,128)(2,1)S(1)}, bf16[128,512]{1,0:T(8,128)(2,1)S(1)}, u32[]{:S(2)}, u32[]{:S(2)}) collective-permute-start(bf16[128,512]{1,0:T(8,128)(2,1)S(1)} %get-tuple-element.52), channel_id=1, source_target_pairs={{0,8},{1,9},{2,10},{3,11},{4,12},{5,13},{6,14},{7,15},{8,0},{9,1},... | collective-permute-start | bytes 393224 | tf_op jit(solution)/shard_map/ppermute | solution.py:232
  72.4 6.4 %collective-permute-start.26 = (bf16[256,512]{1,0:T(8,128)(2,1)S(1)}, bf16[256,512]{1,0:T(8,128)(2,1)S(1)}, u32[]{:S(2)}, u32[]{:S(2)}) collective-permute-start(bf16[256,512]{1,0:T(8,128)(2,1)S(1)} %add_convert_fusion.1), channel_id=1, source_target_pairs={{0,4},{1,5},{2,6},{3,7},{4,0},{5,1},{6,2},{7,3},{8,12},{9,13},{10,... | collective-permute-start | bytes 786440 | tf_op jit(solution)/shard_map/ppermute | solution.py:232

commit v6 on v5

--- a/solution.py
+++ b/solution.py
@@ -9,8 +9,8 @@
 
 BF16, F32 = jnp.bfloat16, jnp.float32
 TILE = 256
-VMEM = 10 * 2**20
-COST = 2e8
+VMEM = 7 * 2**20
+COST = 5e7
 
 
 def contract_last(left, right):
@@ -92,12 +92,11 @@
 
 
 def hidden_body(shards, given, *refs):
-    first, held, last, soon, fetch = given
+    first, held, last, fetch = given
     refs, parts = list(refs), len(shards)
     pieces, w_down, rest = refs[:parts], refs[parts], refs[parts + 1 :]
     before = None if first else rest.pop(0)
     scale = [rest.pop(0), rest.pop(0)] if last else None
-    del rest[:soon]
     outs = [rest.pop(0)] + ([rest.pop(0)] if last or fetch else [])
     acts, piece_sem = rest.pop(0), rest.pop(0)
     width = pieces[0].shape[1]
@@ -141,7 +140,7 @@
         each(later, count, "wait")
 
 
-def hidden(pieces, w_down, total=None, scale=None, soon=(), fetch=(), held=False):
+def hidden(pieces, w_down, total=None, scale=None, fetch=(), held=False):
     shards, pieces = zip(*pieces)
     tok, width = pieces[0].shape
     ff = w_down.shape[0]
@@ -154,14 +153,13 @@
         outs = [jax.ShapeDtypeStruct((tok, ff), BF16)] * 2
     else:
         outs = [jax.ShapeDtypeStruct((tok, ff), F32)]
-    ins, args = ins + [pltpu.VMEM] * len(soon), (*args, *soon)
     scratch = [pltpu.VMEM((tok, parts * width), BF16), pltpu.SemaphoreType.DMA((parts,))]
     if not held:
         scratch += [pltpu.VMEM((ff, parts * width), BF16), pltpu.SemaphoreType.DMA((ff // TILE, parts))]
     if fetch:
         outs += [pltpu.VMEM((ff, len(fetch) * width), BF16)]
         scratch += [pltpu.SemaphoreType.DMA((ff // TILE, len(fetch)))]
-    given = (total is None, held, scale is not None, len(soon), tuple(fetch))
+    given = (total is None, held, scale is not None, tuple(fetch))
     return call(functools.partial(hidden_body, shards, given), ins, outs, args, scratch, 3.0)
 
 
@@ -265,17 +263,16 @@
     far_pair = move(far, pair)
     mid_both = move(mid_row, pair)
     last = [(MID, 1, 1), (FAR, 0, 1), (FAR, 1, 0), (FAR, 1, 1)]
-    (total,) = hidden(
+    total, held = hidden(
         [((NEAR, 1, 1), near_both), ((MID, 0, 1), mid_pair), ((MID, 1, 0), mid_row), ((FAR, 0, 0), far)],
         w_down,
         total,
-        soon=weights,
-
+        fetch=last,
     )
 
     far_row = after(far_row, total)
     far_both = move(far_row, pair)
-    grads = hidden(list(zip(last, (mid_both, far_pair, far_row, far_both))), w_down, total, scale)
+    grads = hidden(list(zip(last, (mid_both, far_pair, far_row, far_both))), held, total, scale, held=True)
 
     step = functools.partial(sums, grads, weights, width)
     (sent_far,) = step(sent=FAR)

time: 79.8 us -> 79 us (0.990)
  Pallas kernels: 29.2 us -> 27.5 us
  waiting for transfers between devices: 28.3 us -> 29.6 us
    pallas_call x11, Pallas kernels: 29.2 us -> 27.5 us  [call(): pl.pallas_call(body, in_specs=[pl.BlockSpec(memory_space=space) for space...]
    ppermute x27, waiting for transfers between devices: 28.3 us -> 29.6 us  [move(): return lax.ppermute(x, 'wid', [(i, i ^ bits) for i in range(n)])]
where the time goes in v6:
time: 79 us; the launch traced here: 78.9 us
  waiting for transfers between devices  29.6 us (37%)
  Pallas kernels  27.5 us (35%)
  starting transfers between devices  20 us (25%)
  other arithmetic  1.4 us (2%)
    ppermute x27, waiting for transfers between devices, move(): return lax.ppermute(x, 'wid', [(i, i ^ bits) for i in range(n)])  29.6 us
    pallas_call x11, Pallas kernels, call(): pl.pallas_call(body, in_specs=[pl.BlockSpec(memory_space=space) for space...  27.5 us
    ppermute x27, starting transfers between devices, move(): return lax.ppermute(x, 'wid', [(i, i ^ bits) for i in range(n)])  20 us
  transfers between devices with their start and end apart: 27, of which 13 were waited for; matrix products, arithmetic and copies ran while one was open for 1% of the time, Pallas kernels for 28%

profile of v6, /device:TPU:0, one launch (start us, length us, event | category | flops | bytes accessed | tf_op | source)
XLA Modules:
  0.0 78.9 jit_solution(6319486113104764636)
XLA Ops:
  0.0 3.0 %collective-permute-start.3 = (bf16[256,512]{1,0:T(8,128)(2,1)}, bf16[256,512]{1,0:T(8,128)(2,1)S(1)}, u32[]{:S(2)}, u32[]{:S(2)}) collective-permute-start(bf16[256,512]{1,0:T(8,128)(2,1)} %refs_0_.1), channel_id=1, source_target_pairs={{0,4},{1,5},{2,6},{3,7},{4,0},{5,1},{6,2},{7,3},{8,12},{9,13},{10,... | collective-permute-start | bytes 786440 | tf_op jit(solution)/shard_map/ppermute | solution.py:230
  3.0 1.5 %collective-permute-start.2 = (bf16[256,512]{1,0:T(8,128)(2,1)}, bf16[256,512]{1,0:T(8,128)(2,1)S(1)}, u32[]{:S(2)}, u32[]{:S(2)}) collective-permute-start(bf16[256,512]{1,0:T(8,128)(2,1)} %refs_0_.1), channel_id=1, source_target_pairs={{0,2},{1,3},{2,0},{3,1},{4,6},{5,7},{6,4},{7,5},{8,10},{9,11},{10,... | collective-permute-start | bytes 786440 | tf_op jit(solution)/shard_map/ppermute | solution.py:230
  4.5 0.0 collective-permute-start.1
  4.5 2.6 %collective-permute-start = (bf16[256,512]{1,0:T(8,128)(2,1)}, bf16[256,512]{1,0:T(8,128)(2,1)S(1)}, u32[]{:S(2)}, u32[]{:S(2)}) collective-permute-start(bf16[256,512]{1,0:T(8,128)(2,1)} %refs_0_.1), channel_id=1, source_target_pairs={{0,8},{1,9},{2,10},{3,11},{4,12},{5,13},{6,14},{7,15},{8,0},{9,1},... | collective-permute-start | bytes 786440 | tf_op jit(solution)/shard_map/ppermute | solution.py:230
  7.1 1.8 %shard_map.64 = (f32[256,1024]{1,0:T(8,128)S(1)}, f32[256,1024]{1,0:T(8,128)S(1)}) custom-call(bf16[256,1024]{1,0:T(8,128)(2,1)} %gate.1, bf16[256,1024]{1,0:T(8,128)(2,1)} %up.1), custom_call_target="tpu_custom_call" | custom-call | flops 50000000 | tf_op jit(solution)/shard_map/pallas_call | solution.py:30
  8.9 3.1 %collective-permute-done.3.refs_3_ = bf16[256,512]{1,0:T(8,128)(2,1)S(1)} collective-permute-done((bf16[256,512]{1,0:T(8,128)(2,1)}, bf16[256,512]{1,0:T(8,128)(2,1)S(1)}, u32[]{:S(2)}, u32[]{:S(2)}) %collective-permute-start.3) | collective-permute-done | bytes 262176 | tf_op jit(solution)/shard_map/ppermute | solution.py:230
  12.1 3.2 %collective-permute-start.9 = (bf16[256,512]{1,0:T(8,128)(2,1)S(1)}, bf16[256,512]{1,0:T(8,128)(2,1)S(1)}, u32[]{:S(2)}, u32[]{:S(2)}) collective-permute-start(bf16[256,512]{1,0:T(8,128)(2,1)S(1)} %collective-permute-done.3.refs_3_), channel_id=1, source_target_pairs={{0,2},{1,3},{2,0},{3,1},{4,6},{5,7},{6,4},{7,5},{8,10},{9,11},{10,... | collective-permute-start | bytes 786440 | tf_op jit(solution)/shard_map/ppermute | solution.py:230
  15.3 0.0 collective-permute-start.8
  15.3 0.5 collective-permute-start.7
  15.8 3.4 %shard_map.65.refs_5_ = f32[256,1024]{1,0:T(8,128)S(1)} custom-call(bf16[256,512]{1,0:T(8,128)(2,1)} %refs_0_.1, bf16[256,512]{1,0:T(8,128)(2,1)S(1)} %collective-permute-done.1.refs_1_, bf16[256,512]{1,0:T(8,128)(2,1)S(1)} %collective-permute-done.2.refs_2_, bf16[256,512]{1,0:T(8,128)(2,1)S(1)} %collective-permute-done.3.refs_3_, bf16[1024,8192]{1,0:T(8,128)(2,1)} %refs_4_.5), custom_call_target="tpu_custom_call" | custom-call | flops 150000000 | tf_op jit(solution)/shard_map/pallas_call | solution.py:30
  19.2 0.9 %collective-permute-done.refs_3_ = bf16[256,512]{1,0:T(8,128)(2,1)S(1)} collective-permute-done((bf16[256,512]{1,0:T(8,128)(2,1)}, bf16[256,512]{1,0:T(8,128)(2,1)S(1)}, u32[]{:S(2)}, u32[]{:S(2)}) %collective-permute-start) | collective-permute-done | bytes 262176 | tf_op jit(solution)/shard_map/ppermute | solution.py:230
  20.0 0.5 collective-permute-start.4
  20.5 0.0 collective-permute-done.9.refs_2_
  20.6 0.0 collective-permute-start.13
  20.6 0.0 collective-permute-done.8.refs_1_
  20.6 0.5 collective-permute-start.12
  21.1 0.0 collective-permute-done.7.refs_0_
  21.1 0.0 slice-start.5
  21.1 3.5 %shard_map.66.refs_5_ = f32[256,1024]{1,0:T(8,128)S(1)} custom-call(bf16[256,512]{1,0:T(8,128)(2,1)S(1)} %collective-permute-done.7.refs_0_, bf16[256,512]{1,0:T(8,128)(2,1)S(1)} %collective-permute-done.8.refs_1_, bf16[256,512]{1,0:T(8,128)(2,1)S(1)} %collective-permute-done.9.refs_2_, bf16[256,512]{1,0:T(8,128)(2,1)S(1)} %collective-permute-done.refs_3_, ...), custom_call_target="tpu_custom_call" | custom-call | flops 150000000 | tf_op jit(solution)/shard_map/pallas_call | solution.py:30
  24.6 0.0 slice-start.2
  24.6 0.0 slice-start.6
  24.7 0.0 slice-start.7
  24.7 3.3 %collective-permute-done.6.refs_3_ = bf16[256,512]{1,0:T(8,128)(2,1)S(1)} collective-permute-done((bf16[256,512]{1,0:T(8,128)(2,1)S(1)}, bf16[256,512]{1,0:T(8,128)(2,1)S(1)}, u32[]{:S(2)}, u32[]{:S(2)}) %collective-permute-start.6) | collective-permute-done | bytes 262176 | tf_op jit(solution)/shard_map/ppermute | solution.py:230
  28.0 0.5 collective-permute-start.11
  28.5 0.0 collective-permute-start.10
  28.5 0.0 collective-permute-done.4.refs_2_
  28.5 0.5 collective-permute-start.5
  29.0 0.0 collective-permute-done.13.refs_1_
  29.0 4.7 %shard_map.67 = (f32[256,1024]{1,0:T(8,128)S(1)}, bf16[1024,2048]{1,0:T(8,128)(2,1)S(1)}) custom-call(bf16[256,512]{1,0:T(8,128)(2,1)S(1)} %collective-permute-done.12.refs_0_, bf16[256,512]{1,0:T(8,128)(2,1)S(1)} %collective-permute-done.13.refs_1_, bf16[256,512]{1,0:T(8,128)(2,1)S(1)} %collective-permute-done.4.refs_2_, ...), custom_call_target="tpu_custom_call" | custom-call | flops 150000000 | tf_op jit(solution)/shard_map/pallas_call | solution.py:30
  33.7 1.4 %collective-permute-done.11.refs_2_ = bf16[256,512]{1,0:T(8,128)(2,1)S(1)} collective-permute-done((bf16[256,512]{1,0:T(8,128)(2,1)S(1)}, bf16[256,512]{1,0:T(8,128)(2,1)S(1)}, u32[]{:S(2)}, u32[]{:S(2)}) %collective-permute-start.11) | collective-permute-done | bytes 262176 | tf_op jit(solution)/shard_map/ppermute | solution.py:230
  35.0 1.5 %collective-permute-done.14.refs_3_ = bf16[256,512]{1,0:T(8,128)(2,1)S(1)} collective-permute-done((bf16[256,512]{1,0:T(8,128)(2,1)S(1)}, bf16[256,512]{1,0:T(8,128)(2,1)S(1)}, u32[]{:S(2)}, u32[]{:S(2)}) %collective-permute-start.14) | collective-permute-done | bytes 262176 | tf_op jit(solution)/shard_map/ppermute | solution.py:230
  36.6 2.0 %shard_map.68 = (bf16[256,1024]{1,0:T(8,128)(2,1)S(1)}, bf16[256,1024]{1,0:T(8,128)(2,1)S(1)}) custom-call(bf16[256,512]{1,0:T(8,128)(2,1)S(1)} %collective-permute-done.5.refs_0_, bf16[256,512]{1,0:T(8,128)(2,1)S(1)} %collective-permute-done.10.refs_1_, bf16[256,512]{1,0:T(8,128)(2,1)S(1)} %collective-permute-done.11.refs_2_, ...), custom_call_target="tpu_custom_call" | custom-call | flops 150000000 | tf_op jit(solution)/shard_map/pallas_call | solution.py:30
  38.7 1.5 %shard_map.70 = bf16[256,1024]{1,0:T(8,128)(2,1)S(1)} custom-call(bf16[256,1024]{1,0:T(8,128)(2,1)S(1)} %get-tuple-element.41.grad_gate, bf16[256,1024]{1,0:T(8,128)(2,1)S(1)} %get-tuple-element.42.grad_up, bf16[8192,1024]{1,0:T(8,128)(2,1)S(1)} %bitcast.1, bf16[8192,1024]{1,0:T(8,128)(2,1)S(1)} %bitcast.3), custom_call_target="tpu_custom_call" | custom-call | flops 37500000 | tf_op jit(solution)/shard_map/pallas_call | solution.py:30
  40.2 0.2 collective-permute-start.15
  40.4 1.5 %shard_map.69 = (f32[256,512]{1,0:T(8,128)S(1)}, f32[256,512]{1,0:T(8,128)S(1)}) custom-call(bf16[256,1024]{1,0:T(8,128)(2,1)S(1)} %get-tuple-element.41.grad_gate, bf16[256,1024]{1,0:T(8,128)(2,1)S(1)} %get-tuple-element.42.grad_up, bf16[8192,1024]{1,0:T(8,128)(2,1)S(1)} %bitcast.1, bf16[8192,1024]{1,0:T(8,128)(2,1)S(1)} %bitcast.3), custom_call_target="tpu_custom_call" | custom-call | flops 75000000 | tf_op jit(solution)/shard_map/pallas_call | solution.py:30
  41.9 0.2 collective-permute-done.15
  42.2 0.1 convert_element_type.39
  42.3 0.1 fusion.2
  42.4 1.5 %shard_map.71 = bf16[256,1024]{1,0:T(8,128)(2,1)S(1)} custom-call(bf16[256,1024]{1,0:T(8,128)(2,1)S(1)} %get-tuple-element.41.grad_gate, bf16[256,1024]{1,0:T(8,128)(2,1)S(1)} %get-tuple-element.42.grad_up, bf16[8192,1024]{1,0:T(8,128)(2,1)S(1)} %bitcast.1, bf16[8192,1024]{1,0:T(8,128)(2,1)S(1)} %bitcast.3), custom_call_target="tpu_custom_call" | custom-call | flops 37500000 | tf_op jit(solution)/shard_map/pallas_call | solution.py:30
  43.9 0.2 collective-permute-start.16
  44.1 0.5 collective-permute-start.21
  44.6 1.2 %collective-permute-done.16.refs_0_ = bf16[256,1024]{1,0:T(8,128)(2,1)S(1)} collective-permute-done((bf16[256,1024]{1,0:T(8,128)(2,1)S(1)}, bf16[256,1024]{1,0:T(8,128)(2,1)S(1)}, u32[]{:S(2)}, u32[]{:S(2)}) %collective-permute-start.16) | collective-permute-done | bytes 524320 | tf_op jit(solution)/shard_map/ppermute | solution.py:230
  45.9 3.0 %shard_map.72 = (f32[256,512]{1,0:T(8,128)S(1)}, bf16[256,512]{1,0:T(8,128)(2,1)S(1)}, bf16[256,1024]{1,0:T(8,128)(2,1)S(1)}) custom-call(bf16[256,1024]{1,0:T(8,128)(2,1)S(1)} %get-tuple-element.41.grad_gate, bf16[256,1024]{1,0:T(8,128)(2,1)S(1)} %get-tuple-element.42.grad_up, bf16[8192,1024]{1,0:T(8,128)(2,1)S(1)} %bitcast.1, ...), custom_call_target="tpu_custom_call" | custom-call | flops 112500000 | tf_op jit(solution)/shard_map/pallas_call | solution.py:30
  48.9 0.2 collective-permute-start.17
  49.1 0.5 collective-permute-start.20
  49.6 3.6 %collective-permute-done.21 = bf16[256,512]{1,0:T(8,128)(2,1)S(1)} collective-permute-done((bf16[256,512]{1,0:T(8,128)(2,1)S(1)}, bf16[256,512]{1,0:T(8,128)(2,1)S(1)}, u32[]{:S(2)}, u32[]{:S(2)}) %collective-permute-start.21) | collective-permute-done | bytes 262176 | tf_op jit(solution)/shard_map/ppermute | solution.py:230
  53.2 0.1 fusion.1
  53.4 0.7 collective-permute-start.22
  54.0 3.0 %shard_map.73 = (f32[256,512]{1,0:T(8,128)S(1)}, bf16[256,512]{1,0:T(8,128)(2,1)S(1)}, bf16[256,1024]{1,0:T(8,128)(2,1)S(1)}) custom-call(bf16[256,1024]{1,0:T(8,128)(2,1)S(1)} %get-tuple-element.41.grad_gate, bf16[256,1024]{1,0:T(8,128)(2,1)S(1)} %get-tuple-element.42.grad_up, bf16[8192,1024]{1,0:T(8,128)(2,1)S(1)} %bitcast.1, ...), custom_call_target="tpu_custom_call" | custom-call | flops 112500000 | tf_op jit(solution)/shard_map/pallas_call | solution.py:30
  57.1 1.0 %collective-permute-start.24 = (bf16[256,512]{1,0:T(8,128)(2,1)S(1)}, bf16[256,512]{1,0:T(8,128)(2,1)S(1)}, u32[]{:S(2)}, u32[]{:S(2)}) collective-permute-start(bf16[256,512]{1,0:T(8,128)(2,1)S(1)} %get-tuple-element.49), channel_id=1, source_target_pairs={{0,2},{1,3},{2,0},{3,1},{4,6},{5,7},{6,4},{7,5},{8,10},{9,11},{10,... | collective-permute-start | bytes 786440 | tf_op jit(solution)/shard_map/ppermute | solution.py:230
  58.1 0.2 collective-permute-done.20
  58.3 2.3 %collective-permute-done.22 = bf16[256,512]{1,0:T(8,128)(2,1)S(1)} collective-permute-done((bf16[256,512]{1,0:T(8,128)(2,1)S(1)}, bf16[256,512]{1,0:T(8,128)(2,1)S(1)}, u32[]{:S(2)}, u32[]{:S(2)}) %collective-permute-start.22) | collective-permute-done | bytes 262176 | tf_op jit(solution)/shard_map/ppermute | solution.py:230
  60.6 0.1 add_convert_fusion.2
  60.8 1.7 %collective-permute-start.23 = (bf16[128,512]{1,0:T(8,128)(2,1)S(1)}, bf16[128,512]{1,0:T(8,128)(2,1)S(1)}, u32[]{:S(2)}, u32[]{:S(2)}) collective-permute-start(bf16[128,512]{1,0:T(8,128)(2,1)S(1)} %get-tuple-element.55), channel_id=1, source_target_pairs={{0,8},{1,9},{2,10},{3,11},{4,12},{5,13},{6,14},{7,15},{8,0},{9,1},... | collective-permute-start | bytes 393224 | tf_op jit(solution)/shard_map/ppermute | solution.py:230
  62.5 1.6 %shard_map.74 = (f32[256,512]{1,0:T(8,128)S(1)}, bf16[256,512]{1,0:T(8,128)(2,1)S(1)}) custom-call(bf16[256,1024]{1,0:T(8,128)(2,1)S(1)} %get-tuple-element.41.grad_gate, bf16[256,1024]{1,0:T(8,128)(2,1)S(1)} %get-tuple-element.42.grad_up, bf16[8192,1024]{1,0:T(8,128)(2,1)S(1)} %bitcast.1, bf16[8192,1024]{1,0:T(8,128)(2,1)S(1)} %bitcast.3, ...), custom_call_target="tpu_custom_call" | custom-call | flops 75000000 | tf_op jit(solution)/shard_map/pallas_call | solution.py:30
  64.0 1.0 %collective-permute-start.19 = (bf16[256,512]{1,0:T(8,128)(2,1)S(1)}, bf16[256,512]{1,0:T(8,128)(2,1)S(1)}, u32[]{:S(2)}, u32[]{:S(2)}) collective-permute-start(bf16[256,512]{1,0:T(8,128)(2,1)S(1)} %get-tuple-element.46), channel_id=1, source_target_pairs={{0,2},{1,3},{2,0},{3,1},{4,6},{5,7},{6,4},{7,5},{8,10},{9,11},{10,... | collective-permute-start | bytes 786440 | tf_op jit(solution)/shard_map/ppermute | solution.py:230
  65.0 0.9 %collective-permute-start.25 = (bf16[128,512]{1,0:T(8,128)(2,1)S(1)}, bf16[128,512]{1,0:T(8,128)(2,1)S(1)}, u32[]{:S(2)}, u32[]{:S(2)}) collective-permute-start(bf16[128,512]{1,0:T(8,128)(2,1)S(1)} %get-tuple-element.56), channel_id=1, source_target_pairs={{0,8},{1,9},{2,10},{3,11},{4,12},{5,13},{6,14},{7,15},{8,0},{9,1},... | collective-permute-start | bytes 393224 | tf_op jit(solution)/shard_map/ppermute | solution.py:230
  65.9 5.7 %collective-permute-done.23 = bf16[128,512]{1,0:T(8,128)(2,1)S(1)} collective-permute-done((bf16[128,512]{1,0:T(8,128)(2,1)S(1)}, bf16[128,512]{1,0:T(8,128)(2,1)S(1)}, u32[]{:S(2)}, u32[]{:S(2)}) %collective-permute-start.23) | collective-permute-done | bytes 131104 | tf_op jit(solution)/shard_map/ppermute | solution.py:230
  71.6 0.1 add_convert_fusion.1
  71.7 0.2 collective-permute-start.26
  71.9 2.0 %collective-permute-done.25 = bf16[128,512]{1,0:T(8,128)(2,1)S(1)} collective-permute-done((bf16[128,512]{1,0:T(8,128)(2,1)S(1)}, bf16[128,512]{1,0:T(8,128)(2,1)S(1)}, u32[]{:S(2)}, u32[]{:S(2)}) %collective-permute-start.25) | collective-permute-done | bytes 131104 | tf_op jit(solution)/shard_map/ppermute | solution.py:230
  73.8 0.1 convert_add_fusion
  73.9 4.2 %collective-permute-done.26 = bf16[256,512]{1,0:T(8,128)(2,1)S(1)} collective-permute-done((bf16[256,512]{1,0:T(8,128)(2,1)S(1)}, bf16[256,512]{1,0:T(8,128)(2,1)S(1)}, u32[]{:S(2)}, u32[]{:S(2)}) %collective-permute-start.26) | collective-permute-done | bytes 262176 | tf_op jit(solution)/shard_map/ppermute | solution.py:230
  78.1 0.8 add_convert_fusion
  (27 shorter events, 0.1 us)
Async XLA Ops:
  0.0 12.0 %collective-permute-start.3 = (bf16[256,512]{1,0:T(8,128)(2,1)}, bf16[256,512]{1,0:T(8,128)(2,1)S(1)}, u32[]{:S(2)}, u32[]{:S(2)}) collective-permute-start(bf16[256,512]{1,0:T(8,128)(2,1)} %refs_0_.1), channel_id=1, source_target_pairs={{0,4},{1,5},{2,6},{3,7},{4,0},{5,1},{6,2},{7,3},{8,12},{9,13},{10,... | collective-permute-start | bytes 786440 | tf_op jit(solution)/shard_map/ppermute | solution.py:230
  3.0 12.2 %collective-permute-start.2 = (bf16[256,512]{1,0:T(8,128)(2,1)}, bf16[256,512]{1,0:T(8,128)(2,1)S(1)}, u32[]{:S(2)}, u32[]{:S(2)}) collective-permute-start(bf16[256,512]{1,0:T(8,128)(2,1)} %refs_0_.1), channel_id=1, source_target_pairs={{0,2},{1,3},{2,0},{3,1},{4,6},{5,7},{6,4},{7,5},{8,10},{9,11},{10,... | collective-permute-start | bytes 786440 | tf_op jit(solution)/shard_map/ppermute | solution.py:230
  4.5 11.2 %collective-permute-start.1 = (bf16[256,512]{1,0:T(8,128)(2,1)}, bf16[256,512]{1,0:T(8,128)(2,1)S(1)}, u32[]{:S(2)}, u32[]{:S(2)}) collective-permute-start(bf16[256,512]{1,0:T(8,128)(2,1)} %refs_0_.1), channel_id=1, source_target_pairs={{0,1},{1,0},{2,3},{3,2},{4,5},{5,4},{6,7},{7,6},{8,9},{9,8},{10,11... | collective-permute-start | bytes 786440 | tf_op jit(solution)/shard_map/ppermute | solution.py:230
  4.5 15.5 %collective-permute-start = (bf16[256,512]{1,0:T(8,128)(2,1)}, bf16[256,512]{1,0:T(8,128)(2,1)S(1)}, u32[]{:S(2)}, u32[]{:S(2)}) collective-permute-start(bf16[256,512]{1,0:T(8,128)(2,1)} %refs_0_.1), channel_id=1, source_target_pairs={{0,8},{1,9},{2,10},{3,11},{4,12},{5,13},{6,14},{7,15},{8,0},{9,1},... | collective-permute-start | bytes 786440 | tf_op jit(solution)/shard_map/ppermute | solution.py:230
  12.1 8.5 %collective-permute-start.9 = (bf16[256,512]{1,0:T(8,128)(2,1)S(1)}, bf16[256,512]{1,0:T(8,128)(2,1)S(1)}, u32[]{:S(2)}, u32[]{:S(2)}) collective-permute-start(bf16[256,512]{1,0:T(8,128)(2,1)S(1)} %collective-permute-done.3.refs_3_), channel_id=1, source_target_pairs={{0,2},{1,3},{2,0},{3,1},{4,6},{5,7},{6,4},{7,5},{8,10},{9,11},{10,... | collective-permute-start | bytes 786440 | tf_op jit(solution)/shard_map/ppermute | solution.py:230
  15.3 5.3 %collective-permute-start.8 = (bf16[256,512]{1,0:T(8,128)(2,1)S(1)}, bf16[256,512]{1,0:T(8,128)(2,1)S(1)}, u32[]{:S(2)}, u32[]{:S(2)}) collective-permute-start(bf16[256,512]{1,0:T(8,128)(2,1)S(1)} %collective-permute-done.3.refs_3_), channel_id=1, source_target_pairs={{0,1},{1,0},{2,3},{3,2},{4,5},{5,4},{6,7},{7,6},{8,9},{9,8},{10,11... | collective-permute-start | bytes 786440 | tf_op jit(solution)/shard_map/ppermute | solution.py:230
  15.3 5.8 %collective-permute-start.7 = (bf16[256,512]{1,0:T(8,128)(2,1)S(1)}, bf16[256,512]{1,0:T(8,128)(2,1)S(1)}, u32[]{:S(2)}, u32[]{:S(2)}) collective-permute-start(bf16[256,512]{1,0:T(8,128)(2,1)S(1)} %collective-permute-done.2.refs_2_), channel_id=1, source_target_pairs={{0,1},{1,0},{2,3},{3,2},{4,5},{5,4},{6,7},{7,6},{8,9},{9,8},{10,11... | collective-permute-start | bytes 786440 | tf_op jit(solution)/shard_map/ppermute | solution.py:230
  20.0 7.9 %collective-permute-start.6 = (bf16[256,512]{1,0:T(8,128)(2,1)S(1)}, bf16[256,512]{1,0:T(8,128)(2,1)S(1)}, u32[]{:S(2)}, u32[]{:S(2)}) collective-permute-start(bf16[256,512]{1,0:T(8,128)(2,1)S(1)} %collective-permute-done.refs_3_), channel_id=1, source_target_pairs={{0,4},{1,5},{2,6},{3,7},{4,0},{5,1},{6,2},{7,3},{8,12},{9,13},{10,... | collective-permute-start | bytes 786440 | tf_op jit(solution)/shard_map/ppermute | solution.py:230
  20.0 8.4 %collective-permute-start.4 = (bf16[256,512]{1,0:T(8,128)(2,1)S(1)}, bf16[256,512]{1,0:T(8,128)(2,1)S(1)}, u32[]{:S(2)}, u32[]{:S(2)}) collective-permute-start(bf16[256,512]{1,0:T(8,128)(2,1)S(1)} %collective-permute-done.refs_3_), channel_id=1, source_target_pairs={{0,2},{1,3},{2,0},{3,1},{4,6},{5,7},{6,4},{7,5},{8,10},{9,11},{10,... | collective-permute-start | bytes 786440 | tf_op jit(solution)/shard_map/ppermute | solution.py:230
  20.6 8.4 %collective-permute-start.13 = (bf16[256,512]{1,0:T(8,128)(2,1)S(1)}, bf16[256,512]{1,0:T(8,128)(2,1)S(1)}, u32[]{:S(2)}, u32[]{:S(2)}) collective-permute-start(bf16[256,512]{1,0:T(8,128)(2,1)S(1)} %collective-permute-done.refs_3_), channel_id=1, source_target_pairs={{0,1},{1,0},{2,3},{3,2},{4,5},{5,4},{6,7},{7,6},{8,9},{9,8},{10,11... | collective-permute-start | bytes 786440 | tf_op jit(solution)/shard_map/ppermute | solution.py:230
  20.6 8.4 %collective-permute-start.12 = (bf16[256,512]{1,0:T(8,128)(2,1)S(1)}, bf16[256,512]{1,0:T(8,128)(2,1)S(1)}, u32[]{:S(2)}, u32[]{:S(2)}) collective-permute-start(bf16[256,512]{1,0:T(8,128)(2,1)S(1)} %collective-permute-done.9.refs_2_), channel_id=1, source_target_pairs={{0,1},{1,0},{2,3},{3,2},{4,5},{5,4},{6,7},{7,6},{8,9},{9,8},{10,11... | collective-permute-start | bytes 786440 | tf_op jit(solution)/shard_map/ppermute | solution.py:230
  21.1 17.5 %slice-start = ((s8[16777216]{0:T(1024)(128)(4,1)}), s8[4194304]{0:T(1024)(128)(4,1)S(1)}, s32[]{:S(2)}) async-start(s8[16777216]{0:T(1024)(128)(4,1)} %bitcast), calls=%async_computation | async-start | bytes 8388608
  21.1 17.5 %slice-start.1 = ((s8[16777216]{0:T(1024)(128)(4,1)}), s8[4194304]{0:T(1024)(128)(4,1)S(1)}, s32[]{:S(2)}) async-start(s8[16777216]{0:T(1024)(128)(4,1)} %bitcast), calls=%async_computation.1 | async-start | bytes 8388608
  21.1 17.5 %slice-start.4 = ((s8[16777216]{0:T(1024)(128)(4,1)}), s8[4194304]{0:T(1024)(128)(4,1)S(1)}, s32[]{:S(2)}) async-start(s8[16777216]{0:T(1024)(128)(4,1)} %bitcast.2), calls=%async_computation.4 | async-start | bytes 8388608
  21.1 17.5 %slice-start.5 = ((s8[16777216]{0:T(1024)(128)(4,1)}), s8[4194304]{0:T(1024)(128)(4,1)S(1)}, s32[]{:S(2)}) async-start(s8[16777216]{0:T(1024)(128)(4,1)} %bitcast.2), calls=%async_computation.5 | async-start | bytes 8388608
  24.6 14.0 %slice-start.2 = ((s8[16777216]{0:T(1024)(128)(4,1)}), s8[4194304]{0:T(1024)(128)(4,1)S(1)}, s32[]{:S(2)}) async-start(s8[16777216]{0:T(1024)(128)(4,1)} %bitcast), calls=%async_computation.2 | async-start | bytes 8388608
  24.6 14.0 %slice-start.3 = ((s8[16777216]{0:T(1024)(128)(4,1)}), s8[4194304]{0:T(1024)(128)(4,1)S(1)}, s32[]{:S(2)}) async-start(s8[16777216]{0:T(1024)(128)(4,1)} %bitcast), calls=%async_computation.3 | async-start | bytes 8388608
  24.6 14.0 %slice-start.6 = ((s8[16777216]{0:T(1024)(128)(4,1)}), s8[4194304]{0:T(1024)(128)(4,1)S(1)}, s32[]{:S(2)}) async-start(s8[16777216]{0:T(1024)(128)(4,1)} %bitcast.2), calls=%async_computation.6 | async-start | bytes 8388608
  24.7 14.0 %slice-start.7 = ((s8[16777216]{0:T(1024)(128)(4,1)}), s8[4194304]{0:T(1024)(128)(4,1)S(1)}, s32[]{:S(2)}) async-start(s8[16777216]{0:T(1024)(128)(4,1)} %bitcast.2), calls=%async_computation.7 | async-start | bytes 8388608
  28.0 7.0 %collective-permute-start.11 = (bf16[256,512]{1,0:T(8,128)(2,1)S(1)}, bf16[256,512]{1,0:T(8,128)(2,1)S(1)}, u32[]{:S(2)}, u32[]{:S(2)}) collective-permute-start(bf16[256,512]{1,0:T(8,128)(2,1)S(1)} %collective-permute-done.6.refs_3_), channel_id=1, source_target_pairs={{0,2},{1,3},{2,0},{3,1},{4,6},{5,7},{6,4},{7,5},{8,10},{9,11},{10,... | collective-permute-start | bytes 786440 | tf_op jit(solution)/shard_map/ppermute | solution.py:230
  28.5 6.5 %collective-permute-start.10 = (bf16[256,512]{1,0:T(8,128)(2,1)S(1)}, bf16[256,512]{1,0:T(8,128)(2,1)S(1)}, u32[]{:S(2)}, u32[]{:S(2)}) collective-permute-start(bf16[256,512]{1,0:T(8,128)(2,1)S(1)} %collective-permute-done.6.refs_3_), channel_id=1, source_target_pairs={{0,1},{1,0},{2,3},{3,2},{4,5},{5,4},{6,7},{7,6},{8,9},{9,8},{10,11... | collective-permute-start | bytes 786440 | tf_op jit(solution)/shard_map/ppermute | solution.py:230
  28.5 6.5 %collective-permute-start.5 = (bf16[256,512]{1,0:T(8,128)(2,1)S(1)}, bf16[256,512]{1,0:T(8,128)(2,1)S(1)}, u32[]{:S(2)}, u32[]{:S(2)}) collective-permute-start(bf16[256,512]{1,0:T(8,128)(2,1)S(1)} %collective-permute-done.4.refs_2_), channel_id=1, source_target_pairs={{0,1},{1,0},{2,3},{3,2},{4,5},{5,4},{6,7},{7,6},{8,9},{9,8},{10,11... | collective-permute-start | bytes 786440 | tf_op jit(solution)/shard_map/ppermute | solution.py:230
  35.0 1.5 %collective-permute-start.14 = (bf16[256,512]{1,0:T(8,128)(2,1)S(1)}, bf16[256,512]{1,0:T(8,128)(2,1)S(1)}, u32[]{:S(2)}, u32[]{:S(2)}) collective-permute-start(bf16[256,512]{1,0:T(8,128)(2,1)S(1)} %collective-permute-done.11.refs_2_), channel_id=1, source_target_pairs={{0,1},{1,0},{2,3},{3,2},{4,5},{5,4},{6,7},{7,6},{8,9},{9,8},{10,11... | collective-permute-start | bytes 786440 | tf_op jit(solution)/shard_map/ppermute | solution.py:230
  40.2 2.0 %collective-permute-start.15 = (bf16[256,1024]{1,0:T(8,128)(2,1)S(1)}, bf16[256,1024]{1,0:T(8,128)(2,1)S(1)}, u32[]{:S(2)}, u32[]{:S(2)}) collective-permute-start(bf16[256,1024]{1,0:T(8,128)(2,1)S(1)} %shard_map.70), channel_id=1, source_target_pairs={{0,1},{1,0},{2,3},{3,2},{4,5},{5,4},{6,7},{7,6},{8,9},{9,8},{10,11... | collective-permute-start | bytes 1572872 | tf_op jit(solution)/shard_map/ppermute | solution.py:230
  43.9 2.0 %collective-permute-start.16 = (bf16[256,1024]{1,0:T(8,128)(2,1)S(1)}, bf16[256,1024]{1,0:T(8,128)(2,1)S(1)}, u32[]{:S(2)}, u32[]{:S(2)}) collective-permute-start(bf16[256,1024]{1,0:T(8,128)(2,1)S(1)} %shard_map.71), channel_id=1, source_target_pairs={{0,1},{1,0},{2,3},{3,2},{4,5},{5,4},{6,7},{7,6},{8,9},{9,8},{10,11... | collective-permute-start | bytes 1572872 | tf_op jit(solution)/shard_map/ppermute | solution.py:230
  44.1 9.1 %collective-permute-start.21 = (bf16[256,512]{1,0:T(8,128)(2,1)S(1)}, bf16[256,512]{1,0:T(8,128)(2,1)S(1)}, u32[]{:S(2)}, u32[]{:S(2)}) collective-permute-start(bf16[256,512]{1,0:T(8,128)(2,1)S(1)} %fusion.2), channel_id=1, source_target_pairs={{0,2},{1,3},{2,0},{3,1},{4,6},{5,7},{6,4},{7,5},{8,10},{9,11},{10,... | collective-permute-start | bytes 786440 | tf_op jit(solution)/shard_map/ppermute | solution.py:230
  48.9 5.1 %collective-permute-start.17 = (bf16[256,1024]{1,0:T(8,128)(2,1)S(1)}, bf16[256,1024]{1,0:T(8,128)(2,1)S(1)}, u32[]{:S(2)}, u32[]{:S(2)}) collective-permute-start(bf16[256,1024]{1,0:T(8,128)(2,1)S(1)} %get-tuple-element.43), channel_id=1, source_target_pairs={{0,1},{1,0},{2,3},{3,2},{4,5},{5,4},{6,7},{7,6},{8,9},{9,8},{10,11... | collective-permute-start | bytes 1572872 | tf_op jit(solution)/shard_map/ppermute | solution.py:230
  49.1 9.2 %collective-permute-start.20 = (bf16[256,512]{1,0:T(8,128)(2,1)S(1)}, bf16[256,512]{1,0:T(8,128)(2,1)S(1)}, u32[]{:S(2)}, u32[]{:S(2)}) collective-permute-start(bf16[256,512]{1,0:T(8,128)(2,1)S(1)} %get-tuple-element.48), channel_id=1, source_target_pairs={{0,2},{1,3},{2,0},{3,1},{4,6},{5,7},{6,4},{7,5},{8,10},{9,11},{10,... | collective-permute-start | bytes 786440 | tf_op jit(solution)/shard_map/ppermute | solution.py:230
  53.4 7.3 %collective-permute-start.22 = (bf16[256,512]{1,0:T(8,128)(2,1)S(1)}, bf16[256,512]{1,0:T(8,128)(2,1)S(1)}, u32[]{:S(2)}, u32[]{:S(2)}) collective-permute-start(bf16[256,512]{1,0:T(8,128)(2,1)S(1)} %fusion.1), channel_id=1, source_target_pairs={{0,4},{1,5},{2,6},{3,7},{4,0},{5,1},{6,2},{7,3},{8,12},{9,13},{10,... | collective-permute-start | bytes 786440 | tf_op jit(solution)/shard_map/ppermute | solution.py:230
  57.1 14.5 %collective-permute-start.24 = (bf16[256,512]{1,0:T(8,128)(2,1)S(1)}, bf16[256,512]{1,0:T(8,128)(2,1)S(1)}, u32[]{:S(2)}, u32[]{:S(2)}) collective-permute-start(bf16[256,512]{1,0:T(8,128)(2,1)S(1)} %get-tuple-element.49), channel_id=1, source_target_pairs={{0,2},{1,3},{2,0},{3,1},{4,6},{5,7},{6,4},{7,5},{8,10},{9,11},{10,... | collective-permute-start | bytes 786440 | tf_op jit(solution)/shard_map/ppermute | solution.py:230
  58.3 4.2 %collective-permute-start.18 = (bf16[256,1024]{1,0:T(8,128)(2,1)S(1)}, bf16[256,1024]{1,0:T(8,128)(2,1)S(1)}, u32[]{:S(2)}, u32[]{:S(2)}) collective-permute-start(bf16[256,1024]{1,0:T(8,128)(2,1)S(1)} %get-tuple-element.44), channel_id=1, source_target_pairs={{0,1},{1,0},{2,3},{3,2},{4,5},{5,4},{6,7},{7,6},{8,9},{9,8},{10,11... | collective-permute-start | bytes 1572872 | tf_op jit(solution)/shard_map/ppermute | solution.py:230
  60.8 10.8 %collective-permute-start.23 = (bf16[128,512]{1,0:T(8,128)(2,1)S(1)}, bf16[128,512]{1,0:T(8,128)(2,1)S(1)}, u32[]{:S(2)}, u32[]{:S(2)}) collective-permute-start(bf16[128,512]{1,0:T(8,128)(2,1)S(1)} %get-tuple-element.55), channel_id=1, source_target_pairs={{0,8},{1,9},{2,10},{3,11},{4,12},{5,13},{6,14},{7,15},{8,0},{9,1},... | collective-permute-start | bytes 393224 | tf_op jit(solution)/shard_map/ppermute | solution.py:230
  64.0 9.8 %collective-permute-start.19 = (bf16[256,512]{1,0:T(8,128)(2,1)S(1)}, bf16[256,512]{1,0:T(8,128)(2,1)S(1)}, u32[]{:S(2)}, u32[]{:S(2)}) collective-permute-start(bf16[256,512]{1,0:T(8,128)(2,1)S(1)} %get-tuple-element.46), channel_id=1, source_target_pairs={{0,2},{1,3},{2,0},{3,1},{4,6},{5,7},{6,4},{7,5},{8,10},{9,11},{10,... | collective-permute-start | bytes 786440 | tf_op jit(solution)/shard_map/ppermute | solution.py:230
  65.0 8.8 %collective-permute-start.25 = (bf16[128,512]{1,0:T(8,128)(2,1)S(1)}, bf16[128,512]{1,0:T(8,128)(2,1)S(1)}, u32[]{:S(2)}, u32[]{:S(2)}) collective-permute-start(bf16[128,512]{1,0:T(8,128)(2,1)S(1)} %get-tuple-element.56), channel_id=1, source_target_pairs={{0,8},{1,9},{2,10},{3,11},{4,12},{5,13},{6,14},{7,15},{8,0},{9,1},... | collective-permute-start | bytes 393224 | tf_op jit(solution)/shard_map/ppermute | solution.py:230
  71.7 6.4 %collective-permute-start.26 = (bf16[256,512]{1,0:T(8,128)(2,1)S(1)}, bf16[256,512]{1,0:T(8,128)(2,1)S(1)}, u32[]{:S(2)}, u32[]{:S(2)}) collective-permute-start(bf16[256,512]{1,0:T(8,128)(2,1)S(1)} %add_convert_fusion.1), channel_id=1, source_target_pairs={{0,4},{1,5},{2,6},{3,7},{4,0},{5,1},{6,2},{7,3},{8,12},{9,13},{10,... | collective-permute-start | bytes 786440 | tf_op jit(solution)/shard_map/ppermute | solution.py:230

commit v7 on v6

--- a/solution.py
+++ b/solution.py
@@ -277,8 +277,8 @@
     step = functools.partial(sums, grads, weights, width)
     (sent_far,) = step(sent=FAR)
     far, cross_far = step(kept=FAR)
-    got_far = move(sent_far, pair).astype(F32)
-    far, cross_far = far + got_far[:, width:], (cross_far + got_far[:, :width]).astype(BF16)
+    got_far = move(sent_far, pair)
+    far, cross_far = far + got_far[:, width:].astype(F32), (cross_far + got_far[:, :width].astype(F32)).astype(BF16)
     (sent_mid,) = sums([after(grad, cross_far) for grad in grads], weights, width, sent=MID)
     mid, cross_mid, sent_near = step(kept=MID, got=move(sent_mid, pair), sent=NEAR)
     far = far + move(cross_far, row).astype(F32)

time: 79 us -> 79 us (level)
  no operation moved by 1% of the time
where the time goes in v7:
time: 79 us; the launch traced here: 78.9 us
  waiting for transfers between devices  29.8 us (38%)
  Pallas kernels  27.5 us (35%)
  starting transfers between devices  20 us (25%)
  other arithmetic  1.25 us (2%)
    ppermute x27, waiting for transfers between devices, move(): return lax.ppermute(x, 'wid', [(i, i ^ bits) for i in range(n)])  29.8 us
    pallas_call x11, Pallas kernels, call(): pl.pallas_call(body, in_specs=[pl.BlockSpec(memory_space=space) for space...  27.5 us
    ppermute x27, starting transfers between devices, move(): return lax.ppermute(x, 'wid', [(i, i ^ bits) for i in range(n)])  20 us
  transfers between devices with their start and end apart: 27, of which 13 were waited for; matrix products, arithmetic and copies ran while one was open for 1% of the time, Pallas kernels for 28%

profile of v7, /device:TPU:0, one launch (start us, length us, event | category | flops | bytes accessed | tf_op | source)
XLA Modules:
  0.0 78.9 jit_solution(16940674301612085042)
XLA Ops:
  0.0 3.0 %collective-permute-start.3 = (bf16[256,512]{1,0:T(8,128)(2,1)}, bf16[256,512]{1,0:T(8,128)(2,1)S(1)}, u32[]{:S(2)}, u32[]{:S(2)}) collective-permute-start(bf16[256,512]{1,0:T(8,128)(2,1)} %refs_0_.1), channel_id=1, source_target_pairs={{0,4},{1,5},{2,6},{3,7},{4,0},{5,1},{6,2},{7,3},{8,12},{9,13},{10,... | collective-permute-start | bytes 786440 | tf_op jit(solution)/shard_map/ppermute | solution.py:230
  3.0 1.5 %collective-permute-start.2 = (bf16[256,512]{1,0:T(8,128)(2,1)}, bf16[256,512]{1,0:T(8,128)(2,1)S(1)}, u32[]{:S(2)}, u32[]{:S(2)}) collective-permute-start(bf16[256,512]{1,0:T(8,128)(2,1)} %refs_0_.1), channel_id=1, source_target_pairs={{0,2},{1,3},{2,0},{3,1},{4,6},{5,7},{6,4},{7,5},{8,10},{9,11},{10,... | collective-permute-start | bytes 786440 | tf_op jit(solution)/shard_map/ppermute | solution.py:230
  4.5 2.6 %collective-permute-start = (bf16[256,512]{1,0:T(8,128)(2,1)}, bf16[256,512]{1,0:T(8,128)(2,1)S(1)}, u32[]{:S(2)}, u32[]{:S(2)}) collective-permute-start(bf16[256,512]{1,0:T(8,128)(2,1)} %refs_0_.1), channel_id=1, source_target_pairs={{0,8},{1,9},{2,10},{3,11},{4,12},{5,13},{6,14},{7,15},{8,0},{9,1},... | collective-permute-start | bytes 786440 | tf_op jit(solution)/shard_map/ppermute | solution.py:230
  7.1 1.8 %shard_map.64 = (f32[256,1024]{1,0:T(8,128)S(1)}, f32[256,1024]{1,0:T(8,128)S(1)}) custom-call(bf16[256,1024]{1,0:T(8,128)(2,1)} %gate.1, bf16[256,1024]{1,0:T(8,128)(2,1)} %up.1), custom_call_target="tpu_custom_call" | custom-call | flops 50000000 | tf_op jit(solution)/shard_map/pallas_call | solution.py:30
  8.9 3.1 %collective-permute-done.3.refs_3_ = bf16[256,512]{1,0:T(8,128)(2,1)S(1)} collective-permute-done((bf16[256,512]{1,0:T(8,128)(2,1)}, bf16[256,512]{1,0:T(8,128)(2,1)S(1)}, u32[]{:S(2)}, u32[]{:S(2)}) %collective-permute-start.3) | collective-permute-done | bytes 262176 | tf_op jit(solution)/shard_map/ppermute | solution.py:230
  12.1 3.2 %collective-permute-start.9 = (bf16[256,512]{1,0:T(8,128)(2,1)S(1)}, bf16[256,512]{1,0:T(8,128)(2,1)S(1)}, u32[]{:S(2)}, u32[]{:S(2)}) collective-permute-start(bf16[256,512]{1,0:T(8,128)(2,1)S(1)} %collective-permute-done.3.refs_3_), channel_id=1, source_target_pairs={{0,2},{1,3},{2,0},{3,1},{4,6},{5,7},{6,4},{7,5},{8,10},{9,11},{10,... | collective-permute-start | bytes 786440 | tf_op jit(solution)/shard_map/ppermute | solution.py:230
  15.3 0.5 collective-permute-start.7
  15.8 3.4 %shard_map.65.refs_5_ = f32[256,1024]{1,0:T(8,128)S(1)} custom-call(bf16[256,512]{1,0:T(8,128)(2,1)} %refs_0_.1, bf16[256,512]{1,0:T(8,128)(2,1)S(1)} %collective-permute-done.1.refs_1_, bf16[256,512]{1,0:T(8,128)(2,1)S(1)} %collective-permute-done.2.refs_2_, bf16[256,512]{1,0:T(8,128)(2,1)S(1)} %collective-permute-done.3.refs_3_, bf16[1024,8192]{1,0:T(8,128)(2,1)} %refs_4_.5), custom_call_target="tpu_custom_call" | custom-call | flops 150000000 | tf_op jit(solution)/shard_map/pallas_call | solution.py:30
  19.2 0.9 %collective-permute-done.refs_3_ = bf16[256,512]{1,0:T(8,128)(2,1)S(1)} collective-permute-done((bf16[256,512]{1,0:T(8,128)(2,1)}, bf16[256,512]{1,0:T(8,128)(2,1)S(1)}, u32[]{:S(2)}, u32[]{:S(2)}) %collective-permute-start) | collective-permute-done | bytes 262176 | tf_op jit(solution)/shard_map/ppermute | solution.py:230
  20.0 0.0 collective-permute-start.6
  20.0 0.5 collective-permute-start.4
  20.5 0.0 collective-permute-done.9.refs_2_
  20.6 0.0 collective-permute-start.13
  20.6 0.5 collective-permute-start.12
  21.1 0.0 collective-permute-done.7.refs_0_
  21.1 0.0 slice-start.5
  21.1 3.5 %shard_map.66.refs_5_ = f32[256,1024]{1,0:T(8,128)S(1)} custom-call(bf16[256,512]{1,0:T(8,128)(2,1)S(1)} %collective-permute-done.7.refs_0_, bf16[256,512]{1,0:T(8,128)(2,1)S(1)} %collective-permute-done.8.refs_1_, bf16[256,512]{1,0:T(8,128)(2,1)S(1)} %collective-permute-done.9.refs_2_, bf16[256,512]{1,0:T(8,128)(2,1)S(1)} %collective-permute-done.refs_3_, ...), custom_call_target="tpu_custom_call" | custom-call | flops 150000000 | tf_op jit(solution)/shard_map/pallas_call | solution.py:30
  24.6 0.0 slice-start.2
  24.6 0.0 slice-start.6
  24.7 0.0 slice-start.7
  24.7 3.3 %collective-permute-done.6.refs_3_ = bf16[256,512]{1,0:T(8,128)(2,1)S(1)} collective-permute-done((bf16[256,512]{1,0:T(8,128)(2,1)S(1)}, bf16[256,512]{1,0:T(8,128)(2,1)S(1)}, u32[]{:S(2)}, u32[]{:S(2)}) %collective-permute-start.6) | collective-permute-done | bytes 262176 | tf_op jit(solution)/shard_map/ppermute | solution.py:230
  28.0 0.5 collective-permute-start.11
  28.5 0.0 collective-permute-start.10
  28.5 0.0 collective-permute-done.4.refs_2_
  28.5 0.5 collective-permute-start.5
  29.0 0.0 collective-permute-done.13.refs_1_
  29.0 0.0 collective-permute-done.12.refs_0_
  29.0 4.7 %shard_map.67 = (f32[256,1024]{1,0:T(8,128)S(1)}, bf16[1024,2048]{1,0:T(8,128)(2,1)S(1)}) custom-call(bf16[256,512]{1,0:T(8,128)(2,1)S(1)} %collective-permute-done.12.refs_0_, bf16[256,512]{1,0:T(8,128)(2,1)S(1)} %collective-permute-done.13.refs_1_, bf16[256,512]{1,0:T(8,128)(2,1)S(1)} %collective-permute-done.4.refs_2_, ...), custom_call_target="tpu_custom_call" | custom-call | flops 150000000 | tf_op jit(solution)/shard_map/pallas_call | solution.py:30
  33.7 1.4 %collective-permute-done.11.refs_2_ = bf16[256,512]{1,0:T(8,128)(2,1)S(1)} collective-permute-done((bf16[256,512]{1,0:T(8,128)(2,1)S(1)}, bf16[256,512]{1,0:T(8,128)(2,1)S(1)}, u32[]{:S(2)}, u32[]{:S(2)}) %collective-permute-start.11) | collective-permute-done | bytes 262176 | tf_op jit(solution)/shard_map/ppermute | solution.py:230
  35.0 0.0 collective-permute-start.14
  35.0 1.5 %collective-permute-done.14.refs_3_ = bf16[256,512]{1,0:T(8,128)(2,1)S(1)} collective-permute-done((bf16[256,512]{1,0:T(8,128)(2,1)S(1)}, bf16[256,512]{1,0:T(8,128)(2,1)S(1)}, u32[]{:S(2)}, u32[]{:S(2)}) %collective-permute-start.14) | collective-permute-done | bytes 262176 | tf_op jit(solution)/shard_map/ppermute | solution.py:230
  36.6 2.0 %shard_map.68 = (bf16[256,1024]{1,0:T(8,128)(2,1)S(1)}, bf16[256,1024]{1,0:T(8,128)(2,1)S(1)}) custom-call(bf16[256,512]{1,0:T(8,128)(2,1)S(1)} %collective-permute-done.5.refs_0_, bf16[256,512]{1,0:T(8,128)(2,1)S(1)} %collective-permute-done.10.refs_1_, bf16[256,512]{1,0:T(8,128)(2,1)S(1)} %collective-permute-done.11.refs_2_, ...), custom_call_target="tpu_custom_call" | custom-call | flops 150000000 | tf_op jit(solution)/shard_map/pallas_call | solution.py:30
  38.7 1.5 %shard_map.70 = bf16[256,1024]{1,0:T(8,128)(2,1)S(1)} custom-call(bf16[256,1024]{1,0:T(8,128)(2,1)S(1)} %get-tuple-element.41.grad_gate, bf16[256,1024]{1,0:T(8,128)(2,1)S(1)} %get-tuple-element.42.grad_up, bf16[8192,1024]{1,0:T(8,128)(2,1)S(1)} %bitcast.1, bf16[8192,1024]{1,0:T(8,128)(2,1)S(1)} %bitcast.3), custom_call_target="tpu_custom_call" | custom-call | flops 37500000 | tf_op jit(solution)/shard_map/pallas_call | solution.py:30
  40.2 0.2 collective-permute-start.15
  40.4 1.5 %shard_map.69 = (f32[256,512]{1,0:T(8,128)S(1)}, f32[256,512]{1,0:T(8,128)S(1)}) custom-call(bf16[256,1024]{1,0:T(8,128)(2,1)S(1)} %get-tuple-element.41.grad_gate, bf16[256,1024]{1,0:T(8,128)(2,1)S(1)} %get-tuple-element.42.grad_up, bf16[8192,1024]{1,0:T(8,128)(2,1)S(1)} %bitcast.1, bf16[8192,1024]{1,0:T(8,128)(2,1)S(1)} %bitcast.3), custom_call_target="tpu_custom_call" | custom-call | flops 75000000 | tf_op jit(solution)/shard_map/pallas_call | solution.py:30
  41.9 0.2 collective-permute-done.15
  42.2 0.1 add_convert_fusion.4
  42.2 1.5 %shard_map.71 = bf16[256,1024]{1,0:T(8,128)(2,1)S(1)} custom-call(bf16[256,1024]{1,0:T(8,128)(2,1)S(1)} %get-tuple-element.41.grad_gate, bf16[256,1024]{1,0:T(8,128)(2,1)S(1)} %get-tuple-element.42.grad_up, bf16[8192,1024]{1,0:T(8,128)(2,1)S(1)} %bitcast.1, bf16[8192,1024]{1,0:T(8,128)(2,1)S(1)} %bitcast.3), custom_call_target="tpu_custom_call" | custom-call | flops 37500000 | tf_op jit(solution)/shard_map/pallas_call | solution.py:30
  43.7 0.2 collective-permute-start.16
  44.0 0.5 collective-permute-start.21
  44.5 1.2 %collective-permute-done.16.refs_0_ = bf16[256,1024]{1,0:T(8,128)(2,1)S(1)} collective-permute-done((bf16[256,1024]{1,0:T(8,128)(2,1)S(1)}, bf16[256,1024]{1,0:T(8,128)(2,1)S(1)}, u32[]{:S(2)}, u32[]{:S(2)}) %collective-permute-start.16) | collective-permute-done | bytes 524320 | tf_op jit(solution)/shard_map/ppermute | solution.py:230
  45.7 3.0 %shard_map.72 = (f32[256,512]{1,0:T(8,128)S(1)}, bf16[256,512]{1,0:T(8,128)(2,1)S(1)}, bf16[256,1024]{1,0:T(8,128)(2,1)S(1)}) custom-call(bf16[256,1024]{1,0:T(8,128)(2,1)S(1)} %get-tuple-element.41.grad_gate, bf16[256,1024]{1,0:T(8,128)(2,1)S(1)} %get-tuple-element.42.grad_up, bf16[8192,1024]{1,0:T(8,128)(2,1)S(1)} %bitcast.1, ...), custom_call_target="tpu_custom_call" | custom-call | flops 112500000 | tf_op jit(solution)/shard_map/pallas_call | solution.py:30
  48.8 0.2 collective-permute-start.17
  49.0 0.5 collective-permute-start.20
  49.5 3.6 %collective-permute-done.21 = bf16[256,512]{1,0:T(8,128)(2,1)S(1)} collective-permute-done((bf16[256,512]{1,0:T(8,128)(2,1)S(1)}, bf16[256,512]{1,0:T(8,128)(2,1)S(1)}, u32[]{:S(2)}, u32[]{:S(2)}) %collective-permute-start.21) | collective-permute-done | bytes 262176 | tf_op jit(solution)/shard_map/ppermute | solution.py:230
  53.1 0.1 add_convert_fusion.3
  53.2 0.7 collective-permute-start.22
  53.9 0.0 collective-permute-done.17.refs_0_
  53.9 3.0 %shard_map.73 = (f32[256,512]{1,0:T(8,128)S(1)}, bf16[256,512]{1,0:T(8,128)(2,1)S(1)}, bf16[256,1024]{1,0:T(8,128)(2,1)S(1)}) custom-call(bf16[256,1024]{1,0:T(8,128)(2,1)S(1)} %get-tuple-element.41.grad_gate, bf16[256,1024]{1,0:T(8,128)(2,1)S(1)} %get-tuple-element.42.grad_up, bf16[8192,1024]{1,0:T(8,128)(2,1)S(1)} %bitcast.1, ...), custom_call_target="tpu_custom_call" | custom-call | flops 112500000 | tf_op jit(solution)/shard_map/pallas_call | solution.py:30
  56.9 1.0 %collective-permute-start.24 = (bf16[256,512]{1,0:T(8,128)(2,1)S(1)}, bf16[256,512]{1,0:T(8,128)(2,1)S(1)}, u32[]{:S(2)}, u32[]{:S(2)}) collective-permute-start(bf16[256,512]{1,0:T(8,128)(2,1)S(1)} %get-tuple-element.49), channel_id=1, source_target_pairs={{0,2},{1,3},{2,0},{3,1},{4,6},{5,7},{6,4},{7,5},{8,10},{9,11},{10,... | collective-permute-start | bytes 786440 | tf_op jit(solution)/shard_map/ppermute | solution.py:230
  57.9 0.2 collective-permute-done.20
  58.2 2.3 %collective-permute-done.22 = bf16[256,512]{1,0:T(8,128)(2,1)S(1)} collective-permute-done((bf16[256,512]{1,0:T(8,128)(2,1)S(1)}, bf16[256,512]{1,0:T(8,128)(2,1)S(1)}, u32[]{:S(2)}, u32[]{:S(2)}) %collective-permute-start.22) | collective-permute-done | bytes 262176 | tf_op jit(solution)/shard_map/ppermute | solution.py:230
  60.5 0.1 add_convert_fusion.2
  60.6 1.7 %collective-permute-start.23 = (bf16[128,512]{1,0:T(8,128)(2,1)S(1)}, bf16[128,512]{1,0:T(8,128)(2,1)S(1)}, u32[]{:S(2)}, u32[]{:S(2)}) collective-permute-start(bf16[128,512]{1,0:T(8,128)(2,1)S(1)} %get-tuple-element.55), channel_id=1, source_target_pairs={{0,8},{1,9},{2,10},{3,11},{4,12},{5,13},{6,14},{7,15},{8,0},{9,1},... | collective-permute-start | bytes 393224 | tf_op jit(solution)/shard_map/ppermute | solution.py:230
  62.3 1.6 %shard_map.74 = (f32[256,512]{1,0:T(8,128)S(1)}, bf16[256,512]{1,0:T(8,128)(2,1)S(1)}) custom-call(bf16[256,1024]{1,0:T(8,128)(2,1)S(1)} %get-tuple-element.41.grad_gate, bf16[256,1024]{1,0:T(8,128)(2,1)S(1)} %get-tuple-element.42.grad_up, bf16[8192,1024]{1,0:T(8,128)(2,1)S(1)} %bitcast.1, bf16[8192,1024]{1,0:T(8,128)(2,1)S(1)} %bitcast.3, ...), custom_call_target="tpu_custom_call" | custom-call | flops 75000000 | tf_op jit(solution)/shard_map/pallas_call | solution.py:30
  63.9 1.0 %collective-permute-start.19 = (bf16[256,512]{1,0:T(8,128)(2,1)S(1)}, bf16[256,512]{1,0:T(8,128)(2,1)S(1)}, u32[]{:S(2)}, u32[]{:S(2)}) collective-permute-start(bf16[256,512]{1,0:T(8,128)(2,1)S(1)} %get-tuple-element.46), channel_id=1, source_target_pairs={{0,2},{1,3},{2,0},{3,1},{4,6},{5,7},{6,4},{7,5},{8,10},{9,11},{10,... | collective-permute-start | bytes 786440 | tf_op jit(solution)/shard_map/ppermute | solution.py:230
  64.9 0.9 %collective-permute-start.25 = (bf16[128,512]{1,0:T(8,128)(2,1)S(1)}, bf16[128,512]{1,0:T(8,128)(2,1)S(1)}, u32[]{:S(2)}, u32[]{:S(2)}) collective-permute-start(bf16[128,512]{1,0:T(8,128)(2,1)S(1)} %get-tuple-element.56), channel_id=1, source_target_pairs={{0,8},{1,9},{2,10},{3,11},{4,12},{5,13},{6,14},{7,15},{8,0},{9,1},... | collective-permute-start | bytes 393224 | tf_op jit(solution)/shard_map/ppermute | solution.py:230
  65.7 5.8 %collective-permute-done.23 = bf16[128,512]{1,0:T(8,128)(2,1)S(1)} collective-permute-done((bf16[128,512]{1,0:T(8,128)(2,1)S(1)}, bf16[128,512]{1,0:T(8,128)(2,1)S(1)}, u32[]{:S(2)}, u32[]{:S(2)}) %collective-permute-start.23) | collective-permute-done | bytes 131104 | tf_op jit(solution)/shard_map/ppermute | solution.py:230
  71.6 0.1 add_convert_fusion.1
  71.7 0.2 collective-permute-start.26
  71.8 1.9 %collective-permute-done.25 = bf16[128,512]{1,0:T(8,128)(2,1)S(1)} collective-permute-done((bf16[128,512]{1,0:T(8,128)(2,1)S(1)}, bf16[128,512]{1,0:T(8,128)(2,1)S(1)}, u32[]{:S(2)}, u32[]{:S(2)}) %collective-permute-start.25) | collective-permute-done | bytes 131104 | tf_op jit(solution)/shard_map/ppermute | solution.py:230
  73.7 0.1 convert_add_fusion
  73.8 4.3 %collective-permute-done.26 = bf16[256,512]{1,0:T(8,128)(2,1)S(1)} collective-permute-done((bf16[256,512]{1,0:T(8,128)(2,1)S(1)}, bf16[256,512]{1,0:T(8,128)(2,1)S(1)}, u32[]{:S(2)}, u32[]{:S(2)}) %collective-permute-start.26) | collective-permute-done | bytes 262176 | tf_op jit(solution)/shard_map/ppermute | solution.py:230
  78.1 0.8 add_convert_fusion
  (26 shorter events, 0.1 us)
Async XLA Ops:
  0.0 12.0 %collective-permute-start.3 = (bf16[256,512]{1,0:T(8,128)(2,1)}, bf16[256,512]{1,0:T(8,128)(2,1)S(1)}, u32[]{:S(2)}, u32[]{:S(2)}) collective-permute-start(bf16[256,512]{1,0:T(8,128)(2,1)} %refs_0_.1), channel_id=1, source_target_pairs={{0,4},{1,5},{2,6},{3,7},{4,0},{5,1},{6,2},{7,3},{8,12},{9,13},{10,... | collective-permute-start | bytes 786440 | tf_op jit(solution)/shard_map/ppermute | solution.py:230
  3.0 12.2 %collective-permute-start.2 = (bf16[256,512]{1,0:T(8,128)(2,1)}, bf16[256,512]{1,0:T(8,128)(2,1)S(1)}, u32[]{:S(2)}, u32[]{:S(2)}) collective-permute-start(bf16[256,512]{1,0:T(8,128)(2,1)} %refs_0_.1), channel_id=1, source_target_pairs={{0,2},{1,3},{2,0},{3,1},{4,6},{5,7},{6,4},{7,5},{8,10},{9,11},{10,... | collective-permute-start | bytes 786440 | tf_op jit(solution)/shard_map/ppermute | solution.py:230
  4.5 11.2 %collective-permute-start.1 = (bf16[256,512]{1,0:T(8,128)(2,1)}, bf16[256,512]{1,0:T(8,128)(2,1)S(1)}, u32[]{:S(2)}, u32[]{:S(2)}) collective-permute-start(bf16[256,512]{1,0:T(8,128)(2,1)} %refs_0_.1), channel_id=1, source_target_pairs={{0,1},{1,0},{2,3},{3,2},{4,5},{5,4},{6,7},{7,6},{8,9},{9,8},{10,11... | collective-permute-start | bytes 786440 | tf_op jit(solution)/shard_map/ppermute | solution.py:230
  4.5 15.5 %collective-permute-start = (bf16[256,512]{1,0:T(8,128)(2,1)}, bf16[256,512]{1,0:T(8,128)(2,1)S(1)}, u32[]{:S(2)}, u32[]{:S(2)}) collective-permute-start(bf16[256,512]{1,0:T(8,128)(2,1)} %refs_0_.1), channel_id=1, source_target_pairs={{0,8},{1,9},{2,10},{3,11},{4,12},{5,13},{6,14},{7,15},{8,0},{9,1},... | collective-permute-start | bytes 786440 | tf_op jit(solution)/shard_map/ppermute | solution.py:230
  12.1 8.5 %collective-permute-start.9 = (bf16[256,512]{1,0:T(8,128)(2,1)S(1)}, bf16[256,512]{1,0:T(8,128)(2,1)S(1)}, u32[]{:S(2)}, u32[]{:S(2)}) collective-permute-start(bf16[256,512]{1,0:T(8,128)(2,1)S(1)} %collective-permute-done.3.refs_3_), channel_id=1, source_target_pairs={{0,2},{1,3},{2,0},{3,1},{4,6},{5,7},{6,4},{7,5},{8,10},{9,11},{10,... | collective-permute-start | bytes 786440 | tf_op jit(solution)/shard_map/ppermute | solution.py:230
  15.3 5.3 %collective-permute-start.8 = (bf16[256,512]{1,0:T(8,128)(2,1)S(1)}, bf16[256,512]{1,0:T(8,128)(2,1)S(1)}, u32[]{:S(2)}, u32[]{:S(2)}) collective-permute-start(bf16[256,512]{1,0:T(8,128)(2,1)S(1)} %collective-permute-done.3.refs_3_), channel_id=1, source_target_pairs={{0,1},{1,0},{2,3},{3,2},{4,5},{5,4},{6,7},{7,6},{8,9},{9,8},{10,11... | collective-permute-start | bytes 786440 | tf_op jit(solution)/shard_map/ppermute | solution.py:230
  15.3 5.8 %collective-permute-start.7 = (bf16[256,512]{1,0:T(8,128)(2,1)S(1)}, bf16[256,512]{1,0:T(8,128)(2,1)S(1)}, u32[]{:S(2)}, u32[]{:S(2)}) collective-permute-start(bf16[256,512]{1,0:T(8,128)(2,1)S(1)} %collective-permute-done.2.refs_2_), channel_id=1, source_target_pairs={{0,1},{1,0},{2,3},{3,2},{4,5},{5,4},{6,7},{7,6},{8,9},{9,8},{10,11... | collective-permute-start | bytes 786440 | tf_op jit(solution)/shard_map/ppermute | solution.py:230
  20.0 7.9 %collective-permute-start.6 = (bf16[256,512]{1,0:T(8,128)(2,1)S(1)}, bf16[256,512]{1,0:T(8,128)(2,1)S(1)}, u32[]{:S(2)}, u32[]{:S(2)}) collective-permute-start(bf16[256,512]{1,0:T(8,128)(2,1)S(1)} %collective-permute-done.refs_3_), channel_id=1, source_target_pairs={{0,4},{1,5},{2,6},{3,7},{4,0},{5,1},{6,2},{7,3},{8,12},{9,13},{10,... | collective-permute-start | bytes 786440 | tf_op jit(solution)/shard_map/ppermute | solution.py:230
  20.0 8.4 %collective-permute-start.4 = (bf16[256,512]{1,0:T(8,128)(2,1)S(1)}, bf16[256,512]{1,0:T(8,128)(2,1)S(1)}, u32[]{:S(2)}, u32[]{:S(2)}) collective-permute-start(bf16[256,512]{1,0:T(8,128)(2,1)S(1)} %collective-permute-done.refs_3_), channel_id=1, source_target_pairs={{0,2},{1,3},{2,0},{3,1},{4,6},{5,7},{6,4},{7,5},{8,10},{9,11},{10,... | collective-permute-start | bytes 786440 | tf_op jit(solution)/shard_map/ppermute | solution.py:230
  20.6 8.4 %collective-permute-start.13 = (bf16[256,512]{1,0:T(8,128)(2,1)S(1)}, bf16[256,512]{1,0:T(8,128)(2,1)S(1)}, u32[]{:S(2)}, u32[]{:S(2)}) collective-permute-start(bf16[256,512]{1,0:T(8,128)(2,1)S(1)} %collective-permute-done.refs_3_), channel_id=1, source_target_pairs={{0,1},{1,0},{2,3},{3,2},{4,5},{5,4},{6,7},{7,6},{8,9},{9,8},{10,11... | collective-permute-start | bytes 786440 | tf_op jit(solution)/shard_map/ppermute | solution.py:230
  20.6 8.4 %collective-permute-start.12 = (bf16[256,512]{1,0:T(8,128)(2,1)S(1)}, bf16[256,512]{1,0:T(8,128)(2,1)S(1)}, u32[]{:S(2)}, u32[]{:S(2)}) collective-permute-start(bf16[256,512]{1,0:T(8,128)(2,1)S(1)} %collective-permute-done.9.refs_2_), channel_id=1, source_target_pairs={{0,1},{1,0},{2,3},{3,2},{4,5},{5,4},{6,7},{7,6},{8,9},{9,8},{10,11... | collective-permute-start | bytes 786440 | tf_op jit(solution)/shard_map/ppermute | solution.py:230
  21.1 17.5 %slice-start = ((s8[16777216]{0:T(1024)(128)(4,1)}), s8[4194304]{0:T(1024)(128)(4,1)S(1)}, s32[]{:S(2)}) async-start(s8[16777216]{0:T(1024)(128)(4,1)} %bitcast), calls=%async_computation | async-start | bytes 8388608
  21.1 17.5 %slice-start.1 = ((s8[16777216]{0:T(1024)(128)(4,1)}), s8[4194304]{0:T(1024)(128)(4,1)S(1)}, s32[]{:S(2)}) async-start(s8[16777216]{0:T(1024)(128)(4,1)} %bitcast), calls=%async_computation.1 | async-start | bytes 8388608
  21.1 17.5 %slice-start.4 = ((s8[16777216]{0:T(1024)(128)(4,1)}), s8[4194304]{0:T(1024)(128)(4,1)S(1)}, s32[]{:S(2)}) async-start(s8[16777216]{0:T(1024)(128)(4,1)} %bitcast.2), calls=%async_computation.4 | async-start | bytes 8388608
  21.1 17.5 %slice-start.5 = ((s8[16777216]{0:T(1024)(128)(4,1)}), s8[4194304]{0:T(1024)(128)(4,1)S(1)}, s32[]{:S(2)}) async-start(s8[16777216]{0:T(1024)(128)(4,1)} %bitcast.2), calls=%async_computation.5 | async-start | bytes 8388608
  24.6 14.0 %slice-start.2 = ((s8[16777216]{0:T(1024)(128)(4,1)}), s8[4194304]{0:T(1024)(128)(4,1)S(1)}, s32[]{:S(2)}) async-start(s8[16777216]{0:T(1024)(128)(4,1)} %bitcast), calls=%async_computation.2 | async-start | bytes 8388608
  24.6 14.0 %slice-start.3 = ((s8[16777216]{0:T(1024)(128)(4,1)}), s8[4194304]{0:T(1024)(128)(4,1)S(1)}, s32[]{:S(2)}) async-start(s8[16777216]{0:T(1024)(128)(4,1)} %bitcast), calls=%async_computation.3 | async-start | bytes 8388608
  24.6 14.0 %slice-start.6 = ((s8[16777216]{0:T(1024)(128)(4,1)}), s8[4194304]{0:T(1024)(128)(4,1)S(1)}, s32[]{:S(2)}) async-start(s8[16777216]{0:T(1024)(128)(4,1)} %bitcast.2), calls=%async_computation.6 | async-start | bytes 8388608
  24.7 14.0 %slice-start.7 = ((s8[16777216]{0:T(1024)(128)(4,1)}), s8[4194304]{0:T(1024)(128)(4,1)S(1)}, s32[]{:S(2)}) async-start(s8[16777216]{0:T(1024)(128)(4,1)} %bitcast.2), calls=%async_computation.7 | async-start | bytes 8388608
  28.0 7.0 %collective-permute-start.11 = (bf16[256,512]{1,0:T(8,128)(2,1)S(1)}, bf16[256,512]{1,0:T(8,128)(2,1)S(1)}, u32[]{:S(2)}, u32[]{:S(2)}) collective-permute-start(bf16[256,512]{1,0:T(8,128)(2,1)S(1)} %collective-permute-done.6.refs_3_), channel_id=1, source_target_pairs={{0,2},{1,3},{2,0},{3,1},{4,6},{5,7},{6,4},{7,5},{8,10},{9,11},{10,... | collective-permute-start | bytes 786440 | tf_op jit(solution)/shard_map/ppermute | solution.py:230
  28.5 6.5 %collective-permute-start.10 = (bf16[256,512]{1,0:T(8,128)(2,1)S(1)}, bf16[256,512]{1,0:T(8,128)(2,1)S(1)}, u32[]{:S(2)}, u32[]{:S(2)}) collective-permute-start(bf16[256,512]{1,0:T(8,128)(2,1)S(1)} %collective-permute-done.6.refs_3_), channel_id=1, source_target_pairs={{0,1},{1,0},{2,3},{3,2},{4,5},{5,4},{6,7},{7,6},{8,9},{9,8},{10,11... | collective-permute-start | bytes 786440 | tf_op jit(solution)/shard_map/ppermute | solution.py:230
  28.5 6.5 %collective-permute-start.5 = (bf16[256,512]{1,0:T(8,128)(2,1)S(1)}, bf16[256,512]{1,0:T(8,128)(2,1)S(1)}, u32[]{:S(2)}, u32[]{:S(2)}) collective-permute-start(bf16[256,512]{1,0:T(8,128)(2,1)S(1)} %collective-permute-done.4.refs_2_), channel_id=1, source_target_pairs={{0,1},{1,0},{2,3},{3,2},{4,5},{5,4},{6,7},{7,6},{8,9},{9,8},{10,11... | collective-permute-start | bytes 786440 | tf_op jit(solution)/shard_map/ppermute | solution.py:230
  35.0 1.5 %collective-permute-start.14 = (bf16[256,512]{1,0:T(8,128)(2,1)S(1)}, bf16[256,512]{1,0:T(8,128)(2,1)S(1)}, u32[]{:S(2)}, u32[]{:S(2)}) collective-permute-start(bf16[256,512]{1,0:T(8,128)(2,1)S(1)} %collective-permute-done.11.refs_2_), channel_id=1, source_target_pairs={{0,1},{1,0},{2,3},{3,2},{4,5},{5,4},{6,7},{7,6},{8,9},{9,8},{10,11... | collective-permute-start | bytes 786440 | tf_op jit(solution)/shard_map/ppermute | solution.py:230
  40.2 2.0 %collective-permute-start.15 = (bf16[256,1024]{1,0:T(8,128)(2,1)S(1)}, bf16[256,1024]{1,0:T(8,128)(2,1)S(1)}, u32[]{:S(2)}, u32[]{:S(2)}) collective-permute-start(bf16[256,1024]{1,0:T(8,128)(2,1)S(1)} %shard_map.70), channel_id=1, source_target_pairs={{0,1},{1,0},{2,3},{3,2},{4,5},{5,4},{6,7},{7,6},{8,9},{9,8},{10,11... | collective-permute-start | bytes 1572872 | tf_op jit(solution)/shard_map/ppermute | solution.py:230
  43.7 2.0 %collective-permute-start.16 = (bf16[256,1024]{1,0:T(8,128)(2,1)S(1)}, bf16[256,1024]{1,0:T(8,128)(2,1)S(1)}, u32[]{:S(2)}, u32[]{:S(2)}) collective-permute-start(bf16[256,1024]{1,0:T(8,128)(2,1)S(1)} %shard_map.71), channel_id=1, source_target_pairs={{0,1},{1,0},{2,3},{3,2},{4,5},{5,4},{6,7},{7,6},{8,9},{9,8},{10,11... | collective-permute-start | bytes 1572872 | tf_op jit(solution)/shard_map/ppermute | solution.py:230
  44.0 9.1 %collective-permute-start.21 = (bf16[256,512]{1,0:T(8,128)(2,1)S(1)}, bf16[256,512]{1,0:T(8,128)(2,1)S(1)}, u32[]{:S(2)}, u32[]{:S(2)}) collective-permute-start(bf16[256,512]{1,0:T(8,128)(2,1)S(1)} %add_convert_fusion.4), channel_id=1, source_target_pairs={{0,2},{1,3},{2,0},{3,1},{4,6},{5,7},{6,4},{7,5},{8,10},{9,11},{10,... | collective-permute-start | bytes 786440 | tf_op jit(solution)/shard_map/ppermute | solution.py:230
  48.8 5.1 %collective-permute-start.17 = (bf16[256,1024]{1,0:T(8,128)(2,1)S(1)}, bf16[256,1024]{1,0:T(8,128)(2,1)S(1)}, u32[]{:S(2)}, u32[]{:S(2)}) collective-permute-start(bf16[256,1024]{1,0:T(8,128)(2,1)S(1)} %get-tuple-element.43), channel_id=1, source_target_pairs={{0,1},{1,0},{2,3},{3,2},{4,5},{5,4},{6,7},{7,6},{8,9},{9,8},{10,11... | collective-permute-start | bytes 1572872 | tf_op jit(solution)/shard_map/ppermute | solution.py:230
  49.0 9.1 %collective-permute-start.20 = (bf16[256,512]{1,0:T(8,128)(2,1)S(1)}, bf16[256,512]{1,0:T(8,128)(2,1)S(1)}, u32[]{:S(2)}, u32[]{:S(2)}) collective-permute-start(bf16[256,512]{1,0:T(8,128)(2,1)S(1)} %get-tuple-element.48), channel_id=1, source_target_pairs={{0,2},{1,3},{2,0},{3,1},{4,6},{5,7},{6,4},{7,5},{8,10},{9,11},{10,... | collective-permute-start | bytes 786440 | tf_op jit(solution)/shard_map/ppermute | solution.py:230
  53.2 7.2 %collective-permute-start.22 = (bf16[256,512]{1,0:T(8,128)(2,1)S(1)}, bf16[256,512]{1,0:T(8,128)(2,1)S(1)}, u32[]{:S(2)}, u32[]{:S(2)}) collective-permute-start(bf16[256,512]{1,0:T(8,128)(2,1)S(1)} %add_convert_fusion.3), channel_id=1, source_target_pairs={{0,4},{1,5},{2,6},{3,7},{4,0},{5,1},{6,2},{7,3},{8,12},{9,13},{10,... | collective-permute-start | bytes 786440 | tf_op jit(solution)/shard_map/ppermute | solution.py:230
  56.9 14.6 %collective-permute-start.24 = (bf16[256,512]{1,0:T(8,128)(2,1)S(1)}, bf16[256,512]{1,0:T(8,128)(2,1)S(1)}, u32[]{:S(2)}, u32[]{:S(2)}) collective-permute-start(bf16[256,512]{1,0:T(8,128)(2,1)S(1)} %get-tuple-element.49), channel_id=1, source_target_pairs={{0,2},{1,3},{2,0},{3,1},{4,6},{5,7},{6,4},{7,5},{8,10},{9,11},{10,... | collective-permute-start | bytes 786440 | tf_op jit(solution)/shard_map/ppermute | solution.py:230
  58.2 4.1 %collective-permute-start.18 = (bf16[256,1024]{1,0:T(8,128)(2,1)S(1)}, bf16[256,1024]{1,0:T(8,128)(2,1)S(1)}, u32[]{:S(2)}, u32[]{:S(2)}) collective-permute-start(bf16[256,1024]{1,0:T(8,128)(2,1)S(1)} %get-tuple-element.44), channel_id=1, source_target_pairs={{0,1},{1,0},{2,3},{3,2},{4,5},{5,4},{6,7},{7,6},{8,9},{9,8},{10,11... | collective-permute-start | bytes 1572872 | tf_op jit(solution)/shard_map/ppermute | solution.py:230
  60.6 11.0 %collective-permute-start.23 = (bf16[128,512]{1,0:T(8,128)(2,1)S(1)}, bf16[128,512]{1,0:T(8,128)(2,1)S(1)}, u32[]{:S(2)}, u32[]{:S(2)}) collective-permute-start(bf16[128,512]{1,0:T(8,128)(2,1)S(1)} %get-tuple-element.55), channel_id=1, source_target_pairs={{0,8},{1,9},{2,10},{3,11},{4,12},{5,13},{6,14},{7,15},{8,0},{9,1},... | collective-permute-start | bytes 393224 | tf_op jit(solution)/shard_map/ppermute | solution.py:230
  63.9 9.9 %collective-permute-start.19 = (bf16[256,512]{1,0:T(8,128)(2,1)S(1)}, bf16[256,512]{1,0:T(8,128)(2,1)S(1)}, u32[]{:S(2)}, u32[]{:S(2)}) collective-permute-start(bf16[256,512]{1,0:T(8,128)(2,1)S(1)} %get-tuple-element.46), channel_id=1, source_target_pairs={{0,2},{1,3},{2,0},{3,1},{4,6},{5,7},{6,4},{7,5},{8,10},{9,11},{10,... | collective-permute-start | bytes 786440 | tf_op jit(solution)/shard_map/ppermute | solution.py:230
  64.9 8.8 %collective-permute-start.25 = (bf16[128,512]{1,0:T(8,128)(2,1)S(1)}, bf16[128,512]{1,0:T(8,128)(2,1)S(1)}, u32[]{:S(2)}, u32[]{:S(2)}) collective-permute-start(bf16[128,512]{1,0:T(8,128)(2,1)S(1)} %get-tuple-element.56), channel_id=1, source_target_pairs={{0,8},{1,9},{2,10},{3,11},{4,12},{5,13},{6,14},{7,15},{8,0},{9,1},... | collective-permute-start | bytes 393224 | tf_op jit(solution)/shard_map/ppermute | solution.py:230
  71.7 6.4 %collective-permute-start.26 = (bf16[256,512]{1,0:T(8,128)(2,1)S(1)}, bf16[256,512]{1,0:T(8,128)(2,1)S(1)}, u32[]{:S(2)}, u32[]{:S(2)}) collective-permute-start(bf16[256,512]{1,0:T(8,128)(2,1)S(1)} %add_convert_fusion.1), channel_id=1, source_target_pairs={{0,4},{1,5},{2,6},{3,7},{4,0},{5,1},{6,2},{7,3},{8,12},{9,13},{10,... | collective-permute-start | bytes 786440 | tf_op jit(solution)/shard_map/ppermute | solution.py:230
